TPU v7x, 32 devices: a whole 2x2x4 slice. The times are simulated.
32 devices in a mesh: row: 4 (over x, core), seq: 8 (over z, y).
Axes of the slice: x: 2, y: 2, z: 4, core: 2. Of those that a mesh axis runs over, the one named last changes fastest.
Arguments:
- frames: float32 [4, 1024, 768], P('row', 'seq'), may hold values from -6 to 6
- clip_lengths: int32 [4, 6], P('row'), may hold values from 0 to 1024, as said below
- query_weight: bfloat16 [768, 768], replicated, may hold values from -0.21875 to 0.21875
- query_bias: float32 [768], replicated, may hold values from -3 to 3
- key_weight: bfloat16 [768, 768], replicated, may hold values from -0.21875 to 0.21875
- value_weight: bfloat16 [768, 768], replicated, may hold values from -0.21875 to 0.21875
- value_bias: float32 [768], replicated, may hold values from -0.3 to 0.3
- out_weight: bfloat16 [768, 768], replicated, may hold values from -3.5 to 3.5
- out_bias: float32 [768], replicated, may hold values from -0.6 to 0.6
- norm1_gain: float32 [768], replicated, may hold values from 0.5 to 1.5
- norm1_bias: float32 [768], replicated, may hold values from -0.6 to 0.6
- up_weight: bfloat16 [768, 3072], replicated, may hold values from -0.21875 to 0.21875
- up_bias: float32 [3072], replicated, may hold values from -1.2 to 1.2
- down_weight: bfloat16 [3072, 768], replicated, may hold values from -0.109375 to 0.109375
- down_bias: float32 [768], replicated, may hold values from -0.6 to 0.6
- norm2_gain: float32 [768], replicated, may hold values from 0.5 to 1.5
- norm2_bias: float32 [768], replicated, may hold values from -0.6 to 0.6
- cotangent: float32 [4, 1024, 768], P('row', 'seq'), may hold values from -6 to 6
Outputs:
- encoded: float32 [4, 1024, 768], P('row', 'seq')
- frames_grad: float32 [4, 1024, 768], P('row', 'seq')
- query_weight_grad: float32 [768, 768], replicated
- query_bias_grad: float32 [768], replicated
- key_weight_grad: float32 [768, 768], replicated
- value_weight_grad: float32 [768, 768], replicated
- value_bias_grad: float32 [768], replicated
- out_weight_grad: float32 [768, 768], replicated
- out_bias_grad: float32 [768], replicated
- norm1_gain_grad: float32 [768], replicated
- norm1_bias_grad: float32 [768], replicated
- up_weight_grad: float32 [768, 3072], replicated
- up_bias_grad: float32 [3072], replicated
- down_weight_grad: float32 [3072, 768], replicated
- down_bias_grad: float32 [768], replicated
- norm2_gain_grad: float32 [768], replicated
- norm2_bias_grad: float32 [768], replicated
Inputs may be any that keep to these rules, and one draw needn't show every extreme that they name: `clip_lengths`: each row's entries sum to 1024, nonzero entries first. The rows fall into aligned groups of 1 row, or of 2 rows where 1 is 1; in each group exactly one row, chosen by the seed, is a single recording: first entry 1024, the rest 0. In the other rows every nonzero entry is 250 or 1500, except the last nonzero one, which is cut at the row's end.
All inputs are finite; a program needn't handle non-finite values.
Results may differ from a plain program's by a relative error of at most 0.02.
Values may be sent and summed in bfloat16 or wider, within the bound.
A program may use at most 192 MiB of HBM per device.

v0:
```python
from functools import partial
import math

import jax
import jax.numpy as jnp
from jax import lax
from jax.sharding import PartitionSpec as P

H = 12
HD = 64


MASK_SCORE = -1e30
NORM_EPSILON = 1e-05


def from_behind(value, axis, by):
    count = lax.axis_size(axis)
    return lax.ppermute(value, axis, [(i, (i + by) % count) for i in range(count)])


def layer_norm(summed, norm_gain, norm_shift):
    centre = jnp.mean(summed, axis=-1, keepdims=True)
    centered = summed - centre
    inverse = lax.rsqrt(jnp.mean(centered * centered, axis=-1, keepdims=True) + NORM_EPSILON)
    normed = centered * inverse
    return (normed * norm_gain + norm_shift, normed, inverse)


def layer_norm_back(upstream, normed, inverse, norm_gain):
    scaled = upstream * norm_gain
    first_mean = jnp.mean(scaled, axis=-1, keepdims=True)
    second_mean = jnp.mean(scaled * normed, axis=-1, keepdims=True)
    summed_grad = inverse * (scaled - first_mean - normed * second_mean)
    return (summed_grad, jnp.sum(upstream * normed, axis=(0, 1)), jnp.sum(upstream, axis=(0, 1)))


def project(inputs, matrix):
    return jnp.einsum("rsk,kn->rsn", inputs, matrix, preferred_element_type=jnp.float32)


def project_back(upstream, matrix):
    return jnp.einsum("rsn,kn->rsk", upstream, matrix, preferred_element_type=jnp.float32)


def matrix_grad(inputs, upstream):
    return jnp.einsum("rsk,rsn->kn", inputs, upstream, preferred_element_type=jnp.float32)


def column_sum(upstream):
    return jnp.sum(upstream.astype(jnp.float32), axis=(0, 1))


def clip_numbers(clip_ends, position):
    return jnp.sum((clip_ends[:, None, :] <= position[None, :, None]).astype(jnp.int32), axis=-1)


def split_heads(tensor):
    return tensor.reshape(tensor.shape[0], tensor.shape[1], H, HD)


def join_heads(tensor):
    return tensor.reshape(tensor.shape[0], tensor.shape[1], H * HD)


def head_scores(queries, keys_block):
    return jnp.einsum(
        "rqhd,rkhd->rhqk", queries, keys_block, preferred_element_type=jnp.float32
    ) * HD ** (-0.5)


def allowed_pairs(query_numbers, key_numbers):
    return (query_numbers[:, :, None] == key_numbers[:, None, :])[:, None]


def online_update(running, queries, query_numbers, keys_block, values_block, key_numbers):
    run_peak, run_total, run_values = running
    allowed = allowed_pairs(query_numbers, key_numbers)
    masked = jnp.where(allowed, head_scores(queries, keys_block), MASK_SCORE)
    new_peak = jnp.maximum(run_peak, jnp.max(masked, axis=-1))
    weights = jnp.where(allowed, jnp.exp(masked - new_peak[..., None]), 0.0)
    rescale = jnp.exp(run_peak - new_peak)
    new_total = run_total * rescale + jnp.sum(weights, axis=-1)
    contrib = jnp.einsum(
        "rhqk,rkhd->rqhd",
        weights.astype(jnp.bfloat16),
        values_block,
        preferred_element_type=jnp.float32,
    )
    new_values = run_values * jnp.swapaxes(rescale, 1, 2)[..., None] + contrib
    return (new_peak, new_total, new_values)


def block_back(
    queries, grad_heads, log_total, delta_rows, query_numbers, keys_flat, values_flat, key_numbers
):
    keys_block = split_heads(keys_flat)
    values_block = split_heads(values_flat)
    allowed = allowed_pairs(query_numbers, key_numbers)
    shifted = jnp.where(
        allowed, head_scores(queries, keys_block) - log_total[..., None], MASK_SCORE
    )
    weights = jnp.exp(shifted)
    grad_weights = jnp.einsum(
        "rqhd,rkhd->rhqk", grad_heads, values_block, preferred_element_type=jnp.float32
    )
    grad_scores = (weights * (grad_weights - delta_rows[..., None])).astype(jnp.bfloat16)
    factor = HD ** (-0.5)
    query_part = (
        jnp.einsum("rhqk,rkhd->rqhd", grad_scores, keys_block, preferred_element_type=jnp.float32)
        * factor
    )
    key_part = (
        jnp.einsum("rhqk,rqhd->rkhd", grad_scores, queries, preferred_element_type=jnp.float32)
        * factor
    )
    value_part = jnp.einsum(
        "rhqk,rqhd->rkhd",
        weights.astype(jnp.bfloat16),
        grad_heads,
        preferred_element_type=jnp.float32,
    )
    return (join_heads(query_part), join_heads(key_part), join_heads(value_part))


def per_device(
    frames,
    clip_lengths,
    query_weight,
    query_bias,
    key_weight,
    value_weight,
    value_bias,
    out_weight,
    out_bias,
    norm1_gain,
    norm1_bias,
    up_weight,
    up_bias,
    down_weight,
    down_bias,
    norm2_gain,
    norm2_bias,
    cotangent,
):
    row_count = frames.shape[0]
    shard_len = frames.shape[1]
    cycle_size = lax.axis_size("seq")
    seq_place = lax.axis_index("seq")
    clip_ends = jnp.cumsum(clip_lengths, axis=1)
    offsets = jnp.arange(shard_len, dtype=jnp.int32)
    own_numbers = clip_numbers(clip_ends, seq_place * shard_len + offsets)
    frames_low = frames.astype(jnp.bfloat16)
    queries = split_heads((project(frames_low, query_weight) + query_bias).astype(jnp.bfloat16))
    keys_own = project(frames_low, key_weight).astype(jnp.bfloat16)
    values_own = (project(frames_low, value_weight) + value_bias).astype(jnp.bfloat16)
    initial = (
        jnp.full((row_count, H, shard_len), MASK_SCORE, jnp.float32),
        jnp.zeros((row_count, H, shard_len), jnp.float32),
        jnp.zeros((row_count, shard_len, H, HD), jnp.float32),
    )
    key_piece = lax.all_gather(keys_own, "seq", axis=1, tiled=True)
    value_piece = lax.all_gather(values_own, "seq", axis=1, tiled=True)
    piece_len = key_piece.shape[1]
    block_len = math.gcd(piece_len, 512)

    def attend_block(block_index, carried):
        offset = block_index * block_len
        key_block = lax.dynamic_slice_in_dim(key_piece, offset, block_len, 1)
        value_block = lax.dynamic_slice_in_dim(value_piece, offset, block_len, 1)
        position = offset + jnp.arange(block_len, dtype=jnp.int32)
        return online_update(
            carried,
            queries,
            own_numbers,
            split_heads(key_block),
            split_heads(value_block),
            clip_numbers(clip_ends, position),
        )

    run_peak, run_total, run_values = lax.fori_loop(
        0, piece_len // block_len, attend_block, initial
    )
    log_total = run_peak + jnp.log(run_total)
    attended_heads = run_values / jnp.swapaxes(run_total, 1, 2)[..., None]
    attended = join_heads(attended_heads)
    attended_low = attended.astype(jnp.bfloat16)
    branch = project(attended_low, out_weight) + out_bias
    hidden, unit_first, inverse_first = layer_norm(frames + branch, norm1_gain, norm1_bias)
    hidden_low = hidden.astype(jnp.bfloat16)
    before = project(hidden_low, up_weight) + up_bias
    active, gelu_back = jax.vjp(partial(jax.nn.gelu, approximate=False), before)
    active_low = active.astype(jnp.bfloat16)
    encoded, unit_second, inverse_second = layer_norm(
        hidden + project(active_low, down_weight) + down_bias, norm2_gain, norm2_bias
    )
    grad_mid, norm2_gain_grad, norm2_bias_grad = layer_norm_back(
        cotangent, unit_second, inverse_second, norm2_gain
    )
    grad_ffn = grad_mid.astype(jnp.bfloat16)
    down_weight_grad = matrix_grad(active_low, grad_ffn)
    down_bias_grad = column_sum(grad_ffn)
    grad_before = gelu_back(project_back(grad_ffn, down_weight))[0].astype(jnp.bfloat16)
    up_weight_grad = matrix_grad(hidden_low, grad_before)
    up_bias_grad = column_sum(grad_before)
    grad_hidden = grad_mid + project_back(grad_before, up_weight)
    grad_first, norm1_gain_grad, norm1_bias_grad = layer_norm_back(
        grad_hidden, unit_first, inverse_first, norm1_gain
    )
    grad_branch = grad_first.astype(jnp.bfloat16)
    out_weight_grad = matrix_grad(attended_low, grad_branch)
    out_bias_grad = column_sum(grad_branch)
    grad_attended = project_back(grad_branch, out_weight).astype(jnp.bfloat16)
    grad_heads = split_heads(grad_attended)
    delta_rows = jnp.swapaxes(
        jnp.sum(grad_heads.astype(jnp.float32) * attended_heads, axis=-1), 1, 2
    )
    query_start, key_start, value_start = block_back(
        queries, grad_heads, log_total, delta_rows, own_numbers, keys_own, values_own, own_numbers
    )

    def key_step(distance, carried):
        key_now, value_now, query_sum, key_sum, value_sum = carried
        key_now, value_now = from_behind((key_now, value_now), "seq", 1)
        key_sum, value_sum = (
            from_behind(key_sum.astype(jnp.bfloat16), "seq", 1).astype(key_sum.dtype),
            from_behind(value_sum.astype(jnp.bfloat16), "seq", 1).astype(value_sum.dtype),
        )
        source = (seq_place - distance) % cycle_size
        source_numbers = clip_numbers(clip_ends, source * shard_len + offsets)
        query_part, key_part, value_part = block_back(
            queries,
            grad_heads,
            log_total,
            delta_rows,
            own_numbers,
            key_now,
            value_now,
            source_numbers,
        )
        return (
            key_now,
            value_now,
            query_sum + query_part,
            key_sum + key_part,
            value_sum + value_part,
        )

    carried = lax.fori_loop(
        1, cycle_size, key_step, (keys_own, values_own, query_start, key_start, value_start)
    )
    query_total = carried[2]
    key_total, value_total = (
        from_behind(carried[3].astype(jnp.bfloat16), "seq", 1).astype(jnp.float32),
        from_behind(carried[4].astype(jnp.bfloat16), "seq", 1).astype(jnp.float32),
    )
    query_low = query_total.astype(jnp.bfloat16)
    key_low = key_total.astype(jnp.bfloat16)
    value_low = value_total.astype(jnp.bfloat16)
    query_weight_grad = matrix_grad(frames_low, query_low)
    query_bias_grad = column_sum(query_low)
    key_weight_grad = matrix_grad(frames_low, key_low)
    value_weight_grad = matrix_grad(frames_low, value_low)
    value_bias_grad = column_sum(value_low)
    frames_grad = (
        grad_first
        + project_back(query_low, query_weight)
        + project_back(key_low, key_weight)
        + project_back(value_low, value_weight)
    )
    shares = (
        lax.psum_scatter(query_weight_grad, "seq", scatter_dimension=0, tiled=True),
        lax.psum_scatter(query_bias_grad, "seq", scatter_dimension=0, tiled=True),
        lax.psum_scatter(key_weight_grad, "seq", scatter_dimension=0, tiled=True),
        lax.psum_scatter(value_weight_grad, "seq", scatter_dimension=0, tiled=True),
        lax.psum_scatter(value_bias_grad, "seq", scatter_dimension=0, tiled=True),
        lax.psum_scatter(out_weight_grad, "seq", scatter_dimension=0, tiled=True),
        lax.psum_scatter(out_bias_grad, "seq", scatter_dimension=0, tiled=True),
        lax.psum_scatter(norm1_gain_grad, "seq", scatter_dimension=0, tiled=True),
        lax.psum_scatter(norm1_bias_grad, "seq", scatter_dimension=0, tiled=True),
        lax.psum_scatter(up_weight_grad, "seq", scatter_dimension=0, tiled=True),
        lax.psum_scatter(up_bias_grad, "seq", scatter_dimension=0, tiled=True),
        lax.psum_scatter(down_weight_grad, "seq", scatter_dimension=0, tiled=True),
        lax.psum_scatter(down_bias_grad, "seq", scatter_dimension=0, tiled=True),
        lax.psum_scatter(norm2_gain_grad, "seq", scatter_dimension=0, tiled=True),
        lax.psum_scatter(norm2_bias_grad, "seq", scatter_dimension=0, tiled=True),
    )
    shares = (
        lax.psum(shares[0].astype(jnp.bfloat16), "row").astype(jnp.float32),
        lax.psum(shares[1].astype(jnp.bfloat16), "row").astype(jnp.float32),
        lax.psum(shares[2].astype(jnp.bfloat16), "row").astype(jnp.float32),
        lax.psum(shares[3].astype(jnp.bfloat16), "row").astype(jnp.float32),
        lax.psum(shares[4].astype(jnp.bfloat16), "row").astype(jnp.float32),
        lax.psum(shares[5].astype(jnp.bfloat16), "row").astype(jnp.float32),
        lax.psum(shares[6].astype(jnp.bfloat16), "row").astype(jnp.float32),
        lax.psum(shares[7].astype(jnp.bfloat16), "row").astype(jnp.float32),
        lax.psum(shares[8].astype(jnp.bfloat16), "row").astype(jnp.float32),
        lax.psum(shares[9].astype(jnp.bfloat16), "row").astype(jnp.float32),
        lax.psum(shares[10].astype(jnp.bfloat16), "row").astype(jnp.float32),
        lax.psum(shares[11].astype(jnp.bfloat16), "row").astype(jnp.float32),
        lax.psum(shares[12].astype(jnp.bfloat16), "row").astype(jnp.float32),
        lax.psum(shares[13].astype(jnp.bfloat16), "row").astype(jnp.float32),
        lax.psum(shares[14].astype(jnp.bfloat16), "row").astype(jnp.float32),
    )
    totals = (
        lax.all_gather(shares[0].astype(jnp.bfloat16), "seq", axis=0, tiled=True).astype(
            jnp.float32
        ),
        lax.all_gather(shares[1].astype(jnp.bfloat16), "seq", axis=0, tiled=True).astype(
            jnp.float32
        ),
        lax.all_gather(shares[2].astype(jnp.bfloat16), "seq", axis=0, tiled=True).astype(
            jnp.float32
        ),
        lax.all_gather(shares[3].astype(jnp.bfloat16), "seq", axis=0, tiled=True).astype(
            jnp.float32
        ),
        lax.all_gather(shares[4].astype(jnp.bfloat16), "seq", axis=0, tiled=True).astype(
            jnp.float32
        ),
        lax.all_gather(shares[5].astype(jnp.bfloat16), "seq", axis=0, tiled=True).astype(
            jnp.float32
        ),
        lax.all_gather(shares[6].astype(jnp.bfloat16), "seq", axis=0, tiled=True).astype(
            jnp.float32
        ),
        lax.all_gather(shares[7].astype(jnp.bfloat16), "seq", axis=0, tiled=True).astype(
            jnp.float32
        ),
        lax.all_gather(shares[8].astype(jnp.bfloat16), "seq", axis=0, tiled=True).astype(
            jnp.float32
        ),
        lax.all_gather(shares[9].astype(jnp.bfloat16), "seq", axis=0, tiled=True).astype(
            jnp.float32
        ),
        lax.all_gather(shares[10].astype(jnp.bfloat16), "seq", axis=0, tiled=True).astype(
            jnp.float32
        ),
        lax.all_gather(shares[11].astype(jnp.bfloat16), "seq", axis=0, tiled=True).astype(
            jnp.float32
        ),
        lax.all_gather(shares[12].astype(jnp.bfloat16), "seq", axis=0, tiled=True).astype(
            jnp.float32
        ),
        lax.all_gather(shares[13].astype(jnp.bfloat16), "seq", axis=0, tiled=True).astype(
            jnp.float32
        ),
        lax.all_gather(shares[14].astype(jnp.bfloat16), "seq", axis=0, tiled=True).astype(
            jnp.float32
        ),
    )
    return (
        encoded,
        frames_grad,
        totals[0],
        totals[1],
        totals[2],
        totals[3],
        totals[4],
        totals[5],
        totals[6],
        totals[7],
        totals[8],
        totals[9],
        totals[10],
        totals[11],
        totals[12],
        totals[13],
        totals[14],
    )


def solution(mesh):
    in_specs = (
        P("row", "seq", None),
        P("row", None),
        P(),
        P(),
        P(),
        P(),
        P(),
        P(),
        P(),
        P(),
        P(),
        P(),
        P(),
        P(),
        P(),
        P(),
        P(),
        P("row", "seq", None),
    )
    out_specs = (
        P("row", "seq", None),
        P("row", "seq", None),
        P(),
        P(),
        P(),
        P(),
        P(),
        P(),
        P(),
        P(),
        P(),
        P(),
        P(),
        P(),
        P(),
        P(),
        P(),
    )
    return jax.shard_map(
        per_device, mesh=mesh, in_specs=in_specs, out_specs=out_specs, check_vma=False
    )
```

profile of v0, /device:TPU:0, one launch (start us, length us, event | category | flops | bytes accessed | tf_op | source)
XLA Modules:
  0.0 1310.2 jit_solution(12762463583045340009)
XLA Ops:
  20.8 36.9 %all-gather.24.cloned.1.call-done = bf16[1024,768]{1,0:T(8,128)(2,1)} async-done(((bf16[128,768]{1,0:T(8,128)(2,1)}), bf16[1024,768]{1,0:T(8,128)(2,1)}) %all-gather.24.cloned.1.call-update) | async-done | bytes 1572880 | tf_op jit(solution)/shard_map/all_gather | solution.py:162
  57.7 45.8 %all-gather.26.cloned.1.call-done = bf16[1024,768]{1,0:T(8,128)(2,1)} async-done(((bf16[128,768]{1,0:T(8,128)(2,1)}), bf16[1024,768]{1,0:T(8,128)(2,1)}) %all-gather.26.cloned.1.call-update) | async-done | bytes 1572880 | tf_op jit(solution)/shard_map/all_gather | solution.py:163
  103.5 24.2 %while.43 = (s32[]{:T(128)}, f32[1,12,128]{2,1,0:T(8,128)S(1)}, f32[1,12,128]{2,1,0:T(8,128)S(1)}, f32[1,128,12,64]{1,3,2,0:T(8,128)}, s32[1,128]{1,0:T(1,128)S(...) while((s32[]{:T(128)}, f32[1,12,128]{2,1,0:T(8,128)S(1)}, ...), condition=%wide.region_6.7_spmd.clone, body=%wide.region_2.6_spmd.clone.sunk | while | flops 211929088 | bytes 34386784 | solution.py:181
  151.2 137.0 %while.42 = (s32[]{:T(128)}, bf16[1,128,768]{1,2,0:T(8,128)(2,1)}, bf16[1,128,768]{1,2,0:T(8,128)(2,1)}, f32[1,128,768]{1,2,0:T(8,128)S(1)}, bf16[1,128,768]{1,2...) while((s32[]{:T(128)}, bf16[1,128,768]{1,2,0:T(8,128)(2,1)}, ...), condition=%wide.region_18.19_spmd.clone, body=%wide.region_16.18_spmd.clone.sunk | while | flops 128108816 | bytes 12827622 | solution.py:249
  198.4 7.5 collective-permute-done
  217.2 9.1 collective-permute-done
  236.0 9.8 collective-permute-done
  254.6 9.7 collective-permute-done
  272.3 8.8 collective-permute-done
  295.2 11.7 collective-permute-done.4
  311.9 11.8 collective-permute-done.5
  341.4 21.8 %reduce-scatter.19.cloned.1.call-done = f32[96,768]{1,0:T(8,128)} async-done(((f32[768,768]{1,0:T(8,128)}), f32[96,768]{1,0:T(8,128)}) %reduce-scatter.19.cloned.1.call-update) | async-done | bytes 294928
  365.0 69.8 %reduce-scatter.13.cloned.1.call-done = f32[96,768]{1,0:T(8,128)} async-done(((f32[768,768]{1,0:T(8,128)}), f32[96,768]{1,0:T(8,128)}) %reduce-scatter.13.cloned.1.call-update) | async-done | bytes 294928 | tf_op jit(solution)/shard_map/reduce_scatter | solution.py:277
  436.4 70.5 %reduce-scatter.21.cloned.1.call-done = f32[96,768]{1,0:T(8,128)} async-done(((f32[768,768]{1,0:T(8,128)}), f32[96,768]{1,0:T(8,128)}) %reduce-scatter.21.cloned.1.call-update) | async-done | bytes 294928
  508.7 70.4 %reduce-scatter.23.cloned.1.call-done = f32[96,768]{1,0:T(8,128)} async-done(((f32[768,768]{1,0:T(8,128)}), f32[96,768]{1,0:T(8,128)}) %reduce-scatter.23.cloned.1.call-update) | async-done | bytes 294928
  580.8 164.8 %reduce-scatter.15.cloned.1.call-done = f32[96,3072]{1,0:T(8,128)} async-done(((f32[768,3072]{1,0:T(8,128)}), f32[96,3072]{1,0:T(8,128)}) %reduce-scatter.15.cloned.1.call-update) | async-done | bytes 1179664 | tf_op jit(solution)/shard_map/reduce_scatter | solution.py:281
  747.8 164.4 %reduce-scatter.17.cloned.1.call-done = f32[384,768]{1,0:T(8,128)} async-done(((f32[3072,768]{1,0:T(8,128)}), f32[384,768]{1,0:T(8,128)}) %reduce-scatter.17.cloned.1.call-update) | async-done | bytes 1179664 | tf_op jit(solution)/shard_map/reduce_scatter | solution.py:283
  914.4 49.8 %all-reduce.23.cloned.1.call-done = (bf16[96,768]{0,1:T(8,128)(2,1)}, bf16[96,768]{0,1:T(8,128)(2,1)}, bf16[96,768]{0,1:T(8,128)(2,1)}, bf16[96,768]{1,0:T(8,128...) async-done(((bf16[96,768]{0,1:T(8,128)(2,1)}, bf16[96,768]{0,1:T(8,128)(2,1)}, bf16[96,768]{0,1:T(8,128)(2,1)}, bf16[96,768]{1,0:T(8,128)(2,1)}, ...) | async-done | bytes 1769488 | tf_op jit(solution)/shard_map/psum | solution.py:289
  976.3 37.9 %all-reduce.17 = (bf16[768]{0:T(1024)(128)(2,1)S(1)}, bf16[768]{0:T(1024)(128)(2,1)S(1)}, bf16[768]{0:T(1024)(128)(2,1)S(1)}, bf16[768]{0:T(1024)(128)(2,1)S(1)}...) all-reduce(f32[768]{0:T(1024)S(1)} %convert_reduce_fusion.4, ...), channel_id=5, replica_groups=mesh['row'=4,'seq'=8] {'seq'}, use_global_device_ids=true, to_apply=%region_22.23.clone | all-reduce | flops 9216 | bytes 55296
  1022.8 33.5 %all-reduce.18 = (bf16[768]{0:T(1024)(128)(2,1)S(1)}, bf16[768]{0:T(1024)(128)(2,1)S(1)}, bf16[768]{0:T(1024)(128)(2,1)S(1)}, bf16[768]{0:T(1024)(128)(2,1)S(1)}...) all-reduce(bf16[768]{0:T(1024)(128)(2,1)S(1)} %dynamic-update-slice, ...), channel_id=1, replica_groups=mesh['row'=4,'seq'=8] {'seq'}, use_global_device_ids=true, to_apply=%add | all-reduce | flops 6144 | bytes 24576
  1061.0 25.9 %all-gather.2 = bf16[8,1,384]{2,1,0:T(2,128)(2,1)S(1)} all-gather(bf16[1,1,384]{2,1,0:T(2,128)(2,1)S(1)} %reshape.941), channel_id=1, replica_groups=mesh['row'=4,'seq'=8] {'seq'}, dimensions={0}, use_global_device_ids=true | all-gather | bytes 6912 | tf_op jit(solution)/shard_map/all_gather | solution.py:336
  1099.2 36.8 %all-gather.18.cloned.1.call-done = bf16[768,768]{1,0:T(8,128)(2,1)} async-done(((bf16[96,768]{1,0:T(8,128)(2,1)}), bf16[768,768]{1,0:T(8,128)(2,1)}) %all-gather.18.cloned.1.call-update) | async-done | bytes 1179664 | tf_op jit(solution)/shard_map/all_gather | solution.py:321
  1138.7 77.9 %all-gather.20.cloned.1.call-done = bf16[768,3072]{1,0:T(8,128)(2,1)} async-done(((bf16[96,3072]{1,0:T(8,128)(2,1)}), bf16[768,3072]{1,0:T(8,128)(2,1)}) %all-gather.20.cloned.1.call-update) | async-done | bytes 4718608 | tf_op jit(solution)/shard_map/all_gather | solution.py:333
  1224.0 72.7 %all-gather.22.cloned.1.call-done = bf16[3072,768]{1,0:T(8,128)(2,1)} async-done(((bf16[384,768]{1,0:T(8,128)(2,1)}), bf16[3072,768]{1,0:T(8,128)(2,1)}) %all-gather.22.cloned.1.call-update) | async-done | bytes 4718608 | tf_op jit(solution)/shard_map/all_gather | solution.py:339
  (424 shorter events, 245.6 us)
Async XLA Ops:
  7.2 50.5 %all-gather.24.cloned.1.call-start = ((), (), s32[]{:S(2)}) async-start(), calls=%async_computation.15 | async-start | bytes 1769472 | tf_op jit(solution)/shard_map/all_gather | solution.py:162
  10.8 92.8 %all-gather.26.cloned.1.call-start = ((), (), s32[]{:S(2)}) async-start(), calls=%async_computation.16 | async-start | bytes 1769472 | tf_op jit(solution)/shard_map/all_gather | solution.py:163
  13.2 350.0 %reduce-scatter.19.cloned.1.call-start = ((), (), s32[]{:S(2)}) async-start(), calls=%async_computation.17 | async-start | bytes 2654208
  155.3 17.7 %collective-permute-start.3 = (bf16[1,128,768]{1,2,0:T(8,128)(2,1)}, bf16[1,128,768]{1,2,0:T(8,128)(2,1)S(1)}, u32[]{:S(2)}, u32[]{:S(2)}) collective-permute-start(bf16[1,128,768]{1,2,0:T(8,128)(2,1)} %get-tuple-element.1009), channel_id=1, source_target_pairs={{0,1},{1,2},{2,3},{3,4},{4,5},{5,6},{6,7},{7,0},{8,9},{9,10},{10,1... | collective-permute-start | bytes 589832 | tf_op jit(solution)/shard_map/while/body/eval_jaxpr/ppermute | solution.py:19
  175.2 17.1 %collective-permute-start.2 = (bf16[1,128,768]{1,2,0:T(8,128)(2,1)}, bf16[1,128,768]{1,2,0:T(8,128)(2,1)S(1)}, u32[]{:S(2)}, u32[]{:S(2)}) collective-permute-start(bf16[1,128,768]{1,2,0:T(8,128)(2,1)} %get-tuple-element.1008), channel_id=1, source_target_pairs={{0,1},{1,2},{2,3},{3,4},{4,5},{5,6},{6,7},{7,0},{8,9},{9,10},{10,1... | collective-permute-start | bytes 589832 | tf_op jit(solution)/shard_map/while/body/eval_jaxpr/ppermute | solution.py:19
  175.3 19.1 %collective-permute-start.3 = (bf16[1,128,768]{1,2,0:T(8,128)(2,1)}, bf16[1,128,768]{1,2,0:T(8,128)(2,1)S(1)}, u32[]{:S(2)}, u32[]{:S(2)}) collective-permute-start(bf16[1,128,768]{1,2,0:T(8,128)(2,1)} %get-tuple-element.1009), channel_id=1, source_target_pairs={{0,1},{1,2},{2,3},{3,4},{4,5},{5,6},{6,7},{7,0},{8,9},{9,10},{10,1... | collective-permute-start | bytes 589832 | tf_op jit(solution)/shard_map/while/body/eval_jaxpr/ppermute | solution.py:19
  195.1 17.6 %collective-permute-start.2 = (bf16[1,128,768]{1,2,0:T(8,128)(2,1)}, bf16[1,128,768]{1,2,0:T(8,128)(2,1)S(1)}, u32[]{:S(2)}, u32[]{:S(2)}) collective-permute-start(bf16[1,128,768]{1,2,0:T(8,128)(2,1)} %get-tuple-element.1008), channel_id=1, source_target_pairs={{0,1},{1,2},{2,3},{3,4},{4,5},{5,6},{6,7},{7,0},{8,9},{9,10},{10,1... | collective-permute-start | bytes 589832 | tf_op jit(solution)/shard_map/while/body/eval_jaxpr/ppermute | solution.py:19
  195.1 19.7 %collective-permute-start.3 = (bf16[1,128,768]{1,2,0:T(8,128)(2,1)}, bf16[1,128,768]{1,2,0:T(8,128)(2,1)S(1)}, u32[]{:S(2)}, u32[]{:S(2)}) collective-permute-start(bf16[1,128,768]{1,2,0:T(8,128)(2,1)} %get-tuple-element.1009), channel_id=1, source_target_pairs={{0,1},{1,2},{2,3},{3,4},{4,5},{5,6},{6,7},{7,0},{8,9},{9,10},{10,1... | collective-permute-start | bytes 589832 | tf_op jit(solution)/shard_map/while/body/eval_jaxpr/ppermute | solution.py:19
  215.5 17.1 %collective-permute-start.2 = (bf16[1,128,768]{1,2,0:T(8,128)(2,1)}, bf16[1,128,768]{1,2,0:T(8,128)(2,1)S(1)}, u32[]{:S(2)}, u32[]{:S(2)}) collective-permute-start(bf16[1,128,768]{1,2,0:T(8,128)(2,1)} %get-tuple-element.1008), channel_id=1, source_target_pairs={{0,1},{1,2},{2,3},{3,4},{4,5},{5,6},{6,7},{7,0},{8,9},{9,10},{10,1... | collective-permute-start | bytes 589832 | tf_op jit(solution)/shard_map/while/body/eval_jaxpr/ppermute | solution.py:19
  215.5 18.8 %collective-permute-start.3 = (bf16[1,128,768]{1,2,0:T(8,128)(2,1)}, bf16[1,128,768]{1,2,0:T(8,128)(2,1)S(1)}, u32[]{:S(2)}, u32[]{:S(2)}) collective-permute-start(bf16[1,128,768]{1,2,0:T(8,128)(2,1)} %get-tuple-element.1009), channel_id=1, source_target_pairs={{0,1},{1,2},{2,3},{3,4},{4,5},{5,6},{6,7},{7,0},{8,9},{9,10},{10,1... | collective-permute-start | bytes 589832 | tf_op jit(solution)/shard_map/while/body/eval_jaxpr/ppermute | solution.py:19
  235.0 17.9 %collective-permute-start.3 = (bf16[1,128,768]{1,2,0:T(8,128)(2,1)}, bf16[1,128,768]{1,2,0:T(8,128)(2,1)S(1)}, u32[]{:S(2)}, u32[]{:S(2)}) collective-permute-start(bf16[1,128,768]{1,2,0:T(8,128)(2,1)} %get-tuple-element.1009), channel_id=1, source_target_pairs={{0,1},{1,2},{2,3},{3,4},{4,5},{5,6},{6,7},{7,0},{8,9},{9,10},{10,1... | collective-permute-start | bytes 589832 | tf_op jit(solution)/shard_map/while/body/eval_jaxpr/ppermute | solution.py:19
  253.6 17.0 %collective-permute-start.3 = (bf16[1,128,768]{1,2,0:T(8,128)(2,1)}, bf16[1,128,768]{1,2,0:T(8,128)(2,1)S(1)}, u32[]{:S(2)}, u32[]{:S(2)}) collective-permute-start(bf16[1,128,768]{1,2,0:T(8,128)(2,1)} %get-tuple-element.1009), channel_id=1, source_target_pairs={{0,1},{1,2},{2,3},{3,4},{4,5},{5,6},{6,7},{7,0},{8,9},{9,10},{10,1... | collective-permute-start | bytes 589832 | tf_op jit(solution)/shard_map/while/body/eval_jaxpr/ppermute | solution.py:19
  293.1 141.7 %reduce-scatter.13.cloned.1.call-start = ((), (), s32[]{:S(2)}) async-start(), calls=%async_computation.9 | async-start | bytes 2654208 | tf_op jit(solution)/shard_map/reduce_scatter | solution.py:277
  295.0 211.8 %reduce-scatter.21.cloned.1.call-start = ((), (), s32[]{:S(2)}) async-start(), calls=%async_computation.18 | async-start | bytes 2654208
  311.8 267.3 %reduce-scatter.23.cloned.1.call-start = ((), (), s32[]{:S(2)}) async-start(), calls=%async_computation.19 | async-start | bytes 2654208
  328.6 417.0 %reduce-scatter.15.cloned.1.call-start = ((), (), s32[]{:S(2)}) async-start(), calls=%async_computation.11 | async-start | bytes 10616832 | tf_op jit(solution)/shard_map/reduce_scatter | solution.py:281
  335.0 577.2 %reduce-scatter.17.cloned.1.call-start = ((), (), s32[]{:S(2)}) async-start(), calls=%async_computation.13 | async-start | bytes 10616832 | tf_op jit(solution)/shard_map/reduce_scatter | solution.py:283
  341.3 622.9 %all-reduce.23.cloned.1.call-start = ((), (), s32[]{:S(2)}) async-start(), calls=%async_computation.20 | async-start | bytes 3833856 | tf_op jit(solution)/shard_map/psum | solution.py:289
  914.4 176.3 %all-gather.12.cloned.1.call-start = ((), (), s32[]{:S(2)}) async-start(), calls=%async_computation.6 | async-start | bytes 1327104 | tf_op jit(solution)/shard_map/all_gather | solution.py:306
  966.0 127.5 %all-gather.14.cloned.1.call-start = ((), (), s32[]{:S(2)}) async-start(), calls=%async_computation.7 | async-start | bytes 1327104 | tf_op jit(solution)/shard_map/all_gather | solution.py:312
  967.8 128.6 %all-gather.16.cloned.1.call-start = ((), (), s32[]{:S(2)}) async-start(), calls=%async_computation.8 | async-start | bytes 1327104 | tf_op jit(solution)/shard_map/all_gather | solution.py:315
  969.5 166.4 %all-gather.18.cloned.1.call-start = ((), (), s32[]{:S(2)}) async-start(), calls=%async_computation.10 | async-start | bytes 1327104 | tf_op jit(solution)/shard_map/all_gather | solution.py:321
  970.3 246.3 %all-gather.20.cloned.1.call-start = ((), (), s32[]{:S(2)}) async-start(), calls=%async_computation.12 | async-start | bytes 5308416 | tf_op jit(solution)/shard_map/all_gather | solution.py:333
  970.9 325.8 %all-gather.22.cloned.1.call-start = ((), (), s32[]{:S(2)}) async-start(), calls=%async_computation.14 | async-start | bytes 5308416 | tf_op jit(solution)/shard_map/all_gather | solution.py:339
  (77 other events, 879.6 us)
Sparse Core Ops, SparseCore 0:
  10.9 46.8 all-gather.23
  60.5 42.9 all-gather.25
  293.2 69.9 reduce-scatter.18
  366.5 68.1 reduce-scatter.12
  438.7 68.1 reduce-scatter.20
  510.8 68.1 reduce-scatter.22
  583.2 162.3 reduce-scatter.14
  749.8 162.3 reduce-scatter.16
  915.6 48.6 all-reduce.22
  966.8 41.6 all-gather.11
  1011.2 39.9 all-gather.13
  1053.8 39.9 all-gather.15
  1096.0 39.8 all-gather.17
  1137.9 78.6 all-gather.19
  1218.7 78.0 all-gather.21
where the time goes:
time: 1310 us
  waiting for transfers between devices  987 us (75%)
  blocking collectives  103 us (8%)
  matrix products  74.9 us (6%)
  other arithmetic  66.8 us (5%)
  local copies, waits for them, and re-layouts  46.1 us (4%)
  between operations  16.6 us (1%)
  starting transfers between devices  13.9 us (1%)
    reduce_scatter x1, waiting for transfers between devices, per_device(): lax.psum_scatter(up_weight_grad, 'seq', scatter_dimension=0, tiled=True)  165 us
    unnamed x18, waiting for transfers between devices  165 us
    reduce_scatter x1, waiting for transfers between devices, per_device(): lax.psum_scatter(down_weight_grad, 'seq', scatter_dimension=0, tiled=True)  164 us
    ppermute x30, waiting for transfers between devices, from_behind(): lax.ppermute(value, axis, [(i, (i + by) % count) for i in range(count)])  104 us
    all_gather x1, waiting for transfers between devices, per_device(): lax.all_gather(shares[9].astype(jnp.bfloat16), 'seq', axis=0, tiled=True)  77.9 us
    all_gather x1, waiting for transfers between devices, per_device(): lax.all_gather(shares[11].astype(jnp.bfloat16), 'seq', axis=0, tiled=True)  72.7 us
    unnamed x2, blocking collectives  71.3 us
    reduce_scatter x1, waiting for transfers between devices, per_device(): lax.psum_scatter(out_weight_grad, 'seq', scatter_dimension=0, tiled=True)  69.8 us
  transfers between devices with their start and end apart: 45, of which 38 were waited for; matrix products, arithmetic and copies ran while one was open for 9% of the time, Pallas kernels for 0%

commit v1 on v0

--- a/solution.py
+++ b/solution.py
@@ -4,6 +4,8 @@
 import jax
 import jax.numpy as jnp
 from jax import lax
+from jax.experimental import pallas as pl
+from jax.experimental.pallas import tpu as pltpu
 from jax.sharding import PartitionSpec as P
 
 H = 12
@@ -370,6 +372,852 @@
     )
 
 
+MESH = pl.DeviceIdType.MESH
+LANES = 128
+F32, BF16 = jnp.float32, jnp.bfloat16
+WAYS = 4
+DOWN, UP, ATTN = 0, 1, 2
+
+
+def dot(a, b):
+    return jnp.dot(a, b, preferred_element_type=F32)
+
+
+def dot_nt(a, b):
+    return lax.dot_general(a, b, (((1,), (1,)), ((), ())), preferred_element_type=F32)
+
+
+def dot_tn(a, b):
+    return lax.dot_general(a, b, (((0,), (0,)), ((), ())), preferred_element_type=F32)
+
+
+def rows_norm(value):
+    centre = jnp.mean(value, axis=-1, keepdims=True)
+    centered = value - centre
+    inverse = lax.rsqrt(jnp.mean(centered * centered, axis=-1, keepdims=True) + NORM_EPSILON)
+    return centered * inverse, inverse
+
+
+def rows_norm_back(scaled, unit, inverse):
+    first = jnp.mean(scaled, axis=-1, keepdims=True)
+    second = jnp.mean(scaled * unit, axis=-1, keepdims=True)
+    return inverse * (scaled - first - unit * second)
+
+
+def layer_kernel(
+    T,
+    D,
+    S,
+    entries,
+    frames,
+    cotangent,
+    lengths,
+    query_w,
+    key_w,
+    value_w,
+    out_w,
+    up_w,
+    down_w,
+    query_b,
+    value_b,
+    out_b,
+    gain1,
+    bias1,
+    up_b,
+    down_b,
+    gain2,
+    bias2,
+    encoded,
+    frames_grad,
+    vectors,
+    sum_down,
+    sum_up,
+    sum_attn,
+    fall,
+    wq,
+    wkv,
+    wo,
+    wup,
+    wdn,
+    kv,
+    qs,
+    qsT,
+    mask,
+    probs,
+    att32,
+    att16,
+    attf,
+    hq,
+    fq,
+    ar,
+    br,
+    asend,
+    bsend,
+    dgelu,
+    hid32,
+    unit1,
+    rstd1,
+    gmid,
+    gfirst,
+    gbr,
+    da16,
+    daT,
+    dq16,
+    dkvT,
+    ys,
+    yr,
+    own,
+    zl,
+    zr,
+    gm,
+    dr,
+    xs,
+    xr,
+    vl,
+    vr,
+    dxs,
+    dxr,
+    dxo,
+    stage,
+    vsend,
+    vrecv,
+    wsem,
+    frs,
+    fss,
+    fys,
+    msr,
+    mss,
+    zlr,
+    zls,
+    zrr,
+    zrs,
+    agzr,
+    agzs,
+    ag2r,
+    ag2s,
+    ag3r,
+    ag3s,
+    agdr,
+    agds,
+    lsem,
+):
+    HW, T2 = D // 2, 2 * T
+    blocks = HW // LANES
+    EIGHTH, SIXTEENTH = D // 8, D // 16
+    row, seq = lax.axis_index("row"), lax.axis_index("seq")
+    x, c = lax.div(row, 2), lax.rem(row, 2)
+    z, y = lax.div(seq, 2), lax.rem(seq, 2)
+    sib, xn, yn = (2 * x + 1 - c, seq), (2 * (1 - x) + c, seq), (row, 2 * z + 1 - y)
+    cross = (2 * (1 - x) + 1 - c, seq)
+    zp = (row, 2 * jnp.minimum(z + 1, 3) + y)
+    zm = (row, 2 * jnp.maximum(z - 1, 0) + y)
+    zz = (row, 2 * jnp.where(z < 2, z + 2, z - 2) + y)
+    z1 = (row, 2 * (z + 1 - 2 * lax.rem(z, 2)) + y)
+    not_first, not_last = z > 0, z < 3
+
+    def many(value, of):
+        return pl.multiple_of(value, of)
+
+    def at(start, size, of=None):
+        return pl.ds(many(start, size if of is None else of), size)
+
+    waits = []
+
+    def send(src, dst, ssem, rsem, device):
+        return pltpu.make_async_remote_copy(
+            src_ref=src, dst_ref=dst, send_sem=ssem, recv_sem=rsem, device_id=device, device_id_type=MESH
+        )
+
+    def start(src, dst, ssem, rsem, device, when=None):
+        copy = send(src, dst, ssem, rsem, device)
+        if when is None:
+            copy.start()
+            waits.append(copy.wait_send)
+        else:
+            pl.when(when)(copy.start)
+            waits.append(lambda: pl.when(when)(copy.wait_send))
+
+    def arrived(ref, rsem):
+        send(ref, ref, mss.at[0], rsem, sib).wait_recv()
+
+    names = {}
+
+    def one(name):
+        index = names.setdefault(name, len(names))
+        return mss.at[index], msr.at[index]
+
+    loads = [
+        pltpu.make_async_copy(query_w.at[:, at(HW * y, HW)], wq, wsem.at[0]),
+        pltpu.make_async_copy(key_w.at[:, at(HW * y, HW)], wkv.at[:, pl.ds(0, HW)], wsem.at[1]),
+        pltpu.make_async_copy(value_w.at[:, at(HW * y, HW)], wkv.at[:, pl.ds(HW, HW)], wsem.at[2]),
+        pltpu.make_async_copy(out_w, wo, wsem.at[3]),
+        pltpu.make_async_copy(up_w, wup, wsem.at[4]),
+        pltpu.make_async_copy(down_w, wdn, wsem.at[5]),
+    ]
+    for load in loads:
+        load.start()
+    barrier = pltpu.get_barrier_semaphore()
+    for device, when in ((sib, None), (xn, None), (yn, None), (zz, None), (cross, None), (zp, not_last), (zm, not_first)):
+
+        def greet(device=device):
+            pl.semaphore_signal(barrier, inc=1, device_id=device, device_id_type=MESH)
+
+        greet() if when is None else pl.when(when)(greet)
+    fall[at(T * seq, T), :] = frames[...].astype(BF16)
+    vectors[...] = jnp.zeros_like(vectors)
+
+    @pl.when(z == 0)
+    def _():
+        zl[...] = jnp.zeros_like(zl)
+        vl[...] = jnp.zeros_like(vl)
+
+    @pl.when(z == 3)
+    def _():
+        zr[...] = jnp.zeros_like(zr)
+        vr[...] = jnp.zeros_like(vr)
+
+    pl.semaphore_wait(barrier, jnp.where(not_first & not_last, 7, 6))
+
+    def slab(z_, y_):
+        return fall.at[at(T * (2 * z_ + y_), T), :]
+
+    def push(z_, direction):
+        device = (zp, zm, yn)[direction]
+        sem = fss.at[direction, z_]
+        return send(slab(z_, y), slab(z_, y), sem, frs.at[2 * z_ + y], device)
+
+    bias_kv = jnp.concatenate([jnp.zeros((1, HW), F32), value_b[:, at(HW * y, HW)]], axis=1)
+
+    def keys_values(z_, y_):
+        rows = at(T * (2 * z_ + y_), T)
+        kv[rows, :] = (dot(fall[rows, :], wkv[...]) + bias_kv).astype(BF16)
+
+    pl.when(not_last)(lambda: push(z, 0).start())
+    pl.when(not_first)(lambda: push(z, 1).start())
+    push(z, 2).start()
+    loads[1].wait()
+    loads[2].wait()
+    keys_values(z, y)
+
+    @pl.loop(0, 4)
+    def _(k):
+        left, right = z - k - 1, z + k + 1
+
+        @pl.when(left >= 0)
+        def _():
+            arrived(slab(left, y), frs.at[2 * left + y])
+            pl.when(not_last)(lambda: push(left, 0).start())
+            push(left, 2).start()
+
+        @pl.when(right <= 3)
+        def _():
+            arrived(slab(right, y), frs.at[2 * right + y])
+            pl.when(not_first)(lambda: push(right, 1).start())
+            push(right, 2).start()
+
+        pl.when(left >= 0)(lambda: keys_values(left, y))
+        pl.when(right <= 3)(lambda: keys_values(right, y))
+
+        @pl.when(z - k >= 0)
+        def _():
+            arrived(slab(z - k, 1 - y), frs.at[2 * (z - k) + 1 - y])
+            keys_values(z - k, 1 - y)
+
+        @pl.when((k > 0) & (z + k <= 3))
+        def _():
+            arrived(slab(z + k, 1 - y), frs.at[2 * (z + k) + 1 - y])
+            keys_values(z + k, 1 - y)
+
+    def frames_sent():
+        @pl.loop(0, 4)
+        def _(j):
+            push(j, 2).wait_send()
+            pl.when(not_last & (j <= z))(lambda: push(j, 0).wait_send())
+            pl.when(not_first & (j >= z))(lambda: push(j, 1).wait_send())
+
+    waits.append(frames_sent)
+    pair_rows = at(T2 * z, T2)
+    loads[0].wait()
+    query = (dot(fall[pair_rows, :], wq[...]) + query_b[:, at(HW * y, HW)]).astype(BF16).astype(F32)
+    query = query * HD ** (-0.5)
+    qs[...] = query.astype(BF16)
+    qsT[...] = query.T.astype(BF16)
+    key_at = lax.broadcasted_iota(jnp.int32, (1, S), 1)
+    query_at = lax.broadcasted_iota(jnp.int32, (T2, 1), 0) + T2 * z
+    key_number, query_number = jnp.zeros((1, S), jnp.int32), jnp.zeros((T2, 1), jnp.int32)
+    clip_end = jnp.int32(0)
+    for entry in range(entries):
+        clip_end = clip_end + lengths[0, entry]
+        key_number = key_number + jnp.where(clip_end <= key_at, 1, 0)
+        query_number = query_number + jnp.where(clip_end <= query_at, 1, 0)
+    mask[...] = jnp.where(query_number == key_number, 0.0, MASK_SCORE)
+
+    low_half = lax.broadcasted_iota(jnp.int32, (T2, LANES), 1) < HD
+
+    def half(value, which):
+        return jnp.where(low_half == (which == 0), value, 0.0)
+
+    @pl.loop(0, blocks)
+    def _(b):
+        lanes, value_lanes = at(LANES * b, LANES), at(HW + LANES * b, LANES, LANES)
+        queries = qs[:, lanes].astype(F32)
+        outs = []
+        for which in range(2):
+            scores = dot_nt(half(queries, which).astype(BF16), kv[:, lanes]) + mask[...]
+            powers = jnp.exp(scores - jnp.max(scores, axis=-1, keepdims=True))
+            low = (powers * (1.0 / jnp.sum(powers, axis=-1, keepdims=True))).astype(BF16)
+            probs[2 * b + which] = low
+            outs.append(dot(low, kv[:, value_lanes]))
+        out = jnp.where(low_half, outs[0], outs[1])
+        att32[:, lanes] = out
+        att16[:, lanes] = out.astype(BF16)
+
+    mine, other = at(T * y, T), at(T * (1 - y), T)
+    heads_here = at(HW * y, HW)
+    start(att16.at[other, :], attf.at[:, heads_here], *one("att"), yn)
+    attf[:, heads_here] = att16[mine, :]
+    loads[3].wait()
+    arrived(attf.at[:, at(HW * (1 - y), HW)], one("att")[1])
+    branch = dot(attf[...], wo[...]) + out_b[...]
+    unit, inverse = rows_norm(frames[...] + branch)
+    hidden = unit * gain1[...] + bias1[...]
+    unit1[...] = unit
+    rstd1[...] = jnp.broadcast_to(inverse, (T, LANES))
+    hid32[...] = hidden
+    hq[at(T * row, T), :] = hidden.astype(BF16)
+    hidden_here = hq.at[at(T * row, T), :]
+    start(hidden_here, hidden_here, *one("hid_x"), xn)
+    start(hidden_here, hidden_here, *one("hid_d"), sib)
+
+    def quad(order):
+        x_ = jnp.where(order < 2, 1 - x, x)
+        c_ = jnp.where(lax.rem(order, 2) == 0, c, 1 - c)
+        return 2 * x_ + c_
+
+    def spread(sent, got, ssem, rsem, to):
+        @pl.when(to != row)
+        def _():
+            send(sent.at[to], got.at[at(T * row, T), :], ssem.at[to], rsem.at[row], (to, seq)).start()
+
+    def spread_sent(sent, ssem):
+        @pl.loop(0, 4)
+        def _(to):
+            @pl.when(to != row)
+            def _():
+                send(sent.at[to], sent.at[to], ssem.at[to], ssem.at[to], sib).wait_send()
+
+    def spread_arrived(got, rsem):
+        @pl.loop(0, 4)
+        def _(source):
+            pl.when(source != row)(lambda: arrived(got.at[at(T * source, T), :], rsem.at[source]))
+
+    loads[4].wait()
+    scale = 2.0 ** -0.5
+
+    @pl.loop(0, 4)
+    def _(order):
+        to = quad(order)
+        columns = at(D * to, D)
+        before = dot(hidden_here[...], wup[:, columns]) + up_b[:, columns]
+        rise = 0.5 * (1.0 + lax.erf(before * scale))
+        dgelu[to] = rise + before * jnp.exp(-0.5 * before * before) * (2.0 * math.pi) ** -0.5
+        asend[to] = (before * rise).astype(BF16)
+        spread(asend, ar, fys.at[0], fys.at[1], to)
+
+    waits.append(lambda: spread_sent(asend, fys.at[0]))
+    ar[at(T * row, T), :] = asend[row]
+    loads[5].wait()
+    fed = hid32[...] + down_b[...]
+    for quarter in range(4):
+        fed = fed + dot(asend[quarter], wdn[pl.ds(D * quarter, D), :])
+    unit2, inverse2 = rows_norm(fed)
+    encoded[...] = unit2 * gain2[...] + bias2[...]
+    cot = cotangent[...]
+    grad_mid = rows_norm_back(cot * gain2[...], unit2, inverse2)
+    vectors[10:11, :] = jnp.sum(cot * unit2, axis=0, keepdims=True)
+    vectors[11:12, :] = jnp.sum(cot, axis=0, keepdims=True)
+    gmid[...] = grad_mid
+    fq[at(T * row, T), :] = grad_mid.astype(BF16)
+    ffn_here = fq.at[at(T * row, T), :]
+    start(ffn_here, ffn_here, *one("ffn_x"), xn)
+    start(ffn_here, ffn_here, *one("ffn_d"), sib)
+    vectors[9:10, :] = jnp.sum(ffn_here[...].astype(F32), axis=0, keepdims=True)
+
+    @pl.loop(0, 4)
+    def _(order):
+        to = quad(order)
+        quarter = at(D * to, D)
+        back = dot_nt(ffn_here[...], wdn[quarter, :]) * dgelu[to]
+        low = back.astype(BF16)
+        bsend[to] = low
+        spread(bsend, br, fys.at[2], fys.at[3], to)
+        vectors[pl.ds(5 + to, 1), :] = jnp.sum(low.astype(F32), axis=0, keepdims=True)
+        gmid[...] += dot_nt(low, wup[:, quarter])
+
+    waits.append(lambda: spread_sent(bsend, fys.at[2]))
+    br[at(T * row, T), :] = bsend[row]
+    grad_hidden = gmid[...]
+    unit = unit1[...]
+    grad_first = rows_norm_back(grad_hidden * gain1[...], unit, rstd1[:, 0:1])
+    vectors[3:4, :] = jnp.sum(grad_hidden * unit, axis=0, keepdims=True)
+    vectors[4:5, :] = jnp.sum(grad_hidden, axis=0, keepdims=True)
+    gfirst[...] = grad_first
+    gbr[mine, :] = grad_first.astype(BF16)
+    vectors[2:3, :] = jnp.sum(gbr[mine, :].astype(F32), axis=0, keepdims=True)
+    start(gbr.at[mine, :], gbr.at[mine, :], *one("gbr"), yn)
+
+    from_x, from_d, from_xd = 2 * (1 - x) + c, 2 * x + 1 - c, 2 * (1 - x) + 1 - c
+
+    def pass_on(buffer, name):
+        part = buffer.at[at(T * from_x, T), :]
+        arrived(part, one(name + "_x")[1])
+        start(part, part, *one(name + "_xd"), sib)
+
+    def quad_ready(buffer, name):
+        arrived(buffer.at[at(T * from_d, T), :], one(name + "_d")[1])
+        arrived(buffer.at[at(T * from_xd, T), :], one(name + "_xd")[1])
+
+    pass_on(hq, "hid")
+    pass_on(fq, "ffn")
+
+    def y_send(t, left, right):
+        ys[t] = dot_tn(left[:, at(HW * (1 - y), HW)], right[...]).astype(BF16)
+        start(ys.at[t], yr.at[t], *one(("y", t)), yn)
+        own[t] = dot_tn(left[:, at(HW * y, HW)], right[...])
+
+    def y_add(t):
+        arrived(yr.at[t], one(("y", t))[1])
+        own[t] += yr[t].astype(F32)
+
+    def z_step(t, i):
+        j = 3 - i
+        pl.when(not_first & (z < j))(lambda: arrived(zl.at[t, j], zlr.at[t, j]))
+
+        @pl.when(z < j)
+        def _():
+            zl[t, j] = (own[t, pl.ds(EIGHTH * j, EIGHTH), :] + zl[t, j].astype(F32)).astype(BF16)
+
+        start(zl.at[t, j], zl.at[t, j], zls.at[t, j], zlr.at[t, j], zp, z < j)
+        j_ = i
+        pl.when(not_last & (z > j_))(lambda: arrived(zr.at[t, j_], zrr.at[t, j_]))
+
+        @pl.when(z > j_)
+        def _():
+            zr[t, j_] = (own[t, pl.ds(EIGHTH * j_, EIGHTH), :] + zr[t, j_].astype(F32)).astype(BF16)
+
+        start(zr.at[t, j_], zr.at[t, j_], zrs.at[t, j_], zrr.at[t, j_], zm, z > j_)
+
+    def z_end(t):
+        pl.when(not_first)(lambda: arrived(zl.at[t, z], zlr.at[t, z]))
+        pl.when(not_last)(lambda: arrived(zr.at[t, z], zrr.at[t, z]))
+        total = own[t, at(EIGHTH * z, EIGHTH), :] + zl[t, z].astype(F32) + zr[t, z].astype(F32)
+        stage[t] = total.astype(BF16)
+
+    def tile(t, h, q_, z_, y_):
+        first = HW * y_ + EIGHTH * z_ + SIXTEENTH * h
+        if t == UP:
+            return sum_up.at[at(first, SIXTEENTH), at(D * q_, D)]
+        whole = sum_down if t == DOWN else sum_attn
+        return whole.at[at(D * q_ + first, SIXTEENTH), :]
+
+    def gather_state(t, h):
+        u = 2 * t + h
+        over_y, over_x = (row, 1 - y), (from_x, y)
+        second, third = ((over_y, yn), (over_x, xn)) if h == 0 else ((over_x, xn), (over_y, yn))
+        both = (from_x, 1 - y)
+        return u, second, third, both
+
+    def gather_send(t, h, place, z_, ssem, rsem, device, src=None):
+        there = tile(t, h, place[0], z_, place[1])
+        return send(there if src is None else src, there, ssem, rsem, device)
+
+    def to_next(t, h, z_, src=None):
+        u, second, third, _ = gather_state(t, h)
+        here = (row, y)
+        gather_send(t, h, here, z_, ag2s.at[u, z_], ag2r.at[u, z_], second[1], src).start()
+        gather_send(t, h, here, z_, ag3s.at[u, z_], ag3r.at[u, z_], third[1], src).start()
+        gather_send(t, h, here, z_, agds.at[u], agdr.at[u], sib, src).start()
+
+    def along_z(t, h, z_, direction, src=None):
+        u = 2 * t + h
+        return gather_send(
+            t, h, (row, y), z_, agzs.at[u, direction, z_], agzr.at[u, z_], (zp, zm)[direction], src
+        )
+
+    def gather_own(t):
+        for h in range(2):
+            src = stage.at[t, pl.ds(SIXTEENTH * h, SIXTEENTH), :]
+            pltpu.make_async_copy(src, tile(t, h, row, z, y), lsem.at[2 * t + h]).start()
+            pl.when(not_last)(lambda: along_z(t, h, z, 0, src).start())
+            pl.when(not_first)(lambda: along_z(t, h, z, 1, src).start())
+            to_next(t, h, z, src)
+
+    def gather_z(t, k):
+        for h in range(2):
+            u = 2 * t + h
+            left, right = z - k, z + k
+
+            @pl.when(left >= 0)
+            def _():
+                arrived(tile(t, h, row, left, y), agzr.at[u, left])
+                pl.when(not_last)(lambda: along_z(t, h, left, 0).start())
+                to_next(t, h, left)
+
+            @pl.when(right <= 3)
+            def _():
+                arrived(tile(t, h, row, right, y), agzr.at[u, right])
+                pl.when(not_first)(lambda: along_z(t, h, right, 1).start())
+                to_next(t, h, right)
+
+    def gather_second(t, k):
+        for h in range(2):
+            u, second, third, _ = gather_state(t, h)
+
+            def take(z_):
+                place = second[0]
+                arrived(tile(t, h, place[0], z_, place[1]), ag2r.at[u, z_])
+                gather_send(t, h, place, z_, ag3s.at[u, 4 + z_], ag3r.at[u, 4 + z_], third[1]).start()
+                gather_send(t, h, place, z_, agds.at[u], agdr.at[u], sib).start()
+
+            pl.when(z - k >= 0)(lambda: take(z - k))
+            pl.when((k > 0) & (z + k <= 3))(lambda: take(z + k))
+
+    def gather_third(t, k):
+        for h in range(2):
+            u, second, third, both = gather_state(t, h)
+
+            def take(z_):
+                for offset, place in ((0, third[0]), (4, both)):
+                    arrived(tile(t, h, place[0], z_, place[1]), ag3r.at[u, offset + z_])
+                    gather_send(t, h, place, z_, agds.at[u], agdr.at[u], sib).start()
+
+            pl.when(z - k >= 0)(lambda: take(z - k))
+            pl.when((k > 0) & (z + k <= 3))(lambda: take(z + k))
+
+    def gather_end(t):
+        for h in range(2):
+            u = 2 * t + h
+            part = tile(t, h, row, z, y)
+            pltpu.make_async_copy(stage.at[t, pl.ds(SIXTEENTH * h, SIXTEENTH), :], part, lsem.at[u]).wait()
+
+            @pl.loop(0, 4)
+            def _(j):
+                pl.when(not_last & (j <= z))(lambda: along_z(t, h, j, 0).wait_send())
+                pl.when(not_first & (j >= z))(lambda: along_z(t, h, j, 1).wait_send())
+                send(part, part, ag2s.at[u, j], ag2r.at[u, j], sib).wait_send()
+                send(part, part, ag3s.at[u, j], ag3r.at[u, j], sib).wait_send()
+                send(part, part, ag3s.at[u, 4 + j], ag3r.at[u, 4 + j], sib).wait_send()
+
+            whole = sum_down.at[pl.ds(0, D), :]
+            send(whole, whole, agds.at[u], agdr.at[u], sib).wait()
+
+    arrived(gbr.at[other, :], one("gbr")[1])
+    da = dot_nt(gbr[...], wo[heads_here, :]).astype(BF16)
+    da16[...] = da
+    daT[...] = da.astype(F32).T.astype(BF16)
+    gm[3] = dot_tn(att16[...], gbr[...]).astype(BF16)
+
+    quad_ready(fq, "ffn")
+    spread_arrived(ar, fys.at[1])
+    y_send(DOWN, ar, fq)
+
+    def attention_back(b):
+        lanes, value_lanes = at(LANES * b, LANES), at(HW + LANES * b, LANES, LANES)
+        heads = da16[:, lanes].astype(F32)
+        product = heads * att32[:, lanes]
+        parts = []
+        for which in range(2):
+            delta = jnp.sum(half(product, which), axis=-1, keepdims=True)
+            grad_probs = dot_nt(half(heads, which).astype(BF16), kv[:, value_lanes])
+            low = probs[2 * b + which]
+            grad_scores = (low.astype(F32) * (grad_probs - delta)).astype(BF16)
+            parts.append(dot(grad_scores, kv[:, lanes]))
+            head = at(LANES * b + HD * which, HD)
+            dkvT[head, :] = dot(qsT[head, :], grad_scores).astype(BF16)
+            dkvT[at(HW + LANES * b + HD * which, HD), :] = dot(daT[head, :], low).astype(BF16)
+        dq16[:, lanes] = (jnp.where(low_half, parts[0], parts[1]) * HD ** (-0.5)).astype(BF16)
+
+    @pl.loop(0, blocks)
+    def _(b):
+        attention_back(b)
+
+    quad_ready(hq, "hid")
+    spread_arrived(br, fys.at[3])
+    y_send(UP, hq, br)
+    y_add(DOWN)
+    for i in range(3):
+        z_step(DOWN, i)
+
+    gm[0] = dot_tn(dq16[...], fall[pair_rows, :]).astype(BF16)
+    for matrix in range(2):
+        gm[1 + matrix] = dot(dkvT[pl.ds(HW * matrix, HW), :], fall[...]).astype(BF16)
+    vectors[0:1, heads_here] = jnp.sum(dq16[...].astype(F32), axis=0, keepdims=True)
+    ones = jnp.ones((8, S), BF16)
+    vectors[1:2, heads_here] = dot_nt(ones, dkvT[pl.ds(HW, HW), :])[0:1, :]
+    for slot in range(2):
+        start(gm.at[1 - c + 2 * slot], dr.at[slot], *one(("d", slot)), sib)
+    z_end(DOWN)
+    gather_own(DOWN)
+    for slot in range(2):
+        arrived(dr.at[slot], one(("d", slot))[1])
+    xs[...] = (gm[c + 2 * (1 - x)].astype(F32) + dr[1 - x].astype(F32)).astype(BF16)
+    start(xs, xr, *one("xs"), xn)
+    own[ATTN] = gm[c + 2 * x].astype(F32) + dr[x].astype(F32)
+    y_add(UP)
+    for i in range(3):
+        z_step(UP, i)
+    gather_z(DOWN, 1)
+    gather_second(DOWN, 0)
+    z_end(UP)
+    gather_own(UP)
+    arrived(xr, one("xs")[1])
+    own[ATTN] += xr[...].astype(F32)
+    for i in range(3):
+        z_step(ATTN, i)
+    gather_z(DOWN, 2)
+    gather_second(DOWN, 1)
+    gather_third(DOWN, 0)
+    gather_z(UP, 1)
+    gather_second(UP, 0)
+    z_end(ATTN)
+    gather_own(ATTN)
+
+    def kv_step(i):
+        j = 3 - i
+        pl.when(not_first & (z < j))(lambda: arrived(vl.at[j], zlr.at[3, j]))
+
+        @pl.when(z < j)
+        def _():
+            vl[j] = (dkvT[:, pl.ds(T2 * j, T2)].astype(F32) + vl[j].astype(F32)).astype(BF16)
+
+        start(vl.at[j], vl.at[j], zls.at[3, j], zlr.at[3, j], zp, z < j)
+        j_ = i
+        pl.when(not_last & (z > j_))(lambda: arrived(vr.at[j_], zrr.at[3, j_]))
+
+        @pl.when(z > j_)
+        def _():
+            vr[j_] = (dkvT[:, pl.ds(T2 * j_, T2)].astype(F32) + vr[j_].astype(F32)).astype(BF16)
+
+        start(vr.at[j_], vr.at[j_], zrs.at[3, j_], zrr.at[3, j_], zm, z > j_)
+
+    for i in range(3):
+        kv_step(i)
+
+    def vector_step(i, device):
+        vsend[i] = vectors[...]
+        start(vsend.at[i], vrecv.at[i], *one(("v", i)), device)
+        arrived(vrecv.at[i], one(("v", i))[1])
+        vectors[...] += vrecv[i]
+
+    gather_z(DOWN, 3)
+    gather_second(DOWN, 2)
+    gather_third(DOWN, 1)
+    vector_step(0, sib)
+    gather_z(UP, 2)
+    gather_second(UP, 1)
+    gather_third(UP, 0)
+    vector_step(1, xn)
+    gather_z(ATTN, 1)
+    gather_second(ATTN, 0)
+    gather_second(DOWN, 3)
+    gather_third(DOWN, 2)
+    vector_step(2, yn)
+    gather_z(UP, 3)
+    gather_second(UP, 2)
+    gather_third(UP, 1)
+    vector_step(3, z1)
+    gather_z(ATTN, 2)
+    gather_second(ATTN, 1)
+    gather_third(ATTN, 0)
+    gather_third(DOWN, 3)
+    vector_step(4, zz)
+
+    pl.when(not_first)(lambda: arrived(vl.at[z], zlr.at[3, z]))
+    pl.when(not_last)(lambda: arrived(vr.at[z], zrr.at[3, z]))
+    total = dkvT[:, pair_rows].astype(F32) + vl[z].astype(F32) + vr[z].astype(F32)
+    into = dot_nt(total.T.astype(BF16), wkv[...]) + dot_nt(dq16[...], wq[...])
+    dxo[...] = into
+    dxs[...] = dxo[other, :].astype(BF16)
+    start(dxs, dxr, *one("dx"), yn)
+
+    gather_z(ATTN, 3)
+    gather_second(UP, 3)
+    gather_third(UP, 2)
+    gather_second(ATTN, 2)
+    gather_third(ATTN, 1)
+    arrived(dxr, one("dx")[1])
+    frames_grad[...] = gfirst[...] + dxo[mine, :] + dxr[...].astype(F32)
+    gather_third(UP, 3)
+    gather_second(ATTN, 3)
+    gather_third(ATTN, 2)
+    gather_third(ATTN, 3)
+    for t in (DOWN, UP, ATTN):
+        gather_end(t)
+    for wait in waits:
+        wait()
+
+
+def fused_layer(
+    frames,
+    clip_lengths,
+    query_weight,
+    query_bias,
+    key_weight,
+    value_weight,
+    value_bias,
+    out_weight,
+    out_bias,
+    norm1_gain,
+    norm1_bias,
+    up_weight,
+    up_bias,
+    down_weight,
+    down_bias,
+    norm2_gain,
+    norm2_bias,
+    cotangent,
+):
+    T, D = frames.shape[1], frames.shape[2]
+    F = up_weight.shape[1]
+    S = T * lax.axis_size("seq")
+    HW, T2, EIGHTH = D // 2, 2 * T, D // 8
+    blocks = HW // LANES
+    entries = clip_lengths.shape[1]
+    vmem, smem, hbm = (
+        pl.BlockSpec(memory_space=pltpu.VMEM),
+        pl.BlockSpec(memory_space=pltpu.SMEM),
+        pl.BlockSpec(memory_space=pl.ANY),
+    )
+    dma = pltpu.SemaphoreType.DMA
+    low, wide = (lambda *shape: pltpu.VMEM(shape, BF16)), (lambda *shape: pltpu.VMEM(shape, F32))
+    scratch = dict(
+        fall=low(S, D),
+        wq=low(D, HW),
+        wkv=low(D, D),
+        wo=low(D, D),
+        wup=low(D, F),
+        wdn=low(F, D),
+        kv=low(S, D),
+        qs=low(T2, HW),
+        qsT=low(HW, T2),
+        mask=wide(T2, S),
+        probs=low(2 * blocks, T2, S),
+        att32=wide(T2, HW),
+        att16=low(T2, HW),
+        attf=low(T, D),
+        hq=low(4 * T, D),
+        fq=low(4 * T, D),
+        ar=low(4 * T, D),
+        br=low(4 * T, D),
+        asend=low(4, T, D),
+        bsend=low(4, T, D),
+        dgelu=wide(4, T, D),
+        hid32=wide(T, D),
+        unit1=wide(T, D),
+        rstd1=wide(T, LANES),
+        gmid=wide(T, D),
+        gfirst=wide(T, D),
+        gbr=low(T2, D),
+        da16=low(T2, HW),
+        daT=low(HW, T2),
+        dq16=low(T2, HW),
+        dkvT=low(D, S),
+        ys=low(2, HW, D),
+        yr=low(2, HW, D),
+        own=wide(3, HW, D),
+        zl=low(3, 4, EIGHTH, D),
+        zr=low(3, 4, EIGHTH, D),
+        gm=low(4, HW, D),
+        dr=low(2, HW, D),
+        xs=low(HW, D),
+        xr=low(HW, D),
+        vl=low(4, D, T2),
+        vr=low(4, D, T2),
+        dxs=low(T, D),
+        dxr=low(T, D),
+        dxo=wide(T2, D),
+        stage=low(3, EIGHTH, D),
+        vsend=wide(5, 16, D),
+        vrecv=wide(5, 16, D),
+        wsem=dma((6,)),
+        frs=dma((8,)),
+        fss=dma((3, 4)),
+        fys=dma((4, 4)),
+        msr=dma((24,)),
+        mss=dma((24,)),
+        zlr=dma((4, 4)),
+        zls=dma((4, 4)),
+        zrr=dma((4, 4)),
+        zrs=dma((4, 4)),
+        agzr=dma((6, 4)),
+        agzs=dma((6, 2, 4)),
+        ag2r=dma((6, 4)),
+        ag2s=dma((6, 4)),
+        ag3r=dma((6, 8)),
+        ag3s=dma((6, 8)),
+        agdr=dma((6,)),
+        agds=dma((6,)),
+        lsem=dma((6,)),
+    )
+    encoded, frames_grad, vectors, sum_down, sum_up, sum_attn = pl.pallas_call(
+        partial(layer_kernel, T, D, S, entries),
+        out_shape=(
+            jax.ShapeDtypeStruct((T, D), F32),
+            jax.ShapeDtypeStruct((T, D), F32),
+            jax.ShapeDtypeStruct((16, D), F32),
+            jax.ShapeDtypeStruct((F, D), BF16),
+            jax.ShapeDtypeStruct((D, F), BF16),
+            jax.ShapeDtypeStruct((4 * D, D), BF16),
+        ),
+        in_specs=[vmem, vmem, smem] + [hbm] * 6 + [vmem] * 9,
+        out_specs=(vmem, vmem, vmem, hbm, hbm, hbm),
+        scratch_shapes=list(scratch.values()),
+        compiler_params=pltpu.CompilerParams(
+            collective_id=0, has_side_effects=True, vmem_limit_bytes=63 << 20
+        ),
+        name="layer",
+    )(
+        frames[0],
+        cotangent[0],
+        clip_lengths,
+        query_weight,
+        key_weight,
+        value_weight,
+        out_weight,
+        up_weight,
+        down_weight,
+        query_bias[None],
+        value_bias[None],
+        out_bias[None],
+        norm1_gain[None],
+        norm1_bias[None],
+        up_bias[None],
+        down_bias[None],
+        norm2_gain[None],
+        norm2_bias[None],
+    )
+    attn = [sum_attn[D * m : D * (m + 1)].astype(F32) for m in range(4)]
+    return (
+        encoded[None],
+        frames_grad[None],
+        attn[0].T,
+        vectors[0],
+        attn[1].T,
+        attn[2].T,
+        vectors[1],
+        attn[3],
+        vectors[2],
+        vectors[3],
+        vectors[4],
+        sum_up.astype(F32),
+        vectors[5:9].reshape(F),
+        sum_down.astype(F32),
+        vectors[9],
+        vectors[10],
+        vectors[11],
+    )
+
+
 def solution(mesh):
     in_specs = (
         P("row", "seq", None),
@@ -410,6 +1258,8 @@
         P(),
         P(),
     )
+    shape = dict(mesh.shape)
+    fused = shape["row"] == 4 and shape["seq"] == 8
     return jax.shard_map(
-        per_device, mesh=mesh, in_specs=in_specs, out_specs=out_specs, check_vma=False
-    )
+        fused_layer if fused else per_device, mesh=mesh, in_specs=in_specs, out_specs=out_specs, check_vma=False
+    )

time: 1310 us -> 251 us (0.19)
  waiting for transfers between devices: 987 us -> 0 us
  Pallas kernels: 0 us -> 212 us
  blocking collectives: 103 us -> 0 us
  matrix products: 74.9 us -> 0 us
  other arithmetic: 66.8 us -> 15.1 us
  local copies, waits for them, and re-layouts: 46.1 us -> 22.7 us
  between operations: 16.6 us -> 0.68 us
  starting transfers between devices: 13.9 us -> 0 us
    reduce_scatter x3 -> x0, waiting for transfers between devices: 399 us -> none  [the longest x1 165 us: per_device(): lax.psum_scatter(up_weight_grad, 'seq', scatter_dimension=0, tiled=True)]
    all_gather x8 -> x0, waiting for transfers between devices: 270 us -> none  [the longest x1 77.9 us: per_device(): lax.all_gather(shares[9].astype(jnp.bfloat16), 'seq', axis=0, tiled=True)]
    pallas_call x0 -> x1, Pallas kernels: none -> 212 us  [fused_layer(): pl.pallas_call(partial(layer_kernel, T, D, S, entries), out_shape=(jax.Sh...]
    unnamed x18 -> x0, waiting for transfers between devices: 165 us -> none
    ppermute x30 -> x0, waiting for transfers between devices: 104 us -> none  [from_behind(): lax.ppermute(value, axis, [(i, (i + by) % count) for i in range(count)])]
    dot_general x62 -> x0, matrix products: 74.9 us -> none  [the longest x6 17.9 us: matrix_grad(): jnp.einsum('rsk,rsn->kn', inputs, upstream, preferred_element_type=jnp.fl...]
    unnamed x2 -> x0, blocking collectives: 71.3 us -> none
    psum x1 -> x0, waiting for transfers between devices: 49.8 us -> none  [per_device(): lax.psum(shares[0].astype(jnp.bfloat16), 'row').astype(jnp.float32)]
  transfers between devices with their start and end apart: 45 -> 0, of which waited for: 38 -> 0; matrix products, arithmetic and copies ran while one was open for 9% -> 0% of each run, Pallas kernels for 0% -> 0%
where the time goes in v1:
time: 251 us; the launch traced here: 250 us
  Pallas kernels  212 us (84%)
  local copies, waits for them, and re-layouts  22.7 us (9%)
  other arithmetic  15.1 us (6%)
    pallas_call x1, Pallas kernels, fused_layer(): pl.pallas_call(partial(layer_kernel, T, D, S, entries), out_shape=(jax.Sh...  212 us
    unnamed x15, local copies, waits for them, and re-layouts  9.54 us
    convert_element_type x1, other arithmetic, fused_layer(): sum_up.astype(F32)  7.52 us

profile of v1, /device:TPU:0, one launch (start us, length us, event | category | flops | bytes accessed | tf_op | source)
XLA Modules:
  0.0 250.1 jit_solution(9586252098549343776)
XLA Ops:
  0.7 1.3 broadcast_in_dim.33.query_b
  1.9 1.3 broadcast_in_dim.34.value_b
  3.2 1.3 broadcast_in_dim.35.out_b
  4.5 1.3 broadcast_in_dim.36.gain1
  5.7 1.3 broadcast_in_dim.37.bias1
  7.0 1.3 broadcast_in_dim.39.down_b
  8.3 1.3 broadcast_in_dim.40.gain2
  9.5 1.3 broadcast_in_dim.41.bias2
  10.8 211.6 %layer.1 = (f32[128,768]{1,0:T(8,128)}, f32[128,768]{1,0:T(8,128)}, f32[16,768]{1,0:T(8,128)}, bf16[3072,768]{1,0:T(8,128)(2,1)}, bf16[768,3072]{1,0:T(8,128)(2,1)}, /*index=5*/bf16[3072,768]{1,0:T(8,128)(2,1)}) custom-call(f32[128,768]{1,0:T(8,128)} %bitcast.15, f32[128,768]{1,0:T(8,128)} %bitcast.16, s32[1,6]{1,0:T(1,128)} %lengths.1, ...), custom_call_target="tpu_custom_call" | custom-call | tf_op jit(solution)/shard_map/layer/pallas_call | solution.py:1162
  222.3 0.8 slice.48
  223.2 1.6 slice_reduce_fusion
  224.8 0.6 reshape.37
  225.4 7.5 %convert_element_type.13 = f32[768,3072]{1,0:T(8,128)} convert(bf16[768,3072]{1,0:T(8,128)(2,1)} %get-tuple-element.27) | non-fusion elementwise | flops 2359296 | bytes 14155776 | tf_op jit(solution)/shard_map/convert_element_type | solution.py:1212
  232.9 0.0 copy-done
  232.9 4.5 %convert_element_type.14 = f32[3072,768]{1,0:T(8,128)} convert(bf16[3072,768]{1,0:T(8,128)(2,1)S(1)} %copy-done) | non-fusion elementwise | flops 2359296 | bytes 14155776 | tf_op jit(solution)/shard_map/convert_element_type | solution.py:1214
  237.4 0.0 slice-done
  237.4 0.0 slice-done.1
  237.4 3.1 %slice_convert_fusion = (f32[768,768]{1,0:T(8,128)}, f32[768,768]{0,1:T(8,128)}, f32[768,768]{0,1:T(8,128)}, f32[768,768]{0,1:T(8,128)S(1)}) fusion(bf16[3072,768]{1,0:T(8,128)(2,1)S(1)} %bitcast.12), kind=kLoop, calls=%fused_computation.3 | loop fusion | flops 2359296 | bytes 14155776 | tf_op jit(solution)/shard_map/convert_element_type | solution.py:1199
  240.5 3.0 %copy.37 = f32[768,768]{1,0:T(8,128)} copy(f32[768,768]{0,1:T(8,128)} %get-tuple-element.55) | data formatting | bytes 4718592
  243.6 3.0 %copy.36 = f32[768,768]{1,0:T(8,128)} copy(f32[768,768]{0,1:T(8,128)} %get-tuple-element.56) | data formatting | bytes 4718592
  246.6 1.9 copy.35
  248.6 0.0 copy-done.2
  248.6 0.7 copy.40
  249.3 0.7 copy.41
  (7 shorter events, 0.0 us)
Async XLA Ops:
  225.4 7.5 %copy-start = (bf16[3072,768]{1,0:T(8,128)(2,1)S(1)}, bf16[3072,768]{1,0:T(8,128)(2,1)}, u32[]{:S(2)}) copy-start(bf16[3072,768]{1,0:T(8,128)(2,1)} %get-tuple-element.28) | copy-start | bytes 14155780
  225.4 12.0 %slice-start = ((s8[4718592]{0:T(1024)(128)(4,1)}), s8[4194304]{0:T(1024)(128)(4,1)S(1)}, s32[]{:S(2)}) async-start(s8[4718592]{0:T(1024)(128)(4,1)} %bitcast.11), calls=%async_computation | async-start | bytes 8388608
  232.9 4.5 %slice-start.1 = ((s8[4718592]{0:T(1024)(128)(4,1)}), s8[524288]{0:T(1024)(128)(4,1)S(1)}, s32[]{:S(2)}) async-start(s8[4718592]{0:T(1024)(128)(4,1)} %bitcast.11), calls=%async_computation.1 | async-start | bytes 1048576
  246.6 1.9 copy-start.2
  246.6 2.7 %copy-start.1 = (f32[128,768]{1,0:T(8,128)S(1)}, f32[128,768]{1,0:T(8,128)}, u32[]{:S(2)}) copy-start(f32[128,768]{1,0:T(8,128)} %get-tuple-element.24) | copy-start | bytes 1179652

commit v2 on v0

--- a/solution.py
+++ b/solution.py
@@ -1,9 +1,12 @@
+import contextlib
 from functools import partial
 import math
 
 import jax
 import jax.numpy as jnp
 from jax import lax
+from jax.experimental import pallas as pl
+from jax.experimental.pallas import tpu as pltpu
 from jax.sharding import PartitionSpec as P
 
 H = 12
@@ -370,6 +373,1201 @@
     )
 
 
+MESH = pl.DeviceIdType.MESH
+LANES = 128
+F32, BF16 = jnp.float32, jnp.bfloat16
+VMEM_GRANT = 49 << 20
+DOWN, UP, ATTN = 0, 1, 2
+
+PIECES = (
+    (DOWN, "zyx", 0, 3),
+    (DOWN, "zxy", 3, 3),
+    (UP, "zyx", 0, 3),
+    (UP, "zxy", 3, 3),
+    (ATTN, "zyx", 0, 2),
+    (ATTN, "zxy", 2, 2),
+    (ATTN, "yxz", 4, 2),
+)
+
+
+def dot(a, b):
+    return jnp.dot(a, b, preferred_element_type=F32)
+
+
+def dot_nt(a, b):
+    return lax.dot_general(a, b, (((1,), (1,)), ((), ())), preferred_element_type=F32)
+
+
+def dot_tn(a, b):
+    return lax.dot_general(a, b, (((0,), (0,)), ((), ())), preferred_element_type=F32)
+
+
+def rows_norm(value):
+    centre = jnp.mean(value, axis=-1, keepdims=True)
+    centered = value - centre
+    inverse = lax.rsqrt(jnp.mean(centered * centered, axis=-1, keepdims=True) + NORM_EPSILON)
+    return centered * inverse, inverse
+
+
+def rows_norm_back(scaled, unit, inverse):
+    first = jnp.mean(scaled, axis=-1, keepdims=True)
+    second = jnp.mean(scaled * unit, axis=-1, keepdims=True)
+    return inverse * (scaled - first - unit * second)
+
+
+def layer_kernel(
+    T,
+    D,
+    S,
+    entries,
+    frames,
+    cotangent,
+    lengths,
+    query_w,
+    key_w,
+    value_w,
+    out_w,
+    up_w,
+    down_w,
+    query_b,
+    value_b,
+    out_b,
+    gain1,
+    bias1,
+    up_b,
+    down_b,
+    gain2,
+    bias2,
+    encoded,
+    frames_grad,
+    vectors,
+    sum_down,
+    sum_up,
+    sum_attn,
+    bias_rows,
+    up_rows,
+    fall,
+    wqkv,
+    wo,
+    wup,
+    wdn,
+    qall,
+    kv,
+    mask,
+    probs,
+    stat,
+    lsed,
+    att32,
+    att16,
+    attf,
+    hq,
+    fq,
+    ar,
+    br,
+    asend,
+    bsend,
+    dgelu,
+    hid32,
+    unit1,
+    rstd1,
+    gmid,
+    gfirst,
+    gbr,
+    doall,
+    dkv32,
+    dall,
+    part_down,
+    part_up,
+    part_attn,
+    got_down,
+    got_up,
+    got_attn,
+    gm,
+    dr,
+    xs,
+    xr,
+    dxs,
+    dxr,
+    dxo,
+    vsend,
+    vrecv,
+    vz,
+    wsem,
+    hes,
+    her,
+    frs,
+    fss,
+    abr,
+    abs_,
+    msr,
+    mss,
+    dor,
+    dos,
+    zsr,
+    zss,
+    agr,
+    ags,
+    agdr,
+    vzr,
+    vzs,
+):
+    HW, T2, FO = D // 2, 2 * T, wup.shape[1] // 8
+    blocks = HW // LANES
+    EIGHTH, SIXTEENTH = D // 8, D // 16
+    out_b, gain1, bias1, down_b, gain2, bias2 = (
+        ref[...].reshape(1, D) for ref in (out_b, gain1, bias1, down_b, gain2, bias2)
+    )
+    row, seq = lax.axis_index("row"), lax.axis_index("seq")
+    x, c = lax.div(row, 2), lax.rem(row, 2)
+    z, y = lax.div(seq, 2), lax.rem(seq, 2)
+    not_first, not_last = z > 0, z < 3
+
+    def device(x_, c_, y_, z_=z):
+        return (2 * x_ + c_, 2 * z_ + y_)
+
+    def octant(x_, c_, y_):
+        return 4 * y_ + 2 * x_ + c_
+
+    sib, xn, yn = device(x, 1 - c, y), device(1 - x, c, y), device(x, c, 1 - y)
+    zp, zm = device(x, c, y, jnp.minimum(z + 1, 3)), device(x, c, y, jnp.maximum(z - 1, 0))
+
+    def many(value, of):
+        return pl.multiple_of(value, of)
+
+    def at(start, size, of=None):
+        return pl.ds(many(start, size if of is None else of), size)
+
+    waits = []
+    scope = contextlib.ExitStack()
+
+    def phase(name):
+        scope.close()
+        if name:
+            scope.enter_context(jax.named_scope(name))
+
+    def send(src, dst, ssem, rsem, to):
+        return pltpu.make_async_remote_copy(
+            src_ref=src, dst_ref=dst, send_sem=ssem, recv_sem=rsem, device_id=to, device_id_type=MESH
+        )
+
+    def start(src, dst, ssem, rsem, to):
+        send(src, dst, ssem, rsem, to).start()
+
+    def arrived(ref, rsem):
+        send(ref, ref, mss.at[0], rsem, sib).wait_recv()
+
+    def sent(ref, ssem):
+        waits.append(send(ref, ref, ssem, msr.at[0], sib).wait_send)
+
+    def sent_along_z(ref_of, ssem, rest=0, lines=1):
+        for blocks_sent, when in ((1, (z == 0) | (z == 3)), (5, (z > 0) & (z < 3))):
+            ref = ref_of(rest + lines * blocks_sent)
+            copy = send(ref, ref, ssem, msr.at[0], sib)
+            waits.append(partial(pl.when(when), copy.wait_send))
+
+    send_names, names = {}, {}
+
+    def group(name):
+        return mss.at[send_names.setdefault(name, len(send_names))]
+
+    def one(name, family=None):
+        return group(family or name), got_of(name)
+
+    def got_of(name):
+        return msr.at[names.setdefault(name, len(names))]
+
+    phase("enter")
+    heads_here = at(HW * y, HW)
+    loads = [
+        pltpu.make_async_copy(query_w.at[:, heads_here], wqkv.at[:, pl.ds(0, HW)], wsem.at[0]),
+        pltpu.make_async_copy(key_w.at[:, heads_here], wqkv.at[:, pl.ds(HW, HW)], wsem.at[1]),
+        pltpu.make_async_copy(value_w.at[:, heads_here], wqkv.at[:, pl.ds(2 * HW, HW)], wsem.at[2]),
+        pltpu.make_async_copy(out_w, wo, wsem.at[3]),
+        pltpu.make_async_copy(up_w, wup, wsem.at[4]),
+        pltpu.make_async_copy(down_w, wdn, wsem.at[5]),
+    ]
+    barrier = pltpu.get_barrier_semaphore()
+    peers = [device(x_, c_, y_) for x_ in (x, 1 - x) for c_ in (c, 1 - c) for y_ in (y, 1 - y)][1:]
+    peers += [device(x, c, y, lax.rem(z + k, 4)) for k in (1, 2, 3)]
+    for peer in peers:
+        pl.semaphore_signal(barrier, inc=1, device_id=peer, device_id_type=MESH)
+    for load in loads:
+        load.start()
+    fall[at(T * seq, T), :] = frames[...].astype(BF16)
+    vectors[...] = jnp.zeros_like(vectors)
+    bias_rows[0:1, :] = query_b[...].reshape(1, D)
+    bias_rows[1:2, :] = value_b[...].reshape(1, D)
+    for quarter in range(4):
+        up_rows[quarter] = jnp.broadcast_to(up_b[pl.ds(D * quarter, D)].reshape(1, D), (8, D))
+    pl.semaphore_wait(barrier, len(peers))
+
+    phase("frames_gather")
+
+    def slab(z_, y_):
+        return fall.at[at(T * (2 * z_ + y_), T), :]
+
+    def push(z_, direction):
+        to = (zp, zm, yn)[direction]
+        return send(slab(z_, y), slab(z_, y), fss.at[direction // 2], frs.at[2 * z_ + y], to)
+
+    pl.when(not_last)(lambda: push(z, 0).start())
+    pl.when(not_first)(lambda: push(z, 1).start())
+    push(z, 2).start()
+    query_bias, value_bias = bias_rows[0:1, heads_here], bias_rows[1:2, heads_here]
+    for load in loads[:3]:
+        load.wait()
+
+    def project_slab(z_, y_):
+        rows = at(T * (2 * z_ + y_), T)
+        flat = dot(fall[rows, :], wqkv[...])
+        query = (flat[:, :HW] + query_bias).astype(BF16).astype(F32) * HD ** (-0.5)
+        qall[rows, :] = query.astype(BF16)
+        kv[rows, pl.ds(0, HW)] = flat[:, HW : 2 * HW].astype(BF16)
+        kv[rows, pl.ds(HW, HW)] = (flat[:, 2 * HW :] + value_bias).astype(BF16)
+
+    project_slab(z, y)
+    key_at = lax.broadcasted_iota(jnp.int32, (1, S), 1)
+    query_at = lax.broadcasted_iota(jnp.int32, (T2, 1), 0) + T2 * z
+    key_number, query_number = jnp.zeros((1, S), jnp.int32), jnp.zeros((T2, 1), jnp.int32)
+    clip_end = jnp.int32(0)
+    for entry in range(entries):
+        clip_end = clip_end + lengths[0, entry]
+        key_number = key_number + jnp.where(clip_end <= key_at, 1, 0)
+        query_number = query_number + jnp.where(clip_end <= query_at, 1, 0)
+    mask[...] = jnp.where(query_number == key_number, 0.0, MASK_SCORE)
+
+    @pl.loop(0, 4)
+    def _(k):
+        left, right = z - k - 1, z + k + 1
+
+        @pl.when(left >= 0)
+        def _():
+            arrived(slab(left, y), frs.at[2 * left + y])
+            pl.when(not_last)(lambda: push(left, 0).start())
+            push(left, 2).start()
+
+        @pl.when(right <= 3)
+        def _():
+            arrived(slab(right, y), frs.at[2 * right + y])
+            pl.when(not_first)(lambda: push(right, 1).start())
+            push(right, 2).start()
+
+        pl.when(left >= 0)(lambda: project_slab(left, y))
+        pl.when(right <= 3)(lambda: project_slab(right, y))
+
+        @pl.when(z - k >= 0)
+        def _():
+            arrived(slab(z - k, 1 - y), frs.at[2 * (z - k) + 1 - y])
+            project_slab(z - k, 1 - y)
+
+        @pl.when((k > 0) & (z + k <= 3))
+        def _():
+            arrived(slab(z + k, 1 - y), frs.at[2 * (z + k) + 1 - y])
+            project_slab(z + k, 1 - y)
+
+    sent(fall.at[pl.ds(0, 4 * T), :], fss.at[1])
+    sent_along_z(lambda count: fall.at[pl.ds(0, T * count), :], fss.at[0])
+
+    phase("attention")
+    pair_rows = at(T2 * z, T2)
+    lane = lax.broadcasted_iota(jnp.int32, (T2, LANES), 1)
+    low_half = lane < HD
+
+    def half(value, which):
+        return jnp.where(low_half == (which == 0), value, 0.0)
+
+    stat[...] = jnp.zeros_like(stat)
+    mine, other = at(T * y, T), at(T * (1 - y), T)
+
+    def heads_push(b):
+        part, there = at(LANES * b, LANES), at(HW * y + LANES * b, LANES, LANES)
+        return send(att16.at[other, part], attf.at[:, there], hes.at[0], her.at[b], yn)
+
+    @pl.loop(0, blocks)
+    def _(b):
+        lanes, value_lanes = at(LANES * b, LANES), at(HW + LANES * b, LANES, LANES)
+        queries = qall[pair_rows, lanes].astype(F32)
+        outs = []
+        for which in range(2):
+            scores = dot_nt(half(queries, which).astype(BF16), kv[:, lanes]) + mask[...]
+            peak = jnp.max(scores, axis=-1, keepdims=True)
+            powers = jnp.exp(scores - peak)
+            total = jnp.sum(powers, axis=-1, keepdims=True)
+            low = (powers * (1.0 / total)).astype(BF16)
+            probs[2 * b + which] = low
+            outs.append(dot(low, kv[:, value_lanes]))
+            stat[0] = jnp.where(lane == 2 * b + which, peak + jnp.log(total), stat[0])
+        out = jnp.where(low_half, outs[0], outs[1])
+        att32[:, lanes] = out
+        att16[:, lanes] = out.astype(BF16)
+        heads_push(b).start()
+
+    phase("heads_exchange")
+    attf[:, heads_here] = att16[mine, :]
+    lsed[z, 0:8, :] = stat[0].T[0:8, :]
+    loads[3].wait()
+    for b in range(blocks):
+        arrived(attf.at[:, at(HW * (1 - y) + LANES * b, LANES, LANES)], her.at[b])
+    sent(att16.at[pl.ds(0, T), :], hes.at[0])
+    phase("out_norm1")
+    branch = dot(attf[...], wo[...]) + out_b
+    unit, inverse = rows_norm(frames[...] + branch)
+    hidden = unit * gain1 + bias1
+    unit1[...] = unit
+    rstd1[...] = jnp.broadcast_to(inverse, (T, LANES))
+    hid32[...] = hidden
+    here = at(T * octant(x, c, y), T)
+
+    def rows_of(buffer, x_, c_, y_):
+        return buffer.at[at(T * octant(x_, c_, y_), T), :]
+
+    def halves_of(buffer, x_, c_, y_):
+        first = T * octant(x_, c_, y_)
+        return buffer.at[at(first, T // 2), :], buffer.at[at(first + T // 2, T // 2), :]
+
+    def share(buffer, name, to, tag):
+        own = rows_of(buffer, x, c, y)
+        start(own, own, *one(name + tag, name), to)
+
+    def from_x(buffer, name):
+        part, top = rows_of(buffer, 1 - x, c, y), halves_of(buffer, 1 - x, c, y)[0]
+        arrived(part, got_of(name + "_x"))
+        start(top, top, *one(name + "_top", name), yn)
+        start(part, part, *one(name + "_dx", name), sib)
+
+    def from_y(buffer, name):
+        part, bottom = rows_of(buffer, x, c, 1 - y), halves_of(buffer, x, c, 1 - y)[1]
+        arrived(part, got_of(name + "_y"))
+        start(bottom, bottom, *one(name + "_bottom", name), xn)
+        start(part, part, *one(name + "_dy", name), sib)
+
+    def from_diagonal(buffer, name):
+        part = rows_of(buffer, 1 - x, c, 1 - y)
+        top, bottom = halves_of(buffer, 1 - x, c, 1 - y)
+        arrived(top, got_of(name + "_top"))
+        arrived(bottom, got_of(name + "_bottom"))
+        start(part, part, *one(name + "_dd", name), sib)
+
+    def from_sibling(buffer, name):
+        arrived(rows_of(buffer, x, 1 - c, y), got_of(name + "_d"))
+        arrived(rows_of(buffer, 1 - x, 1 - c, y), got_of(name + "_dx"))
+        arrived(rows_of(buffer, x, 1 - c, 1 - y), got_of(name + "_dy"))
+        arrived(rows_of(buffer, 1 - x, 1 - c, 1 - y), got_of(name + "_dd"))
+
+    def spread(sent, got, index, x_, c_, y_):
+        to = octant(x_, c_, y_)
+        copy = send(
+            sent.at[to],
+            got.at[here, :],
+            abs_.at[index],
+            abr.at[index, octant(x, c, y)],
+            device(x_, c_, y_),
+        )
+        copy.start()
+
+    def spread_chip(sent, got, index, x_, y_):
+        for c_ in (c, 1 - c):
+            spread(sent, got, index, x_, c_, y_)
+
+    def spread_diagonal(sent, got, index):
+        spread_chip(sent, got, index, 1 - x, 1 - y)
+
+    def spread_y(sent, got, index):
+        spread_chip(sent, got, index, x, 1 - y)
+
+    def spread_arrived(got, index):
+        for x_, c_, y_ in [(x_, c_, y_) for x_ in (x, 1 - x) for c_ in (c, 1 - c) for y_ in (y, 1 - y)][1:]:
+            arrived(rows_of(got, x_, c_, y_), abr.at[index, octant(x_, c_, y_)])
+
+    chips = ((1 - x, y), (x, 1 - y), (1 - x, 1 - y), (x, y))
+
+    sent(hq.at[pl.ds(0, 7 * T), :], group("hid"))
+    sent(fq.at[pl.ds(0, 7 * T), :], group("ffn"))
+    for index, got in enumerate((ar, br)):
+        sent(got.at[pl.ds(0, 7 * T), :], abs_.at[index])
+    hq[here, :] = hidden.astype(BF16)
+    share(hq, "hid", xn, "_x")
+    share(hq, "hid", yn, "_y")
+    share(hq, "hid", sib, "_d")
+
+    phase("up_gelu")
+    loads[4].wait()
+    scale = 2.0 ** -0.5
+    for order, (x_, y_) in enumerate(chips):
+        chip = 2 * y_ + x_
+        before = dot(hq[here, :], wup[:, at(D * chip, D)]) + up_rows[chip][0:1, :]
+        rise = 0.5 * (1.0 + lax.erf(before * scale))
+        dgelu[chip] = rise + before * jnp.exp(-0.5 * before * before) * (2.0 * math.pi) ** -0.5
+        active = (before * rise).astype(BF16)
+        asend[2 * chip] = active[:, :FO]
+        asend[2 * chip + 1] = active[:, FO:]
+        if order < 2:
+            spread_chip(asend, ar, 0, x_, y_)
+    spread(asend, ar, 0, x, 1 - c, y)
+    ar[here, :] = asend[octant(x, c, y)]
+    phase("down_norm2")
+    loads[5].wait()
+    fed = hid32[...] + down_b
+    for eighth in range(8):
+        fed = fed + dot(asend[eighth], wdn[pl.ds(FO * eighth, FO), :])
+    unit2, inverse2 = rows_norm(fed)
+    encoded[...] = unit2 * gain2 + bias2
+    cot = cotangent[...]
+    grad_mid = rows_norm_back(cot * gain2, unit2, inverse2)
+    vectors[10:11, :] = jnp.sum(cot * unit2, axis=0, keepdims=True)
+    vectors[11:12, :] = jnp.sum(cot, axis=0, keepdims=True)
+    gmid[...] = grad_mid
+    fq[here, :] = grad_mid.astype(BF16)
+    share(fq, "ffn", xn, "_x")
+    share(fq, "ffn", sib, "_d")
+    vectors[9:10, :] = jnp.sum(fq[here, :].astype(F32), axis=0, keepdims=True)
+    phase("ffn_back")
+    for order, (x_, y_) in enumerate(chips):
+        chip = 2 * y_ + x_
+        quarter = at(D * chip, D)
+        low = (dot_nt(fq[here, :], wdn[quarter, :]) * dgelu[chip]).astype(BF16)
+        bsend[2 * chip] = low[:, :FO]
+        bsend[2 * chip + 1] = low[:, FO:]
+        if order == 0:
+            spread_chip(bsend, br, 1, x_, y_)
+        vectors[pl.ds(5 + chip, 1), :] = jnp.sum(low.astype(F32), axis=0, keepdims=True)
+        gmid[...] += dot_nt(low, wup[:, quarter])
+    spread(bsend, br, 1, x, 1 - c, y)
+    br[here, :] = bsend[octant(x, c, y)]
+    phase("norm1_back")
+    grad_hidden = gmid[...]
+    unit = unit1[...]
+    grad_first = rows_norm_back(grad_hidden * gain1, unit, rstd1[:, 0:1])
+    vectors[3:4, :] = jnp.sum(grad_hidden * unit, axis=0, keepdims=True)
+    vectors[4:5, :] = jnp.sum(grad_hidden, axis=0, keepdims=True)
+    gfirst[...] = grad_first
+    gbr[mine, :] = grad_first.astype(BF16)
+    start(gbr.at[mine, :], gbr.at[mine, :], *one("gbr"), yn)
+    sent(gbr.at[mine, :], group("gbr"))
+    vectors[2:3, :] = jnp.sum(gbr[mine, :].astype(F32), axis=0, keepdims=True)
+
+    parts, gots = (part_down, part_up, part_attn), (got_down, got_up, got_attn)
+    slab_rows = (FO // 4, D // 4, EIGHTH)
+
+    def part_slab(t, j):
+        return parts[t].at[at(slab_rows[t] * j, slab_rows[t]), :]
+
+    outer = (z == 0) | (z == 3)
+    near = jnp.where(z < 2, 1 - z, 5 - z)
+    inner_there, outer_there = jnp.where(z < 2, 2, 1), jnp.where(z < 2, 3, 0)
+
+    def part_send(t, src, j, to, slot):
+        start(src, gots[t].at[slot], zss.at[t], zsr.at[t, slot], device(x, c, y, to))
+
+    def sum_send(t):
+        sent(parts[t].at[pl.ds(0, 3 * slab_rows[t]), :], zss.at[t])
+
+        @pl.when(outer)
+        def _():
+            for j in (outer_there, inner_there, near):
+                part_send(t, part_slab(t, j), j, near, j)
+
+        @pl.when(jnp.logical_not(outer))
+        def _():
+            part_send(t, part_slab(t, near), near, near, z)
+
+    def sum_pass(t):
+        @pl.when(jnp.logical_not(outer))
+        def _():
+            for j, slot in ((outer_there, z), (inner_there, outer_there)):
+                got = gots[t].at[j]
+                arrived(got, zsr.at[t, j])
+                got[...] = (got[...].astype(F32) + part_slab(t, j)[...].astype(F32)).astype(BF16)
+                part_send(t, got, j, j, slot)
+
+    def own_tile(t):
+        if t == DOWN:
+            return sum_down.at[at(FO * octant(x, c, y) + EIGHTH // 2 * 2 * z, EIGHTH, EIGHTH), :]
+        if t == UP:
+            return sum_up.at[at(D // 4 * z, D // 4), at(FO * octant(x, c, y), FO)]
+        return sum_attn.at[at(D * row + HW * y + EIGHTH * z, EIGHTH), :]
+
+    def sum_end(t):
+        total = part_slab(t, z)[...].astype(F32)
+        for slot in (jnp.where(outer, near, z), jnp.where(outer, inner_there, near)):
+            arrived(gots[t].at[slot], zsr.at[t, slot])
+            total = total + gots[t][slot].astype(F32)
+        own_tile(t)[...] = total.astype(BF16)
+
+    unit_rows = (SIXTEENTH // 3, EIGHTH // 3, SIXTEENTH // 3)
+
+    def tile(u, x_, y_, z_):
+        t, _, first, count = PIECES[u]
+        rows = unit_rows[t]
+        if t == DOWN:
+            start_row = FO * octant(x_, c, y_) + EIGHTH * z_ + rows * first
+            return sum_down.at[at(start_row, rows * count, rows), :]
+        if t == UP:
+            start_row = D // 4 * z_ + rows * first
+            return sum_up.at[at(start_row, rows * count, rows), at(FO * octant(x_, c, y_), FO)]
+        start_row = D * (2 * x_ + c) + HW * y_ + EIGHTH * z_ + rows * first
+        return sum_attn.at[at(start_row, rows * count, rows), :]
+
+    def gather_send(u, place, z_, ssem, rsem, to):
+        part = tile(u, *place, z_)
+        return send(part, part, ssem, rsem, to)
+
+    def to_sibling(u, place, z_):
+        gather_send(u, place, z_, ags.at[u], agdr.at[u], sib).start()
+
+    places = ((x, y), (1 - x, y), (x, 1 - y), (1 - x, 1 - y))
+
+    def order_of(u):
+        over_y, over_x = (2, yn), (1, xn)
+        return (over_y, over_x) if PIECES[u][1] in ("zyx", "yxz") else (over_x, over_y)
+
+    def z_last(u):
+        return PIECES[u][1][2] == "z"
+
+    def along_z(u, p, z_, direction):
+        to = (zp, zm)[direction]
+        return gather_send(u, places[p], z_, ags.at[u], agr.at[u, 4 * p + z_], to)
+
+    def z_out(u, p):
+        pl.when(not_last)(lambda: along_z(u, p, z, 0).start())
+        pl.when(not_first)(lambda: along_z(u, p, z, 1).start())
+
+    def second_sem(u, z_):
+        return agr.at[u, 16] if z_last(u) else agr.at[u, 4 + z_]
+
+    def third_sem(u, slot):
+        return agr.at[u, (17 if z_last(u) else 8) + slot]
+
+    def to_second(u, place, z_):
+        gather_send(u, place, z_, ags.at[u], second_sem(u, z_), order_of(u)[0][1]).start()
+
+    def to_third(u, place, slot):
+        z_ = z if z_last(u) else lax.rem(slot, 4)
+        gather_send(u, place, z_, ags.at[u], third_sem(u, slot), order_of(u)[1][1]).start()
+
+    def gather_own(t):
+        for u in pieces_of(t):
+            z_out(u, 0)
+        for u in pieces_of(t):
+            to_second(u, places[0], z)
+            to_third(u, places[0], 0 if z_last(u) else z)
+            to_sibling(u, places[0], z)
+
+    def pieces_of(t, last=None):
+        return [u for u in range(len(PIECES)) if PIECES[u][0] == t and last in (None, z_last(u))]
+
+    def sides(k, take):
+        pl.when(z - k >= 0)(lambda: take(z - k, not_last, 0))
+        if k > 0:
+            pl.when(z + k <= 3)(lambda: take(z + k, not_first, 1))
+
+    def gather_z(t, k):
+        for u in pieces_of(t, False):
+
+            def take(z_, more, direction):
+                arrived(tile(u, *places[0], z_), agr.at[u, z_])
+                pl.when(more)(lambda: along_z(u, 0, z_, direction).start())
+                to_second(u, places[0], z_)
+                to_third(u, places[0], z_)
+                to_sibling(u, places[0], z_)
+
+            sides(k, take)
+
+    def gather_second(t, k):
+        for u in pieces_of(t, False):
+
+            def take(z_, more, direction):
+                place = places[order_of(u)[0][0]]
+                arrived(tile(u, *place, z_), second_sem(u, z_))
+                to_third(u, place, 4 + z_)
+                to_sibling(u, place, z_)
+
+            sides(k, take)
+
+    def gather_third(t, k):
+        for u in pieces_of(t, False):
+
+            def take(z_, more, direction):
+                for offset, p in ((0, order_of(u)[1][0]), (4, 3)):
+                    arrived(tile(u, *places[p], z_), third_sem(u, offset + z_))
+                    to_sibling(u, places[p], z_)
+
+            sides(k, take)
+
+    def plane_first(t):
+        for u in pieces_of(t, True):
+            p = order_of(u)[0][0]
+            arrived(tile(u, *places[p], z), second_sem(u, z))
+            to_third(u, places[p], 1)
+            z_out(u, p)
+            to_sibling(u, places[p], z)
+
+    def plane_second(t):
+        for u in pieces_of(t, True):
+            for slot, p in ((0, order_of(u)[1][0]), (1, 3)):
+                arrived(tile(u, *places[p], z), third_sem(u, slot))
+                z_out(u, p)
+                to_sibling(u, places[p], z)
+
+    def plane_z(t, k):
+        for u in pieces_of(t, True):
+            for p in (0, order_of(u)[0][0], order_of(u)[1][0], 3):
+
+                def take(z_, more, direction):
+                    arrived(tile(u, *places[p], z_), agr.at[u, 4 * p + z_])
+                    pl.when(more)(lambda: along_z(u, p, z_, direction).start())
+                    to_sibling(u, places[p], z_)
+
+                sides(k, take)
+
+    def gather_end():
+        for u, (_, _, _, count) in enumerate(PIECES):
+
+            def as_many(blocks_sent):
+                return sum_down.at[pl.ds(0, unit_rows[DOWN] * count * blocks_sent), :]
+
+            arrived(as_many(16), agdr.at[u])
+            if z_last(u):
+                sent_along_z(as_many, ags.at[u], 19, 4)
+            else:
+                sent_along_z(as_many, ags.at[u], 28)
+
+    def out_back():
+        arrived(gbr.at[other, :], got_of("gbr"))
+        da = dot_nt(gbr[...], wo[heads_here, :]).astype(BF16)
+        doall[pair_rows, :] = da
+        product = da.astype(F32) * att32[...]
+        stat[1] = jnp.zeros((T2, LANES), F32)
+        for head in range(2 * blocks):
+            lanes = slice(LANES * (head // 2), LANES * (head // 2 + 1))
+            delta = jnp.sum(half(product[:, lanes], head % 2), axis=-1, keepdims=True)
+            stat[1] = jnp.where(lane == head, delta, stat[1])
+        lsed[z, 8:16, :] = stat[1].T[0:8, :]
+        pl.when(not_last)(lambda: grads_push(z, 0))
+        pl.when(not_first)(lambda: grads_push(z, 1))
+        gm[3] = dot_tn(att16[...], gbr[...]).astype(BF16)
+
+    def grads_rows(z_):
+        return doall.at[at(T2 * z_, T2), :], lsed.at[z_]
+
+    def grads_copies(z_, direction):
+        to = (zp, zm)[direction]
+        return [
+            send(ref, ref, dos.at[index], dor.at[index, z_], to)
+            for index, ref in enumerate(grads_rows(z_))
+        ]
+
+    def grads_push(z_, direction):
+        for copy in grads_copies(z_, direction):
+            copy.start()
+
+    sent_along_z(lambda count: fall.at[pl.ds(0, T * count), :], dos.at[0])
+    sent_along_z(lambda count: lsed.at[pl.ds(0, count)], dos.at[1])
+
+    def grads_arrive(k):
+        def take(z_, more, direction):
+            for index, ref in enumerate(grads_rows(z_)):
+                arrived(ref, dor.at[index, z_])
+            pl.when(more)(lambda: grads_push(z_, direction))
+
+        pl.when(z - k >= 0)(lambda: take(z - k, not_last, 0))
+        pl.when(z + k <= 3)(lambda: take(z + k, not_first, 1))
+
+    def queries_back():
+        @pl.loop(0, blocks)
+        def _(b):
+            lanes, value_lanes = at(LANES * b, LANES), at(HW + LANES * b, LANES, LANES)
+            heads = doall[pair_rows, lanes].astype(F32)
+            product = heads * att32[:, lanes]
+            pieces = []
+            for which in range(2):
+                delta = jnp.sum(half(product, which), axis=-1, keepdims=True)
+                grad_probs = dot_nt(half(heads, which).astype(BF16), kv[:, value_lanes])
+                grad_scores = probs[2 * b + which].astype(F32) * (grad_probs - delta)
+                pieces.append(dot(grad_scores.astype(BF16), kv[:, lanes]))
+            total = jnp.where(low_half, pieces[0], pieces[1]) * HD ** (-0.5)
+            dall[:, lanes] = total.astype(BF16)
+
+    def keys_back(z_):
+        rows = at(T2 * z_, T2)
+
+        @pl.loop(0, blocks)
+        def _(b):
+            lanes, value_lanes = at(LANES * b, LANES), at(HW + LANES * b, LANES, LANES)
+            keys, values = kv[pair_rows, lanes].astype(F32), kv[pair_rows, value_lanes].astype(F32)
+            queries, grads = qall[rows, lanes], doall[rows, lanes]
+            key_pieces, value_pieces = [], []
+            for which in range(2):
+                head = 2 * b + which
+                scores = dot_nt(half(keys, which).astype(BF16), queries) + mask[:, rows]
+                powers = jnp.exp(scores - lsed[z_, pl.ds(head, 1), :])
+                grad_probs = dot_nt(half(values, which).astype(BF16), grads)
+                grad_scores = powers * (grad_probs - lsed[z_, pl.ds(8 + head, 1), :])
+                key_pieces.append(dot(grad_scores.astype(BF16), queries))
+                value_pieces.append(dot(powers.astype(BF16), grads))
+            dkv32[:, lanes] += jnp.where(low_half, key_pieces[0], key_pieces[1])
+            dkv32[:, value_lanes] += jnp.where(low_half, value_pieces[0], value_pieces[1])
+
+    def keys_back_at(k):
+        pl.when(z - k >= 0)(lambda: keys_back(z - k))
+        if k > 0:
+            pl.when(z + k <= 3)(lambda: keys_back(z + k))
+
+    def attention_weights():
+        dall[:, pl.ds(HW, D)] = dkv32[...].astype(BF16)
+        grads = dot_tn(dall[...], fall[pair_rows, :])
+        for matrix in range(3):
+            gm[matrix] = grads[HW * matrix : HW * (matrix + 1), :].astype(BF16)
+        sent(dr, group("d"))
+        for slot in range(2):
+            start(gm.at[1 - c + 2 * slot], dr.at[slot], *one(("d", slot), "d"), sib)
+
+    def input_grad():
+        into = dot_nt(dall[...], wqkv[...])
+        dxo[...] = into
+        dxs[...] = dxo[other, :].astype(BF16)
+        start(dxs, dxr, *one("dx"), yn)
+        sent(dxs, group("dx"))
+        sums = jnp.sum(dall[...].astype(F32), axis=0, keepdims=True)
+        vectors[0:1, heads_here] = sums[:, :HW]
+        vectors[1:2, heads_here] = sums[:, 2 * HW :]
+
+    def input_grad_end():
+        arrived(dxr, got_of("dx"))
+        frames_grad[...] = gfirst[...] + dxo[mine, :] + dxr[...].astype(F32)
+
+    def attention_x():
+        for slot in range(2):
+            arrived(dr.at[slot], got_of(("d", slot)))
+        xs[...] = (gm[c + 2 * (1 - x)].astype(F32) + dr[1 - x].astype(F32)).astype(BF16)
+        start(xs, xr, *one("xs"), xn)
+        sent(xs, group("xs"))
+
+    def attention_z():
+        arrived(xr, got_of("xs"))
+        part_attn[...] = (gm[c + 2 * x].astype(F32) + dr[x].astype(F32) + xr[...].astype(F32)).astype(BF16)
+        sum_send(ATTN)
+
+    def down_grad():
+        part_down[...] = dot_tn(ar[...], fq[...]).astype(BF16)
+        sum_send(DOWN)
+
+    def up_grad():
+        part_up[...] = dot_tn(hq[...], br[...]).astype(BF16)
+        sum_send(UP)
+
+    def vector_step(i, to):
+        vsend[i] = vectors[...]
+        start(vsend.at[i], vrecv.at[i], *one(("v", i)), to)
+        sent(vsend.at[i], group(("v", i)))
+
+    def vector_add(i):
+        arrived(vrecv.at[i], got_of(("v", i)))
+        vectors[...] += vrecv[i]
+
+    def vector_z():
+        vsend[3] = vectors[...]
+        vz[z] = vectors[...]
+        sent(vz.at[pl.ds(0, 3)], vzs.at[0])
+        for k in (1, 2, 3):
+            j = lax.rem(z + k, 4)
+            start(vsend.at[3], vz.at[z], vzs.at[0], vzr.at[z], device(x, c, y, j))
+
+    def vector_end():
+        for k in (1, 2, 3):
+            j = lax.rem(z + k, 4)
+            arrived(vz.at[j], vzr.at[j])
+        vectors[...] = (vz[0] + vz[1]) + (vz[2] + vz[3])
+
+    dkv32[...] = jnp.zeros_like(dkv32)
+    phase("hid_forward")
+    from_x(hq, "hid")
+    from_y(hq, "hid")
+    phase("out_back")
+    out_back()
+    share(fq, "ffn", yn, "_y")
+    spread_diagonal(asend, ar, 0)
+    phase("queries_back")
+    queries_back()
+    phase("ffn_x")
+    from_x(fq, "ffn")
+    phase("keys_back0")
+    keys_back_at(0)
+    phase("ffn_y")
+    from_y(fq, "ffn")
+    spread_y(bsend, br, 1)
+    phase("grads1")
+    grads_arrive(1)
+    spread_diagonal(bsend, br, 1)
+    phase("keys_back1")
+    keys_back_at(1)
+    phase("hid_diag")
+    from_diagonal(hq, "hid")
+    phase("grads2")
+    grads_arrive(2)
+    phase("keys_back2")
+    keys_back_at(2)
+    phase("ffn_diag")
+    from_diagonal(fq, "ffn")
+    phase("grads3")
+    grads_arrive(3)
+    phase("keys_back3")
+    keys_back_at(3)
+    phase("attn_weights")
+    attention_weights()
+    phase("wait_down")
+    from_sibling(fq, "ffn")
+    spread_arrived(ar, 0)
+    phase("down_grad")
+    down_grad()
+    phase("attention_x")
+    attention_x()
+    phase("input_grad")
+    input_grad()
+    phase("wait_up")
+    from_sibling(hq, "hid")
+    spread_arrived(br, 1)
+    phase("up_grad")
+    up_grad()
+    phase("vec0")
+    vector_step(0, sib)
+    vector_add(0)
+    vector_step(1, xn)
+    phase("down_pass")
+    sum_pass(DOWN)
+    phase("up_pass")
+    sum_pass(UP)
+    phase("down_end")
+    sum_end(DOWN)
+    gather_own(DOWN)
+    vector_add(1)
+    vector_step(2, yn)
+    phase("attention_z")
+    attention_z()
+    phase("g_d1")
+    gather_z(DOWN, 1)
+    gather_second(DOWN, 0)
+    phase("up_end")
+    sum_end(UP)
+    gather_own(UP)
+    phase("attn_pass")
+    sum_pass(ATTN)
+    vector_add(2)
+    vector_z()
+    input_grad_end()
+    phase("g_d2")
+    gather_z(DOWN, 2)
+    gather_second(DOWN, 1)
+    gather_third(DOWN, 0)
+    phase("attn_end")
+    sum_end(ATTN)
+    gather_own(ATTN)
+    phase("g1")
+    gather_z(UP, 1)
+    gather_second(UP, 0)
+    vector_end()
+    phase("g2")
+    gather_z(DOWN, 3)
+    gather_second(DOWN, 2)
+    gather_third(DOWN, 1)
+    gather_z(UP, 2)
+    gather_second(UP, 1)
+    gather_third(UP, 0)
+    plane_first(ATTN)
+    gather_z(ATTN, 1)
+    gather_second(ATTN, 0)
+    plane_second(ATTN)
+    phase("g3")
+    gather_second(DOWN, 3)
+    gather_third(DOWN, 2)
+    gather_z(UP, 3)
+    gather_second(UP, 2)
+    gather_third(UP, 1)
+    gather_z(ATTN, 2)
+    gather_second(ATTN, 1)
+    gather_third(ATTN, 0)
+    plane_z(ATTN, 1)
+    phase("g4")
+    gather_third(DOWN, 3)
+    gather_second(UP, 3)
+    gather_third(UP, 2)
+    gather_z(ATTN, 3)
+    gather_second(ATTN, 2)
+    gather_third(ATTN, 1)
+    plane_z(ATTN, 2)
+    phase("g5")
+    gather_third(UP, 3)
+    gather_second(ATTN, 3)
+    gather_third(ATTN, 2)
+    plane_z(ATTN, 3)
+    gather_third(ATTN, 3)
+    phase("gather_end")
+    gather_end()
+    phase("sends_end")
+    assert (len(send_names), len(names)) == (mss.shape[0], msr.shape[0])
+    for wait in waits:
+        wait()
+    phase(None)
+
+
+def fused_layer(
+    frames,
+    clip_lengths,
+    query_weight,
+    query_bias,
+    key_weight,
+    value_weight,
+    value_bias,
+    out_weight,
+    out_bias,
+    norm1_gain,
+    norm1_bias,
+    up_weight,
+    up_bias,
+    down_weight,
+    down_bias,
+    norm2_gain,
+    norm2_bias,
+    cotangent,
+):
+    T, D = frames.shape[1], frames.shape[2]
+    F = up_weight.shape[1]
+    S = T * lax.axis_size("seq")
+    HW, T2, EIGHTH, FO = D // 2, 2 * T, D // 8, F // 8
+    blocks = HW // LANES
+    entries = clip_lengths.shape[1]
+    vmem, smem, hbm = (
+        pl.BlockSpec(memory_space=pltpu.VMEM),
+        pl.BlockSpec(memory_space=pltpu.SMEM),
+        pl.BlockSpec(memory_space=pl.ANY),
+    )
+    dma, n = pltpu.SemaphoreType.DMA, len(PIECES)
+    low, wide = (lambda *shape: pltpu.VMEM(shape, BF16)), (lambda *shape: pltpu.VMEM(shape, F32))
+    scratch = dict(
+        bias_rows=wide(8, D),
+        up_rows=wide(4, 8, D),
+        fall=low(S, D),
+        wqkv=low(D, 3 * HW),
+        wo=low(D, D),
+        wup=low(D, F),
+        wdn=low(F, D),
+        qall=low(S, HW),
+        kv=low(S, D),
+        mask=wide(T2, S),
+        probs=low(2 * blocks, T2, S),
+        stat=wide(2, T2, LANES),
+        lsed=wide(5, 16, T2),
+        att32=wide(T2, HW),
+        att16=low(T2, HW),
+        attf=low(T, D),
+        hq=low(8 * T, D),
+        fq=low(8 * T, D),
+        ar=low(8 * T, FO),
+        br=low(8 * T, FO),
+        asend=low(8, T, FO),
+        bsend=low(8, T, FO),
+        dgelu=wide(4, T, D),
+        hid32=wide(T, D),
+        unit1=wide(T, D),
+        rstd1=wide(T, LANES),
+        gmid=wide(T, D),
+        gfirst=wide(T, D),
+        gbr=low(T2, D),
+        doall=low(S, HW),
+        dkv32=wide(T2, D),
+        dall=low(T2, 3 * HW),
+        part_down=low(FO, D),
+        part_up=low(D, FO),
+        part_attn=low(HW, D),
+        got_down=low(4, FO // 4, D),
+        got_up=low(4, D // 4, FO),
+        got_attn=low(4, EIGHTH, D),
+        gm=low(4, HW, D),
+        dr=low(2, HW, D),
+        xs=low(HW, D),
+        xr=low(HW, D),
+        dxs=low(T, D),
+        dxr=low(T, D),
+        dxo=wide(T2, D),
+        vsend=wide(4, 16, D),
+        vrecv=wide(3, 16, D),
+        vz=wide(4, 16, D),
+        wsem=dma((6,)),
+        hes=dma((1,)),
+        her=dma((blocks,)),
+        frs=dma((8,)),
+        fss=dma((2,)),
+        abr=dma((2, 8)),
+        abs_=dma((2,)),
+        msr=dma((24,)),
+        mss=dma((9,)),
+        dor=dma((2, 4)),
+        dos=dma((2,)),
+        zsr=dma((3, 4)),
+        zss=dma((3,)),
+        agr=dma((n, 19)),
+        ags=dma((n,)),
+        agdr=dma((n,)),
+        vzr=dma((4,)),
+        vzs=dma((1,)),
+    )
+    results = pl.pallas_call(
+        partial(layer_kernel, T, D, S, entries),
+        out_shape=(
+            pltpu.VMEM((T, D), F32),
+            pltpu.VMEM((T, D), F32),
+            pltpu.VMEM((16, D), F32),
+            pltpu.VMEM((F, D), BF16),
+            pltpu.VMEM((D, F), BF16),
+            pltpu.VMEM((4 * D, D), BF16),
+        ),
+        in_specs=[vmem, vmem, smem] + [hbm] * 6 + [vmem] * 9,
+        out_specs=(vmem,) * 6,
+        scratch_shapes=list(scratch.values()),
+        compiler_params=pltpu.CompilerParams(
+            collective_id=0, has_side_effects=True, vmem_limit_bytes=VMEM_GRANT
+        ),
+        name="layer",
+    )(
+        frames[0],
+        cotangent[0],
+        clip_lengths,
+        query_weight,
+        key_weight,
+        value_weight,
+        out_weight,
+        up_weight,
+        down_weight,
+        query_bias,
+        value_bias,
+        out_bias,
+        norm1_gain,
+        norm1_bias,
+        up_bias,
+        down_bias,
+        norm2_gain,
+        norm2_bias,
+    )
+    return widen(*results)
+
+
+def widen_kernel(
+    last,
+    T,
+    D,
+    encoded,
+    frames_grad,
+    vectors,
+    down,
+    up,
+    attn,
+    encoded_out,
+    frames_grad_out,
+    query_out,
+    query_b,
+    key_out,
+    value_out,
+    value_b,
+    out_out,
+    out_b,
+    gain1,
+    bias1,
+    up_out,
+    up_b,
+    down_out,
+    down_b,
+    gain2,
+    bias2,
+    sems,
+):
+    step = pl.program_id(0)
+    copies = [
+        pltpu.make_async_copy(encoded, encoded_out, sems.at[0]),
+        pltpu.make_async_copy(frames_grad, frames_grad_out, sems.at[1]),
+    ]
+
+    @pl.when(step == 0)
+    def _():
+        for copy in copies:
+            copy.start()
+        for ref, index in (
+            (query_b, 0),
+            (value_b, 1),
+            (out_b, 2),
+            (gain1, 3),
+            (bias1, 4),
+            (down_b, 9),
+            (gain2, 10),
+            (bias2, 11),
+        ):
+            ref[...] = vectors[index : index + 1, :].reshape(D)
+        for quarter in range(4):
+            up_b[pl.ds(D * quarter, D)] = vectors[5 + quarter : 6 + quarter, :].reshape(D)
+
+    def rows(size, first=0):
+        return pl.ds(pl.multiple_of(first + size * step, size), size)
+
+    down_out[...] = down[rows(down_out.shape[0]), :].astype(F32)
+    up_out[...] = up[rows(up_out.shape[0]), :].astype(F32)
+    out_out[...] = attn[rows(LANES, 3 * D), :].astype(F32)
+    for m, target in enumerate((query_out, key_out, value_out)):
+        target[...] = attn[rows(LANES, m * D), :].astype(F32).T
+
+    @pl.when(step == last)
+    def _():
+        for copy in copies:
+            copy.wait()
+
+
+def widen(encoded, frames_grad, vectors, sum_down, sum_up, sum_attn):
+    T, D = encoded.shape
+    F = sum_up.shape[1]
+    steps = D // LANES
+    hbm, vmem = pl.BlockSpec(memory_space=pl.ANY), pl.BlockSpec(memory_space=pltpu.VMEM)
+    parts = (encoded, frames_grad, vectors, sum_down, sum_up, sum_attn)
+    parts = [pltpu.with_memory_space_constraint(part, pltpu.VMEM) for part in parts]
+
+    def down(width):
+        return pl.BlockSpec((width, D), lambda i: (i, 0))
+
+    up = pl.BlockSpec((D // steps, F), lambda i: (i, 0))
+    turned = pl.BlockSpec((D, LANES), lambda i: (0, i))
+    flat = pl.BlockSpec((D,), lambda i: (0,))
+    wide_flat = pl.BlockSpec((F,), lambda i: (0,))
+    square, vector = jax.ShapeDtypeStruct((D, D), F32), jax.ShapeDtypeStruct((D,), F32)
+    tokens = jax.ShapeDtypeStruct((T, D), F32)
+    outs = (
+        (tokens, hbm),
+        (tokens, hbm),
+        (square, turned),
+        (vector, flat),
+        (square, turned),
+        (square, turned),
+        (vector, flat),
+        (square, down(LANES)),
+        (vector, flat),
+        (vector, flat),
+        (vector, flat),
+        (jax.ShapeDtypeStruct((D, F), F32), up),
+        (jax.ShapeDtypeStruct((F,), F32), wide_flat),
+        (jax.ShapeDtypeStruct((F, D), F32), down(F // steps)),
+        (vector, flat),
+        (vector, flat),
+        (vector, flat),
+    )
+    results = pl.pallas_call(
+        partial(widen_kernel, steps - 1, T, D),
+        grid=(steps,),
+        out_shape=tuple(shape for shape, _ in outs),
+        in_specs=[vmem] * 6,
+        out_specs=tuple(spec for _, spec in outs),
+        scratch_shapes=[pltpu.SemaphoreType.DMA((2,))],
+        compiler_params=pltpu.CompilerParams(vmem_limit_bytes=VMEM_GRANT),
+        name="widen",
+    )(*parts)
+    return (results[0][None], results[1][None]) + tuple(results[2:])
+
+
 def solution(mesh):
     in_specs = (
         P("row", "seq", None),
@@ -410,6 +1608,8 @@
         P(),
         P(),
     )
+    shape = dict(mesh.shape)
+    fused = shape["row"] == 4 and shape["seq"] == 8
     return jax.shard_map(
-        per_device, mesh=mesh, in_specs=in_specs, out_specs=out_specs, check_vma=False
-    )
+        fused_layer if fused else per_device, mesh=mesh, in_specs=in_specs, out_specs=out_specs, check_vma=False
+    )

time: 1310 us -> 163 us (0.12)
  waiting for transfers between devices: 987 us -> 0 us
  Pallas kernels: 0 us -> 162 us
  blocking collectives: 103 us -> 0 us
  matrix products: 74.9 us -> 0 us
  other arithmetic: 66.8 us -> 0 us
  local copies, waits for them, and re-layouts: 46.1 us -> 0 us
  between operations: 16.6 us -> 0.83 us
  starting transfers between devices: 13.9 us -> 0 us
    reduce_scatter x3 -> x0, waiting for transfers between devices: 399 us -> none  [the longest x1 165 us: per_device(): lax.psum_scatter(up_weight_grad, 'seq', scatter_dimension=0, tiled=True)]
    all_gather x8 -> x0, waiting for transfers between devices: 270 us -> none  [the longest x1 77.9 us: per_device(): lax.all_gather(shares[9].astype(jnp.bfloat16), 'seq', axis=0, tiled=True)]
    unnamed x18 -> x0, waiting for transfers between devices: 165 us -> none
    pallas_call x0 -> x2, Pallas kernels: none -> 162 us  [the longest x1 152 us: fused_layer(): pl.pallas_call(partial(layer_kernel, T, D, S, entries), out_shape=(pltpu....]
    ppermute x30 -> x0, waiting for transfers between devices: 104 us -> none  [from_behind(): lax.ppermute(value, axis, [(i, (i + by) % count) for i in range(count)])]
    dot_general x62 -> x0, matrix products: 74.9 us -> none  [the longest x6 17.9 us: matrix_grad(): jnp.einsum('rsk,rsn->kn', inputs, upstream, preferred_element_type=jnp.fl...]
    unnamed x2 -> x0, blocking collectives: 71.3 us -> none
    psum x1 -> x0, waiting for transfers between devices: 49.8 us -> none  [per_device(): lax.psum(shares[0].astype(jnp.bfloat16), 'row').astype(jnp.float32)]
  transfers between devices with their start and end apart: 45 -> 0, of which waited for: 38 -> 0; matrix products, arithmetic and copies ran while one was open for 9% -> 0% of each run, Pallas kernels for 0% -> 0%
where the time goes in v2:
time: 163 us; the launch traced here: 162 us
  Pallas kernels  162 us (99%)
    pallas_call x1, Pallas kernels, fused_layer(): pl.pallas_call(partial(layer_kernel, T, D, S, entries), out_shape=(pltpu....  152 us
    pallas_call x1, Pallas kernels, widen(): pl.pallas_call(partial(widen_kernel, steps - 1, T, D), grid=(steps,), out...  9.84 us

profile of v2, /device:TPU:0, one launch (start us, length us, event | category | flops | bytes accessed | tf_op | source)
XLA Modules:
  0.0 162.4 jit_solution(12072452993489138806)
XLA Ops:
  0.7 151.8 %layer.1 = (f32[128,768]{1,0:T(8,128)S(1)}, f32[128,768]{1,0:T(8,128)S(1)}, f32[16,768]{1,0:T(8,128)S(1)}, bf16[3072,768]{1,0:T(8,128)(2,1)S(1)}, bf16[768,3072]...) custom-call(f32[128,768]{1,0:T(8,128)} %bitcast.4, f32[128,768]{1,0:T(8,128)} %bitcast.5, s32[1,6]{1,0:T(1,128)} %lengths.1, ...), custom_call_target="tpu_custom_call" | custom-call | tf_op jit(solution)/shard_map/layer/pallas_call | solution.py:1414
  152.4 9.8 %widen.1 = (f32[128,768]{1,0:T(8,128)}, f32[128,768]{1,0:T(8,128)}, f32[768,768]{1,0:T(8,128)}, f32[768]{0:T(1024)}, f32[768,768]{1,0:T(8,128)}, /*index=5*/f32[...) custom-call(f32[128,768]{1,0:T(8,128)S(1)} %get-tuple-element.40.enc, ...), custom_call_target="tpu_custom_call" | custom-call | tf_op jit(solution)/shard_map/widen/pallas_call | solution.py:1558

commit v3 on v2

--- a/solution.py
+++ b/solution.py
@@ -377,16 +377,19 @@
 LANES = 128
 F32, BF16 = jnp.float32, jnp.bfloat16
 VMEM_GRANT = 49 << 20
-DOWN, UP, ATTN = 0, 1, 2
+DOWN, UP, QUERY_OUT, KEY_VALUE = range(4)
 
 PIECES = (
-    (DOWN, "zyx", 0, 3),
-    (DOWN, "zxy", 3, 3),
+    (DOWN, "zyx", 0, 2),
+    (DOWN, "zxy", 2, 3),
+    (DOWN, "xyz", 5, 1),
     (UP, "zyx", 0, 3),
-    (UP, "zxy", 3, 3),
-    (ATTN, "zyx", 0, 2),
-    (ATTN, "zxy", 2, 2),
-    (ATTN, "yxz", 4, 2),
+    (UP, "zxy", 3, 2),
+    (UP, "xyz", 5, 1),
+    (QUERY_OUT, "zxy", 0, 1),
+    (QUERY_OUT, "yxz", 1, 2),
+    (KEY_VALUE, "zyx", 0, 2),
+    (KEY_VALUE, "zxy", 2, 1),
 )
 
 
@@ -464,8 +467,8 @@
     fq,
     ar,
     br,
-    asend,
-    bsend,
+    actives,
+    slopes,
     dgelu,
     hid32,
     unit1,
@@ -476,12 +479,20 @@
     doall,
     dkv32,
     dall,
+    give_down,
+    give_up,
+    take_down,
+    take_up,
+    keep_down,
+    keep_up,
     part_down,
     part_up,
-    part_attn,
+    part_qo,
+    part_kv,
     got_down,
     got_up,
-    got_attn,
+    got_qo,
+    got_kv,
     gm,
     dr,
     xs,
@@ -497,8 +508,6 @@
     her,
     frs,
     fss,
-    abr,
-    abs_,
     msr,
     mss,
     dor,
@@ -537,7 +546,7 @@
     def at(start, size, of=None):
         return pl.ds(many(start, size if of is None else of), size)
 
-    waits = []
+    waits = {}
     scope = contextlib.ExitStack()
 
     def phase(name):
@@ -556,14 +565,14 @@
     def arrived(ref, rsem):
         send(ref, ref, mss.at[0], rsem, sib).wait_recv()
 
-    def sent(ref, ssem):
-        waits.append(send(ref, ref, ssem, msr.at[0], sib).wait_send)
-
-    def sent_along_z(ref_of, ssem, rest=0, lines=1):
+    def sent(key, ref, ssem):
+        waits.setdefault(key, lambda: send(ref, ref, ssem, msr.at[0], sib).wait_send())
+
+    def sent_along_z(key, ref_of, ssem, rest=0, lines=1):
         for blocks_sent, when in ((1, (z == 0) | (z == 3)), (5, (z > 0) & (z < 3))):
             ref = ref_of(rest + lines * blocks_sent)
-            copy = send(ref, ref, ssem, msr.at[0], sib)
-            waits.append(partial(pl.when(when), copy.wait_send))
+            wait = partial(lambda ref: send(ref, ref, ssem, msr.at[0], sib).wait_send(), ref)
+            waits[key, blocks_sent] = partial(lambda when, wait: pl.when(when)(wait), when, wait)
 
     send_names, names = {}, {}
 
@@ -587,7 +596,7 @@
         pltpu.make_async_copy(down_w, wdn, wsem.at[5]),
     ]
     barrier = pltpu.get_barrier_semaphore()
-    peers = [device(x_, c_, y_) for x_ in (x, 1 - x) for c_ in (c, 1 - c) for y_ in (y, 1 - y)][1:]
+    peers = [sib, xn, yn, device(1 - x, c, 1 - y)]
     peers += [device(x, c, y, lax.rem(z + k, 4)) for k in (1, 2, 3)]
     for peer in peers:
         pl.semaphore_signal(barrier, inc=1, device_id=peer, device_id_type=MESH)
@@ -665,8 +674,8 @@
             arrived(slab(z + k, 1 - y), frs.at[2 * (z + k) + 1 - y])
             project_slab(z + k, 1 - y)
 
-    sent(fall.at[pl.ds(0, 4 * T), :], fss.at[1])
-    sent_along_z(lambda count: fall.at[pl.ds(0, T * count), :], fss.at[0])
+    sent("frames_y", fall.at[pl.ds(0, 4 * T), :], fss.at[1])
+    sent_along_z("frames_z", lambda count: fall.at[pl.ds(0, T * count), :], fss.at[0])
 
     phase("attention")
     pair_rows = at(T2 * z, T2)
@@ -708,7 +717,7 @@
     loads[3].wait()
     for b in range(blocks):
         arrived(attf.at[:, at(HW * (1 - y) + LANES * b, LANES, LANES)], her.at[b])
-    sent(att16.at[pl.ds(0, T), :], hes.at[0])
+    sent("heads", att16.at[pl.ds(0, T), :], hes.at[0])
     phase("out_norm1")
     branch = dot(attf[...], wo[...]) + out_b
     unit, inverse = rows_norm(frames[...] + branch)
@@ -716,100 +725,68 @@
     unit1[...] = unit
     rstd1[...] = jnp.broadcast_to(inverse, (T, LANES))
     hid32[...] = hidden
-    here = at(T * octant(x, c, y), T)
-
-    def rows_of(buffer, x_, c_, y_):
-        return buffer.at[at(T * octant(x_, c_, y_), T), :]
-
-    def halves_of(buffer, x_, c_, y_):
-        first = T * octant(x_, c_, y_)
+    here = at(T * (2 * y + x), T)
+
+    def rows_of(buffer, x_, y_):
+        return buffer.at[at(T * (2 * y_ + x_), T), :]
+
+    def halves_of(buffer, x_, y_):
+        first = T * (2 * y_ + x_)
         return buffer.at[at(first, T // 2), :], buffer.at[at(first + T // 2, T // 2), :]
 
-    def share(buffer, name, to, tag):
-        own = rows_of(buffer, x, c, y)
-        start(own, own, *one(name + tag, name), to)
+    def share_x(buffer, name):
+        own = rows_of(buffer, x, y)
+        start(own, own, *one(name + "_x", name), xn)
+
+    def share_y(buffer, name):
+        own = rows_of(buffer, x, y)
+        start(own, own, *one(name + "_y", name), yn)
 
     def from_x(buffer, name):
-        part, top = rows_of(buffer, 1 - x, c, y), halves_of(buffer, 1 - x, c, y)[0]
-        arrived(part, got_of(name + "_x"))
+        arrived(rows_of(buffer, 1 - x, y), got_of(name + "_x"))
+        top = halves_of(buffer, 1 - x, y)[0]
         start(top, top, *one(name + "_top", name), yn)
-        start(part, part, *one(name + "_dx", name), sib)
 
     def from_y(buffer, name):
-        part, bottom = rows_of(buffer, x, c, 1 - y), halves_of(buffer, x, c, 1 - y)[1]
-        arrived(part, got_of(name + "_y"))
+        arrived(rows_of(buffer, x, 1 - y), got_of(name + "_y"))
+        bottom = halves_of(buffer, x, 1 - y)[1]
         start(bottom, bottom, *one(name + "_bottom", name), xn)
-        start(part, part, *one(name + "_dy", name), sib)
 
     def from_diagonal(buffer, name):
-        part = rows_of(buffer, 1 - x, c, 1 - y)
-        top, bottom = halves_of(buffer, 1 - x, c, 1 - y)
+        top, bottom = halves_of(buffer, 1 - x, 1 - y)
         arrived(top, got_of(name + "_top"))
         arrived(bottom, got_of(name + "_bottom"))
-        start(part, part, *one(name + "_dd", name), sib)
-
-    def from_sibling(buffer, name):
-        arrived(rows_of(buffer, x, 1 - c, y), got_of(name + "_d"))
-        arrived(rows_of(buffer, 1 - x, 1 - c, y), got_of(name + "_dx"))
-        arrived(rows_of(buffer, x, 1 - c, 1 - y), got_of(name + "_dy"))
-        arrived(rows_of(buffer, 1 - x, 1 - c, 1 - y), got_of(name + "_dd"))
-
-    def spread(sent, got, index, x_, c_, y_):
-        to = octant(x_, c_, y_)
-        copy = send(
-            sent.at[to],
-            got.at[here, :],
-            abs_.at[index],
-            abr.at[index, octant(x, c, y)],
-            device(x_, c_, y_),
-        )
-        copy.start()
-
-    def spread_chip(sent, got, index, x_, y_):
-        for c_ in (c, 1 - c):
-            spread(sent, got, index, x_, c_, y_)
-
-    def spread_diagonal(sent, got, index):
-        spread_chip(sent, got, index, 1 - x, 1 - y)
-
-    def spread_y(sent, got, index):
-        spread_chip(sent, got, index, x, 1 - y)
-
-    def spread_arrived(got, index):
-        for x_, c_, y_ in [(x_, c_, y_) for x_ in (x, 1 - x) for c_ in (c, 1 - c) for y_ in (y, 1 - y)][1:]:
-            arrived(rows_of(got, x_, c_, y_), abr.at[index, octant(x_, c_, y_)])
 
     chips = ((1 - x, y), (x, 1 - y), (1 - x, 1 - y), (x, y))
 
-    sent(hq.at[pl.ds(0, 7 * T), :], group("hid"))
-    sent(fq.at[pl.ds(0, 7 * T), :], group("ffn"))
-    for index, got in enumerate((ar, br)):
-        sent(got.at[pl.ds(0, 7 * T), :], abs_.at[index])
+    for buffer, name in ((hq, "hid"), (fq, "ffn")):
+        sent(name, buffer.at[pl.ds(0, 3 * T), :], group(name))
     hq[here, :] = hidden.astype(BF16)
-    share(hq, "hid", xn, "_x")
-    share(hq, "hid", yn, "_y")
-    share(hq, "hid", sib, "_d")
+    share_x(hq, "hid")
+    share_y(hq, "hid")
 
     phase("up_gelu")
     loads[4].wait()
     scale = 2.0 ** -0.5
-    for order, (x_, y_) in enumerate(chips):
+
+    def active(hidden_rows, chip):
+        before = dot(hidden_rows, wup[:, at(D * chip, D)]) + up_rows[chip][0:1, :]
+        rise = 0.5 * (1.0 + lax.erf(before * scale))
+        slope = rise + before * jnp.exp(-0.5 * before * before) * (2.0 * math.pi) ** -0.5
+        return (before * rise).astype(BF16), slope
+
+    def grad_before(ffn_rows, chip, slope):
+        return (dot_nt(ffn_rows, wdn[at(D * chip, D), :]) * slope).astype(BF16)
+
+    for x_, y_ in chips:
         chip = 2 * y_ + x_
-        before = dot(hq[here, :], wup[:, at(D * chip, D)]) + up_rows[chip][0:1, :]
-        rise = 0.5 * (1.0 + lax.erf(before * scale))
-        dgelu[chip] = rise + before * jnp.exp(-0.5 * before * before) * (2.0 * math.pi) ** -0.5
-        active = (before * rise).astype(BF16)
-        asend[2 * chip] = active[:, :FO]
-        asend[2 * chip + 1] = active[:, FO:]
-        if order < 2:
-            spread_chip(asend, ar, 0, x_, y_)
-    spread(asend, ar, 0, x, 1 - c, y)
-    ar[here, :] = asend[octant(x, c, y)]
+        actives[chip], dgelu[chip] = active(hq[here, :], chip)
+    ar[here, :] = actives[2 * y + x]
     phase("down_norm2")
     loads[5].wait()
     fed = hid32[...] + down_b
-    for eighth in range(8):
-        fed = fed + dot(asend[eighth], wdn[pl.ds(FO * eighth, FO), :])
+    for quarter in range(4):
+        fed = fed + dot(actives[quarter], wdn[pl.ds(D * quarter, D), :])
     unit2, inverse2 = rows_norm(fed)
     encoded[...] = unit2 * gain2 + bias2
     cot = cotangent[...]
@@ -818,22 +795,25 @@
     vectors[11:12, :] = jnp.sum(cot, axis=0, keepdims=True)
     gmid[...] = grad_mid
     fq[here, :] = grad_mid.astype(BF16)
-    share(fq, "ffn", xn, "_x")
-    share(fq, "ffn", sib, "_d")
+    share_x(fq, "ffn")
+    share_y(fq, "ffn")
     vectors[9:10, :] = jnp.sum(fq[here, :].astype(F32), axis=0, keepdims=True)
     phase("ffn_back")
-    for order, (x_, y_) in enumerate(chips):
+    for x_, y_ in chips:
         chip = 2 * y_ + x_
-        quarter = at(D * chip, D)
-        low = (dot_nt(fq[here, :], wdn[quarter, :]) * dgelu[chip]).astype(BF16)
-        bsend[2 * chip] = low[:, :FO]
-        bsend[2 * chip + 1] = low[:, FO:]
-        if order == 0:
-            spread_chip(bsend, br, 1, x_, y_)
+        low = grad_before(fq[here, :], chip, dgelu[chip])
         vectors[pl.ds(5 + chip, 1), :] = jnp.sum(low.astype(F32), axis=0, keepdims=True)
-        gmid[...] += dot_nt(low, wup[:, quarter])
-    spread(bsend, br, 1, x, 1 - c, y)
-    br[here, :] = bsend[octant(x, c, y)]
+        gmid[...] += dot_nt(low, wup[:, at(D * chip, D)])
+    br[here, :] = low
+
+    def plane_active(x_, y_):
+        rows = at(T * (2 * y_ + x_), T)
+        ar[rows, :], slopes[rows, :] = active(hq[rows, :], 2 * y + x)
+
+    def plane_back(x_, y_):
+        rows = at(T * (2 * y_ + x_), T)
+        br[rows, :] = grad_before(fq[rows, :], 2 * y + x, slopes[rows, :])
+
     phase("norm1_back")
     grad_hidden = gmid[...]
     unit = unit1[...]
@@ -843,11 +823,13 @@
     gfirst[...] = grad_first
     gbr[mine, :] = grad_first.astype(BF16)
     start(gbr.at[mine, :], gbr.at[mine, :], *one("gbr"), yn)
-    sent(gbr.at[mine, :], group("gbr"))
+    sent("gbr", gbr.at[mine, :], group("gbr"))
     vectors[2:3, :] = jnp.sum(gbr[mine, :].astype(F32), axis=0, keepdims=True)
 
-    parts, gots = (part_down, part_up, part_attn), (got_down, got_up, got_attn)
-    slab_rows = (FO // 4, D // 4, EIGHTH)
+    parts, gots = (part_down, part_up, part_qo, part_kv), (got_down, got_up, got_qo, got_kv)
+    given, taken, kept = (give_down, give_up), (take_down, take_up), (keep_down, keep_up)
+    HALF = HW // 2
+    slab_rows = (FO // 4, D // 4, HALF // 4, HALF // 4)
 
     def part_slab(t, j):
         return parts[t].at[at(slab_rows[t] * j, slab_rows[t]), :]
@@ -860,7 +842,6 @@
         start(src, gots[t].at[slot], zss.at[t], zsr.at[t, slot], device(x, c, y, to))
 
     def sum_send(t):
-        sent(parts[t].at[pl.ds(0, 3 * slab_rows[t]), :], zss.at[t])
 
         @pl.when(outer)
         def _():
@@ -880,12 +861,16 @@
                 got[...] = (got[...].astype(F32) + part_slab(t, j)[...].astype(F32)).astype(BF16)
                 part_send(t, got, j, j, slot)
 
+    def attn_row(t, x_, y_, z_):
+        matrix = 3 * x_ if t == QUERY_OUT else 1 + x_
+        return D * matrix + HW * y_ + HALF * c + HALF // 4 * z_
+
     def own_tile(t):
         if t == DOWN:
             return sum_down.at[at(FO * octant(x, c, y) + EIGHTH // 2 * 2 * z, EIGHTH, EIGHTH), :]
         if t == UP:
             return sum_up.at[at(D // 4 * z, D // 4), at(FO * octant(x, c, y), FO)]
-        return sum_attn.at[at(D * row + HW * y + EIGHTH * z, EIGHTH), :]
+        return sum_attn.at[at(attn_row(t, x, y, z), HALF // 4), :]
 
     def sum_end(t):
         total = part_slab(t, z)[...].astype(F32)
@@ -894,7 +879,8 @@
             total = total + gots[t][slot].astype(F32)
         own_tile(t)[...] = total.astype(BF16)
 
-    unit_rows = (SIXTEENTH // 3, EIGHTH // 3, SIXTEENTH // 3)
+    unit = SIXTEENTH // 3
+    unit_rows = (unit, 2 * unit, unit, unit)
 
     def tile(u, x_, y_, z_):
         t, _, first, count = PIECES[u]
@@ -905,7 +891,7 @@
         if t == UP:
             start_row = D // 4 * z_ + rows * first
             return sum_up.at[at(start_row, rows * count, rows), at(FO * octant(x_, c, y_), FO)]
-        start_row = D * (2 * x_ + c) + HW * y_ + EIGHTH * z_ + rows * first
+        start_row = attn_row(t, x_, y_, z_) + rows * first
         return sum_attn.at[at(start_row, rows * count, rows), :]
 
     def gather_send(u, place, z_, ssem, rsem, to):
@@ -946,7 +932,7 @@
         gather_send(u, place, z_, ags.at[u], third_sem(u, slot), order_of(u)[1][1]).start()
 
     def gather_own(t):
-        for u in pieces_of(t):
+        for u in pieces_of(t, False):
             z_out(u, 0)
         for u in pieces_of(t):
             to_second(u, places[0], z)
@@ -999,15 +985,18 @@
             p = order_of(u)[0][0]
             arrived(tile(u, *places[p], z), second_sem(u, z))
             to_third(u, places[p], 1)
-            z_out(u, p)
             to_sibling(u, places[p], z)
 
     def plane_second(t):
         for u in pieces_of(t, True):
             for slot, p in ((0, order_of(u)[1][0]), (1, 3)):
                 arrived(tile(u, *places[p], z), third_sem(u, slot))
+                to_sibling(u, places[p], z)
+
+    def plane_out(t):
+        for u in pieces_of(t, True):
+            for p in (0, order_of(u)[0][0], order_of(u)[1][0], 3):
                 z_out(u, p)
-                to_sibling(u, places[p], z)
 
     def plane_z(t, k):
         for u in pieces_of(t, True):
@@ -1028,9 +1017,16 @@
 
             arrived(as_many(16), agdr.at[u])
             if z_last(u):
-                sent_along_z(as_many, ags.at[u], 19, 4)
+                sent_along_z(("gather", u), as_many, ags.at[u], 19, 4)
             else:
-                sent_along_z(as_many, ags.at[u], 28)
+                sent_along_z(("gather", u), as_many, ags.at[u], 28)
+
+    def matrix_put(family, x_, value):
+        for half_ in range(2):
+            gm[family, half_, x_] = value[HALF * half_ : HALF * (half_ + 1), :].astype(BF16)
+
+    def matrices_send(family):
+        start(gm.at[family, 1 - c], dr.at[family], *one(("d", family)), sib)
 
     def out_back():
         arrived(gbr.at[other, :], got_of("gbr"))
@@ -1043,35 +1039,27 @@
             delta = jnp.sum(half(product[:, lanes], head % 2), axis=-1, keepdims=True)
             stat[1] = jnp.where(lane == head, delta, stat[1])
         lsed[z, 8:16, :] = stat[1].T[0:8, :]
-        pl.when(not_last)(lambda: grads_push(z, 0))
-        pl.when(not_first)(lambda: grads_push(z, 1))
-        gm[3] = dot_tn(att16[...], gbr[...]).astype(BF16)
+        pl.when(not_last)(lambda: grads_push(z, zp))
+        pl.when(not_first)(lambda: grads_push(z, zm))
+        matrix_put(0, 1, dot_tn(att16[...], gbr[...]))
 
     def grads_rows(z_):
         return doall.at[at(T2 * z_, T2), :], lsed.at[z_]
 
-    def grads_copies(z_, direction):
-        to = (zp, zm)[direction]
-        return [
-            send(ref, ref, dos.at[index], dor.at[index, z_], to)
-            for index, ref in enumerate(grads_rows(z_))
-        ]
-
-    def grads_push(z_, direction):
-        for copy in grads_copies(z_, direction):
-            copy.start()
-
-    sent_along_z(lambda count: fall.at[pl.ds(0, T * count), :], dos.at[0])
-    sent_along_z(lambda count: lsed.at[pl.ds(0, count)], dos.at[1])
+    def grads_push(z_, to):
+        for index, ref in enumerate(grads_rows(z_)):
+            start(ref, ref, dos.at[index], dor.at[index, z_], to)
+
+    sent_along_z("grads", lambda count: fall.at[pl.ds(0, T * count), :], dos.at[0])
+    sent_along_z("logs", lambda count: lsed.at[pl.ds(0, count)], dos.at[1])
 
     def grads_arrive(k):
         def take(z_, more, direction):
             for index, ref in enumerate(grads_rows(z_)):
                 arrived(ref, dor.at[index, z_])
-            pl.when(more)(lambda: grads_push(z_, direction))
-
-        pl.when(z - k >= 0)(lambda: take(z - k, not_last, 0))
-        pl.when(z + k <= 3)(lambda: take(z + k, not_first, 1))
+            pl.when(more)(lambda: grads_push(z_, (zp, zm)[direction]))
+
+        sides(k, take)
 
     def queries_back():
         @pl.loop(0, blocks)
@@ -1113,21 +1101,22 @@
         if k > 0:
             pl.when(z + k <= 3)(lambda: keys_back(z + k))
 
-    def attention_weights():
+    def query_weights():
+        matrix_put(0, 0, dot_tn(dall[:, pl.ds(0, HW)], fall[pair_rows, :]))
+        matrices_send(0)
+
+    def key_value_weights():
         dall[:, pl.ds(HW, D)] = dkv32[...].astype(BF16)
-        grads = dot_tn(dall[...], fall[pair_rows, :])
-        for matrix in range(3):
-            gm[matrix] = grads[HW * matrix : HW * (matrix + 1), :].astype(BF16)
-        sent(dr, group("d"))
-        for slot in range(2):
-            start(gm.at[1 - c + 2 * slot], dr.at[slot], *one(("d", slot), "d"), sib)
+        grads = dot_tn(dall[:, pl.ds(HW, D)], fall[pair_rows, :])
+        matrix_put(1, 0, grads[:HW, :])
+        matrix_put(1, 1, grads[HW:, :])
+        matrices_send(1)
 
     def input_grad():
         into = dot_nt(dall[...], wqkv[...])
         dxo[...] = into
         dxs[...] = dxo[other, :].astype(BF16)
         start(dxs, dxr, *one("dx"), yn)
-        sent(dxs, group("dx"))
         sums = jnp.sum(dall[...].astype(F32), axis=0, keepdims=True)
         vectors[0:1, heads_here] = sums[:, :HW]
         vectors[1:2, heads_here] = sums[:, 2 * HW :]
@@ -1136,30 +1125,36 @@
         arrived(dxr, got_of("dx"))
         frames_grad[...] = gfirst[...] + dxo[mine, :] + dxr[...].astype(F32)
 
-    def attention_x():
-        for slot in range(2):
-            arrived(dr.at[slot], got_of(("d", slot)))
-        xs[...] = (gm[c + 2 * (1 - x)].astype(F32) + dr[1 - x].astype(F32)).astype(BF16)
-        start(xs, xr, *one("xs"), xn)
-        sent(xs, group("xs"))
-
-    def attention_z():
-        arrived(xr, got_of("xs"))
-        part_attn[...] = (gm[c + 2 * x].astype(F32) + dr[x].astype(F32) + xr[...].astype(F32)).astype(BF16)
-        sum_send(ATTN)
-
-    def down_grad():
-        part_down[...] = dot_tn(ar[...], fq[...]).astype(BF16)
-        sum_send(DOWN)
-
-    def up_grad():
-        part_up[...] = dot_tn(hq[...], br[...]).astype(BF16)
-        sum_send(UP)
+    def attention_x(family):
+        arrived(dr.at[family], got_of(("d", family)))
+        xs[family] = (gm[family, c, 1 - x].astype(F32) + dr[family, 1 - x].astype(F32)).astype(BF16)
+        start(xs.at[family], xr.at[family], *one(("xs", family)), xn)
+
+    def attention_z(family):
+        arrived(xr.at[family], got_of(("xs", family)))
+        total = gm[family, c, x].astype(F32) + dr[family, x].astype(F32) + xr[family].astype(F32)
+        parts[2 + family][...] = total.astype(BF16)
+        sum_send(2 + family)
+
+    def pair_half(t, half_):
+        columns = at(FO * half_, FO)
+        if t == DOWN:
+            return dot_tn(ar[:, columns], fq[...])
+        return dot_tn(hq[...], br[:, columns])
+
+    def pair_send(t):
+        given[t][...] = pair_half(t, 1 - c).astype(BF16)
+        start(given[t], taken[t], *one(("pair", t)), sib)
+        kept[t][...] = pair_half(t, c)
+
+    def pair_add(t):
+        arrived(taken[t], got_of(("pair", t)))
+        parts[t][...] = (kept[t][...] + taken[t][...].astype(F32)).astype(BF16)
+        sum_send(t)
 
     def vector_step(i, to):
         vsend[i] = vectors[...]
         start(vsend.at[i], vrecv.at[i], *one(("v", i)), to)
-        sent(vsend.at[i], group(("v", i)))
 
     def vector_add(i):
         arrived(vrecv.at[i], got_of(("v", i)))
@@ -1168,7 +1163,6 @@
     def vector_z():
         vsend[3] = vectors[...]
         vz[z] = vectors[...]
-        sent(vz.at[pl.ds(0, 3)], vzs.at[0])
         for k in (1, 2, 3):
             j = lax.rem(z + k, 4)
             start(vsend.at[3], vz.at[z], vzs.at[0], vzr.at[z], device(x, c, y, j))
@@ -1180,132 +1174,137 @@
         vectors[...] = (vz[0] + vz[1]) + (vz[2] + vz[3])
 
     dkv32[...] = jnp.zeros_like(dkv32)
-    phase("hid_forward")
+    for t in range(4):
+        sent(("sum", t), parts[t].at[pl.ds(0, 3 * slab_rows[t]), :], zss.at[t])
+    for t in (DOWN, UP):
+        sent(("pair", t), given[t], group(("pair", t)))
+    sent("dx", dxs, group("dx"))
+    for family in range(2):
+        sent(("d", family), dr.at[family], group(("d", family)))
+        sent(("xs", family), xs.at[family], group(("xs", family)))
+    for i in range(3):
+        sent(("v", i), vsend.at[i], group(("v", i)))
+    sent("vz", vz.at[pl.ds(0, 3)], vzs.at[0])
+    from_y(hq, "hid")
+    plane_active(x, 1 - y)
+    out_back()
     from_x(hq, "hid")
-    from_y(hq, "hid")
-    phase("out_back")
-    out_back()
-    share(fq, "ffn", yn, "_y")
-    spread_diagonal(asend, ar, 0)
-    phase("queries_back")
+    from_y(fq, "ffn")
+    plane_active(1 - x, y)
+    from_x(fq, "ffn")
     queries_back()
-    phase("ffn_x")
-    from_x(fq, "ffn")
-    phase("keys_back0")
+    from_diagonal(hq, "hid")
+    query_weights()
+    plane_active(1 - x, 1 - y)
+    grads_arrive(1)
+    from_diagonal(fq, "ffn")
+    pair_send(DOWN)
+    pair_add(DOWN)
     keys_back_at(0)
-    phase("ffn_y")
-    from_y(fq, "ffn")
-    spread_y(bsend, br, 1)
-    phase("grads1")
-    grads_arrive(1)
-    spread_diagonal(bsend, br, 1)
-    phase("keys_back1")
+    plane_back(1 - x, y)
+    plane_back(x, 1 - y)
+    plane_back(1 - x, 1 - y)
+    pair_send(UP)
+    attention_x(0)
+    grads_arrive(2)
+    sum_pass(DOWN)
     keys_back_at(1)
-    phase("hid_diag")
-    from_diagonal(hq, "hid")
-    phase("grads2")
-    grads_arrive(2)
-    phase("keys_back2")
+    pair_add(UP)
     keys_back_at(2)
-    phase("ffn_diag")
-    from_diagonal(fq, "ffn")
-    phase("grads3")
     grads_arrive(3)
-    phase("keys_back3")
+    sum_end(DOWN)
     keys_back_at(3)
-    phase("attn_weights")
-    attention_weights()
-    phase("wait_down")
-    from_sibling(fq, "ffn")
-    spread_arrived(ar, 0)
-    phase("down_grad")
-    down_grad()
-    phase("attention_x")
-    attention_x()
-    phase("input_grad")
+    key_value_weights()
+    gather_own(DOWN)
     input_grad()
-    phase("wait_up")
-    from_sibling(hq, "hid")
-    spread_arrived(br, 1)
-    phase("up_grad")
-    up_grad()
-    phase("vec0")
-    vector_step(0, sib)
-    vector_add(0)
-    vector_step(1, xn)
-    phase("down_pass")
-    sum_pass(DOWN)
-    phase("up_pass")
     sum_pass(UP)
-    phase("down_end")
-    sum_end(DOWN)
-    gather_own(DOWN)
-    vector_add(1)
-    vector_step(2, yn)
-    phase("attention_z")
-    attention_z()
-    phase("g_d1")
+    attention_x(1)
+    attention_z(0)
     gather_z(DOWN, 1)
-    gather_second(DOWN, 0)
-    phase("up_end")
     sum_end(UP)
     gather_own(UP)
-    phase("attn_pass")
-    sum_pass(ATTN)
+    vector_step(0, sib)
+    sum_pass(QUERY_OUT)
+    gather_z(DOWN, 2)
+    vector_add(0)
+    plane_first(DOWN)
+    attention_z(1)
+    gather_z(UP, 1)
+    sum_end(QUERY_OUT)
+    plane_second(DOWN)
+    plane_first(UP)
+    gather_z(UP, 2)
+    sum_pass(KEY_VALUE)
+    plane_out(DOWN)
+    gather_own(QUERY_OUT)
+    sum_end(KEY_VALUE)
+    gather_own(KEY_VALUE)
+    gather_second(DOWN, 0)
+    gather_z(QUERY_OUT, 1)
+    gather_z(KEY_VALUE, 1)
+    gather_z(UP, 3)
+    plane_second(UP)
+    plane_out(UP)
+    gather_z(DOWN, 3)
+    plane_z(DOWN, 1)
+    gather_z(QUERY_OUT, 2)
+    gather_z(QUERY_OUT, 3)
+    vector_step(1, xn)
+    plane_first(QUERY_OUT)
+    gather_second(QUERY_OUT, 0)
+    gather_z(KEY_VALUE, 2)
+    gather_second(UP, 3)
+    plane_z(UP, 1)
+    plane_z(DOWN, 2)
+    plane_z(UP, 2)
+    gather_second(KEY_VALUE, 1)
+    plane_second(QUERY_OUT)
+    gather_second(UP, 2)
+    vector_add(1)
+    gather_second(QUERY_OUT, 2)
+    gather_z(KEY_VALUE, 3)
+    gather_second(QUERY_OUT, 3)
+    vector_step(2, yn)
+    plane_out(QUERY_OUT)
+    gather_third(KEY_VALUE, 1)
+    gather_second(DOWN, 1)
+    gather_second(KEY_VALUE, 2)
+    gather_second(DOWN, 3)
+    gather_third(DOWN, 0)
+    plane_z(UP, 3)
+    gather_third(UP, 3)
+    gather_second(QUERY_OUT, 1)
+    plane_z(QUERY_OUT, 1)
+    gather_third(UP, 2)
+    gather_second(DOWN, 2)
+    gather_second(UP, 1)
+    gather_second(KEY_VALUE, 0)
     vector_add(2)
+    gather_third(DOWN, 1)
+    gather_third(KEY_VALUE, 2)
+    gather_third(QUERY_OUT, 2)
+    gather_third(QUERY_OUT, 0)
+    gather_third(QUERY_OUT, 3)
+    plane_z(QUERY_OUT, 2)
     vector_z()
+    gather_second(UP, 0)
+    gather_third(DOWN, 3)
+    gather_third(UP, 1)
+    gather_second(KEY_VALUE, 3)
+    gather_third(QUERY_OUT, 1)
+    gather_third(DOWN, 2)
+    plane_z(DOWN, 3)
+    gather_third(KEY_VALUE, 0)
     input_grad_end()
-    phase("g_d2")
-    gather_z(DOWN, 2)
-    gather_second(DOWN, 1)
-    gather_third(DOWN, 0)
-    phase("attn_end")
-    sum_end(ATTN)
-    gather_own(ATTN)
-    phase("g1")
-    gather_z(UP, 1)
-    gather_second(UP, 0)
+    gather_third(UP, 0)
+    gather_third(KEY_VALUE, 3)
+    plane_z(QUERY_OUT, 3)
     vector_end()
-    phase("g2")
-    gather_z(DOWN, 3)
-    gather_second(DOWN, 2)
-    gather_third(DOWN, 1)
-    gather_z(UP, 2)
-    gather_second(UP, 1)
-    gather_third(UP, 0)
-    plane_first(ATTN)
-    gather_z(ATTN, 1)
-    gather_second(ATTN, 0)
-    plane_second(ATTN)
-    phase("g3")
-    gather_second(DOWN, 3)
-    gather_third(DOWN, 2)
-    gather_z(UP, 3)
-    gather_second(UP, 2)
-    gather_third(UP, 1)
-    gather_z(ATTN, 2)
-    gather_second(ATTN, 1)
-    gather_third(ATTN, 0)
-    plane_z(ATTN, 1)
-    phase("g4")
-    gather_third(DOWN, 3)
-    gather_second(UP, 3)
-    gather_third(UP, 2)
-    gather_z(ATTN, 3)
-    gather_second(ATTN, 2)
-    gather_third(ATTN, 1)
-    plane_z(ATTN, 2)
-    phase("g5")
-    gather_third(UP, 3)
-    gather_second(ATTN, 3)
-    gather_third(ATTN, 2)
-    plane_z(ATTN, 3)
-    gather_third(ATTN, 3)
     phase("gather_end")
     gather_end()
     phase("sends_end")
     assert (len(send_names), len(names)) == (mss.shape[0], msr.shape[0])
-    for wait in waits:
+    for wait in waits.values():
         wait()
     phase(None)
 
@@ -1360,12 +1359,12 @@
         att32=wide(T2, HW),
         att16=low(T2, HW),
         attf=low(T, D),
-        hq=low(8 * T, D),
-        fq=low(8 * T, D),
-        ar=low(8 * T, FO),
-        br=low(8 * T, FO),
-        asend=low(8, T, FO),
-        bsend=low(8, T, FO),
+        hq=low(4 * T, D),
+        fq=low(4 * T, D),
+        ar=low(4 * T, D),
+        br=low(4 * T, D),
+        actives=low(4, T, D),
+        slopes=wide(4 * T, D),
         dgelu=wide(4, T, D),
         hid32=wide(T, D),
         unit1=wide(T, D),
@@ -1376,16 +1375,24 @@
         doall=low(S, HW),
         dkv32=wide(T2, D),
         dall=low(T2, 3 * HW),
+        give_down=low(FO, D),
+        give_up=low(D, FO),
+        take_down=low(FO, D),
+        take_up=low(D, FO),
+        keep_down=wide(FO, D),
+        keep_up=wide(D, FO),
         part_down=low(FO, D),
         part_up=low(D, FO),
-        part_attn=low(HW, D),
+        part_qo=low(HW // 2, D),
+        part_kv=low(HW // 2, D),
         got_down=low(4, FO // 4, D),
         got_up=low(4, D // 4, FO),
-        got_attn=low(4, EIGHTH, D),
-        gm=low(4, HW, D),
-        dr=low(2, HW, D),
-        xs=low(HW, D),
-        xr=low(HW, D),
+        got_qo=low(4, HW // 8, D),
+        got_kv=low(4, HW // 8, D),
+        gm=low(2, 2, 2, HW // 2, D),
+        dr=low(2, 2, HW // 2, D),
+        xs=low(2, HW // 2, D),
+        xr=low(2, HW // 2, D),
         dxs=low(T, D),
         dxr=low(T, D),
         dxo=wide(T2, D),
@@ -1397,14 +1404,12 @@
         her=dma((blocks,)),
         frs=dma((8,)),
         fss=dma((2,)),
-        abr=dma((2, 8)),
-        abs_=dma((2,)),
-        msr=dma((24,)),
-        mss=dma((9,)),
+        msr=dma((19,)),
+        mss=dma((13,)),
         dor=dma((2, 4)),
         dos=dma((2,)),
-        zsr=dma((3, 4)),
-        zss=dma((3,)),
+        zsr=dma((4, 4)),
+        zss=dma((4,)),
         agr=dma((n, 19)),
         ags=dma((n,)),
         agdr=dma((n,)),

time: 163 us -> 147 us (0.902)
  Pallas kernels: 162 us -> 146 us
    pallas_call x1, Pallas kernels: 152 us -> 136 us  [fused_layer(): pl.pallas_call(partial(layer_kernel, T, D, S, entries), out_shape=(pltpu....]
where the time goes in v3:
time: 147 us
  Pallas kernels  146 us (99%)
    pallas_call x1, Pallas kernels, fused_layer(): pl.pallas_call(partial(layer_kernel, T, D, S, entries), out_shape=(pltpu....  136 us
    pallas_call x1, Pallas kernels, widen(): pl.pallas_call(partial(widen_kernel, steps - 1, T, D), grid=(steps,), out...  9.84 us

profile of v3, /device:TPU:0, one launch (start us, length us, event | category | flops | bytes accessed | tf_op | source)
XLA Modules:
  0.0 147.1 jit_solution(10900901041661326054)
XLA Ops:
  0.7 136.4 %layer.1 = (f32[128,768]{1,0:T(8,128)S(1)}, f32[128,768]{1,0:T(8,128)S(1)}, f32[16,768]{1,0:T(8,128)S(1)}, bf16[3072,768]{1,0:T(8,128)(2,1)S(1)}, bf16[768,3072]...) custom-call(f32[128,768]{1,0:T(8,128)} %bitcast.4, f32[128,768]{1,0:T(8,128)} %bitcast.5, s32[1,6]{1,0:T(1,128)} %lengths.1, ...), custom_call_target="tpu_custom_call" | custom-call | tf_op jit(solution)/shard_map/layer/pallas_call | solution.py:1419
  137.1 9.8 %widen.1 = (f32[128,768]{1,0:T(8,128)}, f32[128,768]{1,0:T(8,128)}, f32[768,768]{1,0:T(8,128)}, f32[768]{0:T(1024)}, f32[768,768]{1,0:T(8,128)}, /*index=5*/f32[...) custom-call(f32[128,768]{1,0:T(8,128)S(1)} %get-tuple-element.40.enc, ...), custom_call_target="tpu_custom_call" | custom-call | tf_op jit(solution)/shard_map/widen/pallas_call | solution.py:1563

commit v4 on v3

--- a/solution.py
+++ b/solution.py
@@ -377,19 +377,20 @@
 LANES = 128
 F32, BF16 = jnp.float32, jnp.bfloat16
 VMEM_GRANT = 49 << 20
-DOWN, UP, QUERY_OUT, KEY_VALUE = range(4)
+DOWN, UP = 0, 1
+DOWN_0, DOWN_1, UP_0, UP_1, QUERY_OUT, KEY_VALUE = range(6)
+CHUNKS = 2
 
 PIECES = (
-    (DOWN, "zyx", 0, 2),
-    (DOWN, "zxy", 2, 3),
-    (DOWN, "xyz", 5, 1),
-    (UP, "zyx", 0, 3),
-    (UP, "zxy", 3, 2),
-    (UP, "xyz", 5, 1),
+    (DOWN_0, "zxy", 0, 3),
+    (DOWN_1, "zyx", 0, 2),
+    (DOWN_1, "xyz", 2, 1),
+    (UP_0, "zxy", 0, 3),
+    (UP_1, "zyx", 0, 2),
+    (UP_1, "xyz", 2, 1),
     (QUERY_OUT, "zxy", 0, 1),
     (QUERY_OUT, "yxz", 1, 2),
-    (KEY_VALUE, "zyx", 0, 2),
-    (KEY_VALUE, "zxy", 2, 1),
+    (KEY_VALUE, "zyx", 0, 3),
 )
 
 
@@ -447,6 +448,18 @@
     sum_down,
     sum_up,
     sum_attn,
+    frames_v,
+    cotangent_v,
+    lengths_v,
+    v0,
+    v1,
+    v2,
+    v3,
+    v4,
+    v5,
+    v6,
+    v7,
+    up_v,
     bias_rows,
     up_rows,
     fall,
@@ -504,6 +517,7 @@
     vrecv,
     vz,
     wsem,
+    asem,
     hes,
     her,
     frs,
@@ -523,9 +537,6 @@
     HW, T2, FO = D // 2, 2 * T, wup.shape[1] // 8
     blocks = HW // LANES
     EIGHTH, SIXTEENTH = D // 8, D // 16
-    out_b, gain1, bias1, down_b, gain2, bias2 = (
-        ref[...].reshape(1, D) for ref in (out_b, gain1, bias1, down_b, gain2, bias2)
-    )
     row, seq = lax.axis_index("row"), lax.axis_index("seq")
     x, c = lax.div(row, 2), lax.rem(row, 2)
     z, y = lax.div(seq, 2), lax.rem(seq, 2)
@@ -600,28 +611,44 @@
     peers += [device(x, c, y, lax.rem(z + k, 4)) for k in (1, 2, 3)]
     for peer in peers:
         pl.semaphore_signal(barrier, inc=1, device_id=peer, device_id_type=MESH)
-    for load in loads:
+    vectors_v = (v0, v1, v2, v3, v4, v5, v6, v7)
+    arrays = (frames, cotangent, lengths, query_b, value_b, out_b, gain1, bias1, up_b, down_b, gain2, bias2)
+    here_ = (frames_v, cotangent_v, lengths_v, *vectors_v[:5], up_v, *vectors_v[5:])
+    small = [pltpu.make_async_copy(array, ref, asem.at[i]) for i, (array, ref) in enumerate(zip(arrays, here_))]
+    small[0].start()
+    for load in loads[:3] + small[1:] + loads[3:]:
         load.start()
+    frames, cotangent, lengths = here_[:3]
+    query_b, value_b, out_b, gain1, bias1, up_b, down_b, gain2, bias2 = here_[3:]
+    vectors[...] = jnp.zeros_like(vectors)
+    small[0].wait()
     fall[at(T * seq, T), :] = frames[...].astype(BF16)
-    vectors[...] = jnp.zeros_like(vectors)
+    pl.semaphore_wait(barrier, len(peers))
+
+    phase("frames_gather")
+
+    CHUNK = T // CHUNKS
+
+    def chunk(z_, y_, h):
+        return fall.at[at(T * (2 * z_ + y_) + CHUNK * h, CHUNK), :]
+
+    def push(z_, h, direction):
+        to = (zp, zm, yn)[direction]
+        start(chunk(z_, y, h), chunk(z_, y, h), fss.at[direction // 2], frs.at[h, 2 * z_ + y], to)
+
+    for h in range(CHUNKS):
+        pl.when(not_last)(lambda: push(z, h, 0))
+        pl.when(not_first)(lambda: push(z, h, 1))
+        push(z, h, 2)
+    for load in small[1:]:
+        load.wait()
     bias_rows[0:1, :] = query_b[...].reshape(1, D)
     bias_rows[1:2, :] = value_b[...].reshape(1, D)
     for quarter in range(4):
         up_rows[quarter] = jnp.broadcast_to(up_b[pl.ds(D * quarter, D)].reshape(1, D), (8, D))
-    pl.semaphore_wait(barrier, len(peers))
-
-    phase("frames_gather")
-
-    def slab(z_, y_):
-        return fall.at[at(T * (2 * z_ + y_), T), :]
-
-    def push(z_, direction):
-        to = (zp, zm, yn)[direction]
-        return send(slab(z_, y), slab(z_, y), fss.at[direction // 2], frs.at[2 * z_ + y], to)
-
-    pl.when(not_last)(lambda: push(z, 0).start())
-    pl.when(not_first)(lambda: push(z, 1).start())
-    push(z, 2).start()
+    out_b, gain1, bias1, down_b, gain2, bias2 = (
+        ref[...].reshape(1, D) for ref in (out_b, gain1, bias1, down_b, gain2, bias2)
+    )
     query_bias, value_bias = bias_rows[0:1, heads_here], bias_rows[1:2, heads_here]
     for load in loads[:3]:
         load.wait()
@@ -638,9 +665,9 @@
     key_at = lax.broadcasted_iota(jnp.int32, (1, S), 1)
     query_at = lax.broadcasted_iota(jnp.int32, (T2, 1), 0) + T2 * z
     key_number, query_number = jnp.zeros((1, S), jnp.int32), jnp.zeros((T2, 1), jnp.int32)
-    clip_end = jnp.int32(0)
+    clip_end = jnp.zeros((1, 1), jnp.int32)
     for entry in range(entries):
-        clip_end = clip_end + lengths[0, entry]
+        clip_end = clip_end + lengths[0:1, entry : entry + 1]
         key_number = key_number + jnp.where(clip_end <= key_at, 1, 0)
         query_number = query_number + jnp.where(clip_end <= query_at, 1, 0)
     mask[...] = jnp.where(query_number == key_number, 0.0, MASK_SCORE)
@@ -649,30 +676,29 @@
     def _(k):
         left, right = z - k - 1, z + k + 1
 
-        @pl.when(left >= 0)
-        def _():
-            arrived(slab(left, y), frs.at[2 * left + y])
-            pl.when(not_last)(lambda: push(left, 0).start())
-            push(left, 2).start()
-
-        @pl.when(right <= 3)
-        def _():
-            arrived(slab(right, y), frs.at[2 * right + y])
-            pl.when(not_first)(lambda: push(right, 1).start())
-            push(right, 2).start()
+        for h in range(CHUNKS):
+
+            @pl.when(left >= 0)
+            def _():
+                arrived(chunk(left, y, h), frs.at[h, 2 * left + y])
+                pl.when(not_last)(lambda: push(left, h, 0))
+                push(left, h, 2)
+
+            @pl.when(right <= 3)
+            def _():
+                arrived(chunk(right, y, h), frs.at[h, 2 * right + y])
+                pl.when(not_first)(lambda: push(right, h, 1))
+                push(right, h, 2)
+
+        def across_y(z_):
+            for h in range(CHUNKS):
+                arrived(chunk(z_, 1 - y, h), frs.at[h, 2 * z_ + 1 - y])
+            project_slab(z_, 1 - y)
 
         pl.when(left >= 0)(lambda: project_slab(left, y))
         pl.when(right <= 3)(lambda: project_slab(right, y))
-
-        @pl.when(z - k >= 0)
-        def _():
-            arrived(slab(z - k, 1 - y), frs.at[2 * (z - k) + 1 - y])
-            project_slab(z - k, 1 - y)
-
-        @pl.when((k > 0) & (z + k <= 3))
-        def _():
-            arrived(slab(z + k, 1 - y), frs.at[2 * (z + k) + 1 - y])
-            project_slab(z + k, 1 - y)
+        pl.when(z - k >= 0)(lambda: across_y(z - k))
+        pl.when((k > 0) & (z + k <= 3))(lambda: across_y(z + k))
 
     sent("frames_y", fall.at[pl.ds(0, 4 * T), :], fss.at[1])
     sent_along_z("frames_z", lambda count: fall.at[pl.ds(0, T * count), :], fss.at[0])
@@ -692,20 +718,30 @@
         part, there = at(LANES * b, LANES), at(HW * y + LANES * b, LANES, LANES)
         return send(att16.at[other, part], attf.at[:, there], hes.at[0], her.at[b], yn)
 
+    def both(value):
+        return jnp.concatenate([half(value, 0), half(value, 1)], axis=0).astype(BF16)
+
+    def pick(stacked):
+        return jnp.where(low_half, stacked[:T2], stacked[T2:])
+
+    def block_lanes(b):
+        return at(LANES * b, LANES), at(HW + LANES * b, LANES, LANES)
+
     @pl.loop(0, blocks)
     def _(b):
-        lanes, value_lanes = at(LANES * b, LANES), at(HW + LANES * b, LANES, LANES)
+        lanes, value_lanes = block_lanes(b)
         queries = qall[pair_rows, lanes].astype(F32)
         outs = []
         for which in range(2):
+            head = 2 * b + which
             scores = dot_nt(half(queries, which).astype(BF16), kv[:, lanes]) + mask[...]
             peak = jnp.max(scores, axis=-1, keepdims=True)
             powers = jnp.exp(scores - peak)
             total = jnp.sum(powers, axis=-1, keepdims=True)
             low = (powers * (1.0 / total)).astype(BF16)
-            probs[2 * b + which] = low
+            probs[head] = low
             outs.append(dot(low, kv[:, value_lanes]))
-            stat[0] = jnp.where(lane == 2 * b + which, peak + jnp.log(total), stat[0])
+            stat[0] = jnp.where(lane == head, peak + jnp.log(total), stat[0])
         out = jnp.where(low_half, outs[0], outs[1])
         att32[:, lanes] = out
         att16[:, lanes] = out.astype(BF16)
@@ -735,22 +771,30 @@
         return buffer.at[at(first, T // 2), :], buffer.at[at(first + T // 2, T // 2), :]
 
     def share_x(buffer, name):
-        own = rows_of(buffer, x, y)
-        start(own, own, *one(name + "_x", name), xn)
+        top, bottom = halves_of(buffer, x, y)
+        start(top, top, *one(name + "_x", name), xn)
+        start(bottom, bottom, *one(name + "_x_rest", name), xn)
 
     def share_y(buffer, name):
-        own = rows_of(buffer, x, y)
-        start(own, own, *one(name + "_y", name), yn)
+        top, bottom = halves_of(buffer, x, y)
+        start(bottom, bottom, *one(name + "_y", name), yn)
+        start(top, top, *one(name + "_y_rest", name), yn)
 
     def from_x(buffer, name):
-        arrived(rows_of(buffer, 1 - x, y), got_of(name + "_x"))
         top = halves_of(buffer, 1 - x, y)[0]
+        arrived(top, got_of(name + "_x"))
         start(top, top, *one(name + "_top", name), yn)
 
     def from_y(buffer, name):
-        arrived(rows_of(buffer, x, 1 - y), got_of(name + "_y"))
         bottom = halves_of(buffer, x, 1 - y)[1]
+        arrived(bottom, got_of(name + "_y"))
         start(bottom, bottom, *one(name + "_bottom", name), xn)
+
+    def rest_x(buffer, name):
+        arrived(halves_of(buffer, 1 - x, y)[1], got_of(name + "_x_rest"))
+
+    def rest_y(buffer, name):
+        arrived(halves_of(buffer, x, 1 - y)[0], got_of(name + "_y_rest"))
 
     def from_diagonal(buffer, name):
         top, bottom = halves_of(buffer, 1 - x, 1 - y)
@@ -826,10 +870,11 @@
     sent("gbr", gbr.at[mine, :], group("gbr"))
     vectors[2:3, :] = jnp.sum(gbr[mine, :].astype(F32), axis=0, keepdims=True)
 
-    parts, gots = (part_down, part_up, part_qo, part_kv), (got_down, got_up, got_qo, got_kv)
+    parts = (*(part_down.at[q] for q in range(2)), *(part_up.at[q] for q in range(2)), part_qo, part_kv)
+    gots = (*(got_down.at[q] for q in range(2)), *(got_up.at[q] for q in range(2)), got_qo, got_kv)
     given, taken, kept = (give_down, give_up), (take_down, take_up), (keep_down, keep_up)
     HALF = HW // 2
-    slab_rows = (FO // 4, D // 4, HALF // 4, HALF // 4)
+    slab_rows = (FO // 8, FO // 8, D // 8, D // 8, HALF // 4, HALF // 4)
 
     def part_slab(t, j):
         return parts[t].at[at(slab_rows[t] * j, slab_rows[t]), :]
@@ -866,10 +911,10 @@
         return D * matrix + HW * y_ + HALF * c + HALF // 4 * z_
 
     def own_tile(t):
-        if t == DOWN:
-            return sum_down.at[at(FO * octant(x, c, y) + EIGHTH // 2 * 2 * z, EIGHTH, EIGHTH), :]
-        if t == UP:
-            return sum_up.at[at(D // 4 * z, D // 4), at(FO * octant(x, c, y), FO)]
+        if t <= DOWN_1:
+            return sum_down.at[at(FO * octant(x, c, y) + FO // 2 * t + FO // 8 * z, FO // 8), :]
+        if t <= UP_1:
+            return sum_up.at[at(D // 2 * (t - UP_0) + D // 8 * z, D // 8), at(FO * octant(x, c, y), FO)]
         return sum_attn.at[at(attn_row(t, x, y, z), HALF // 4), :]
 
     def sum_end(t):
@@ -880,16 +925,16 @@
         own_tile(t)[...] = total.astype(BF16)
 
     unit = SIXTEENTH // 3
-    unit_rows = (unit, 2 * unit, unit, unit)
+    unit_rows = (unit, unit, 2 * unit, 2 * unit, unit, unit)
 
     def tile(u, x_, y_, z_):
         t, _, first, count = PIECES[u]
         rows = unit_rows[t]
-        if t == DOWN:
-            start_row = FO * octant(x_, c, y_) + EIGHTH * z_ + rows * first
+        if t <= DOWN_1:
+            start_row = FO * octant(x_, c, y_) + FO // 2 * t + FO // 8 * z_ + rows * first
             return sum_down.at[at(start_row, rows * count, rows), :]
-        if t == UP:
-            start_row = D // 4 * z_ + rows * first
+        if t <= UP_1:
+            start_row = D // 2 * (t - UP_0) + D // 8 * z_ + rows * first
             return sum_up.at[at(start_row, rows * count, rows), at(FO * octant(x_, c, y_), FO)]
         start_row = attn_row(t, x_, y_, z_) + rows * first
         return sum_attn.at[at(start_row, rows * count, rows), :]
@@ -1013,7 +1058,7 @@
         for u, (_, _, _, count) in enumerate(PIECES):
 
             def as_many(blocks_sent):
-                return sum_down.at[pl.ds(0, unit_rows[DOWN] * count * blocks_sent), :]
+                return sum_down.at[pl.ds(0, unit * count * blocks_sent), :]
 
             arrived(as_many(16), agdr.at[u])
             if z_last(u):
@@ -1064,7 +1109,7 @@
     def queries_back():
         @pl.loop(0, blocks)
         def _(b):
-            lanes, value_lanes = at(LANES * b, LANES), at(HW + LANES * b, LANES, LANES)
+            lanes, value_lanes = block_lanes(b)
             heads = doall[pair_rows, lanes].astype(F32)
             product = heads * att32[:, lanes]
             pieces = []
@@ -1081,20 +1126,19 @@
 
         @pl.loop(0, blocks)
         def _(b):
-            lanes, value_lanes = at(LANES * b, LANES), at(HW + LANES * b, LANES, LANES)
-            keys, values = kv[pair_rows, lanes].astype(F32), kv[pair_rows, value_lanes].astype(F32)
+            lanes, value_lanes = block_lanes(b)
             queries, grads = qall[rows, lanes], doall[rows, lanes]
-            key_pieces, value_pieces = [], []
+            scores = dot_nt(both(kv[pair_rows, lanes].astype(F32)), queries)
+            grad_probs = dot_nt(both(kv[pair_rows, value_lanes].astype(F32)), grads)
+            lows, grad_scores = [], []
             for which in range(2):
-                head = 2 * b + which
-                scores = dot_nt(half(keys, which).astype(BF16), queries) + mask[:, rows]
-                powers = jnp.exp(scores - lsed[z_, pl.ds(head, 1), :])
-                grad_probs = dot_nt(half(values, which).astype(BF16), grads)
-                grad_scores = powers * (grad_probs - lsed[z_, pl.ds(8 + head, 1), :])
-                key_pieces.append(dot(grad_scores.astype(BF16), queries))
-                value_pieces.append(dot(powers.astype(BF16), grads))
-            dkv32[:, lanes] += jnp.where(low_half, key_pieces[0], key_pieces[1])
-            dkv32[:, value_lanes] += jnp.where(low_half, value_pieces[0], value_pieces[1])
+                part, head = slice(T2 * which, T2 * (which + 1)), 2 * b + which
+                powers = jnp.exp(scores[part] + mask[:, rows] - lsed[z_, pl.ds(head, 1), :])
+                shifted = grad_probs[part] - lsed[z_, pl.ds(8 + head, 1), :]
+                lows.append(powers.astype(BF16))
+                grad_scores.append((powers * shifted).astype(BF16))
+            dkv32[:, lanes] += pick(dot(jnp.concatenate(grad_scores, axis=0), queries))
+            dkv32[:, value_lanes] += pick(dot(jnp.concatenate(lows, axis=0), grads))
 
     def keys_back_at(k):
         pl.when(z - k >= 0)(lambda: keys_back(z - k))
@@ -1133,8 +1177,8 @@
     def attention_z(family):
         arrived(xr.at[family], got_of(("xs", family)))
         total = gm[family, c, x].astype(F32) + dr[family, x].astype(F32) + xr[family].astype(F32)
-        parts[2 + family][...] = total.astype(BF16)
-        sum_send(2 + family)
+        parts[4 + family][...] = total.astype(BF16)
+        sum_send(4 + family)
 
     def pair_half(t, half_):
         columns = at(FO * half_, FO)
@@ -1143,14 +1187,20 @@
         return dot_tn(hq[...], br[:, columns])
 
     def pair_send(t):
-        given[t][...] = pair_half(t, 1 - c).astype(BF16)
-        start(given[t], taken[t], *one(("pair", t)), sib)
-        kept[t][...] = pair_half(t, c)
-
-    def pair_add(t):
-        arrived(taken[t], got_of(("pair", t)))
-        parts[t][...] = (kept[t][...] + taken[t][...].astype(F32)).astype(BF16)
-        sum_send(t)
+        half_ = pair_half(t, 1 - c).astype(BF16)
+        rows = half_.shape[0] // 2
+        for q in range(2):
+            given[t][q] = half_[rows * q : rows * (q + 1)]
+            start(given[t].at[q], taken[t].at[q], *one(("pair", t, q), ("pair", t)), sib)
+        half_ = pair_half(t, c)
+        for q in range(2):
+            kept[t][q] = half_[rows * q : rows * (q + 1)]
+
+    def pair_add(family):
+        t, q = family // 2, family % 2
+        arrived(taken[t].at[q], got_of(("pair", t, q)))
+        parts[family][...] = (kept[t][q] + taken[t][q].astype(F32)).astype(BF16)
+        sum_send(family)
 
     def vector_step(i, to):
         vsend[i] = vectors[...]
@@ -1174,7 +1224,7 @@
         vectors[...] = (vz[0] + vz[1]) + (vz[2] + vz[3])
 
     dkv32[...] = jnp.zeros_like(dkv32)
-    for t in range(4):
+    for t in range(6):
         sent(("sum", t), parts[t].at[pl.ds(0, 3 * slab_rows[t]), :], zss.at[t])
     for t in (DOWN, UP):
         sent(("pair", t), given[t], group(("pair", t)))
@@ -1185,119 +1235,153 @@
     for i in range(3):
         sent(("v", i), vsend.at[i], group(("v", i)))
     sent("vz", vz.at[pl.ds(0, 3)], vzs.at[0])
+    from_x(hq, "hid")
     from_y(hq, "hid")
+    rest_x(hq, "hid")
+    rest_y(hq, "hid")
+    from_y(fq, "ffn")
     plane_active(x, 1 - y)
+    plane_active(1 - x, y)
     out_back()
-    from_x(hq, "hid")
-    from_y(fq, "ffn")
-    plane_active(1 - x, y)
     from_x(fq, "ffn")
+    rest_y(fq, "ffn")
     queries_back()
+    rest_x(fq, "ffn")
     from_diagonal(hq, "hid")
-    query_weights()
     plane_active(1 - x, 1 - y)
-    grads_arrive(1)
     from_diagonal(fq, "ffn")
     pair_send(DOWN)
-    pair_add(DOWN)
+    grads_arrive(1)
+    pair_add(DOWN_0)
+    plane_back(1 - x, 1 - y)
+    query_weights()
+    plane_back(x, 1 - y)
+    keys_back_at(1)
+    attention_x(0)
+    sum_pass(DOWN_0)
+    pair_add(DOWN_1)
+    plane_back(1 - x, y)
+    grads_arrive(2)
+    pair_send(UP)
+    sum_pass(DOWN_1)
+    keys_back_at(2)
+    sum_end(DOWN_0)
+    gather_own(DOWN_0)
     keys_back_at(0)
-    plane_back(1 - x, y)
-    plane_back(x, 1 - y)
-    plane_back(1 - x, 1 - y)
-    pair_send(UP)
-    attention_x(0)
-    grads_arrive(2)
-    sum_pass(DOWN)
-    keys_back_at(1)
-    pair_add(UP)
-    keys_back_at(2)
+    pair_add(UP_0)
+    sum_end(DOWN_1)
+    gather_own(DOWN_1)
     grads_arrive(3)
-    sum_end(DOWN)
     keys_back_at(3)
+    gather_z(DOWN_0, 1)
     key_value_weights()
-    gather_own(DOWN)
+    pair_add(UP_1)
+    sum_pass(UP_0)
+    attention_x(1)
     input_grad()
-    sum_pass(UP)
-    attention_x(1)
+    gather_z(DOWN_0, 2)
     attention_z(0)
-    gather_z(DOWN, 1)
-    sum_end(UP)
-    gather_own(UP)
+    sum_pass(UP_1)
+    gather_z(DOWN_1, 1)
     vector_step(0, sib)
+    plane_first(DOWN_1)
+    gather_z(DOWN_0, 3)
+    gather_second(DOWN_0, 0)
+    sum_end(UP_0)
+    gather_own(UP_0)
+    sum_end(UP_1)
+    gather_own(UP_1)
+    attention_z(1)
+    gather_z(DOWN_1, 2)
     sum_pass(QUERY_OUT)
-    gather_z(DOWN, 2)
+    plane_second(DOWN_1)
+    gather_z(UP_1, 1)
     vector_add(0)
-    plane_first(DOWN)
-    attention_z(1)
-    gather_z(UP, 1)
+    plane_out(DOWN_1)
+    gather_second(DOWN_1, 0)
+    gather_z(UP_1, 2)
+    sum_pass(KEY_VALUE)
     sum_end(QUERY_OUT)
-    plane_second(DOWN)
-    plane_first(UP)
-    gather_z(UP, 2)
-    sum_pass(KEY_VALUE)
-    plane_out(DOWN)
+    gather_z(UP_0, 1)
+    plane_first(UP_1)
+    plane_z(DOWN_1, 1)
     gather_own(QUERY_OUT)
     sum_end(KEY_VALUE)
+    gather_second(DOWN_0, 2)
     gather_own(KEY_VALUE)
-    gather_second(DOWN, 0)
+    gather_second(DOWN_1, 2)
+    gather_z(UP_1, 3)
+    gather_z(UP_0, 2)
+    plane_second(UP_1)
+    gather_z(DOWN_1, 3)
+    plane_out(UP_1)
+    plane_first(QUERY_OUT)
+    input_grad_end()
+    gather_third(DOWN_0, 2)
+    gather_second(UP_1, 1)
     gather_z(QUERY_OUT, 1)
     gather_z(KEY_VALUE, 1)
-    gather_z(UP, 3)
-    plane_second(UP)
-    plane_out(UP)
-    gather_z(DOWN, 3)
-    plane_z(DOWN, 1)
+    gather_second(UP_1, 2)
+    gather_second(DOWN_1, 3)
+    vector_step(1, xn)
+    gather_second(DOWN_0, 3)
+    plane_z(DOWN_1, 2)
     gather_z(QUERY_OUT, 2)
+    plane_second(QUERY_OUT)
+    gather_z(UP_0, 3)
+    gather_second(UP_0, 2)
+    gather_second(DOWN_0, 1)
+    plane_z(UP_1, 1)
+    gather_z(KEY_VALUE, 2)
+    plane_out(QUERY_OUT)
+    gather_third(DOWN_1, 0)
+    vector_add(1)
+    gather_z(KEY_VALUE, 3)
+    gather_second(DOWN_1, 1)
+    vector_step(2, yn)
+    gather_third(DOWN_1, 2)
+    plane_z(QUERY_OUT, 1)
+    gather_second(KEY_VALUE, 0)
+    gather_second(QUERY_OUT, 1)
+    gather_second(UP_1, 3)
+    gather_second(QUERY_OUT, 2)
+    gather_second(QUERY_OUT, 0)
+    gather_third(UP_0, 2)
+    gather_second(UP_1, 0)
+    gather_second(KEY_VALUE, 3)
+    gather_second(UP_0, 1)
+    gather_third(DOWN_1, 3)
+    gather_third(UP_1, 2)
+    vector_add(2)
+    gather_third(DOWN_0, 1)
+    plane_z(UP_1, 2)
+    gather_third(QUERY_OUT, 0)
+    gather_second(UP_0, 0)
+    plane_z(QUERY_OUT, 2)
+    gather_second(UP_0, 3)
     gather_z(QUERY_OUT, 3)
-    vector_step(1, xn)
-    plane_first(QUERY_OUT)
-    gather_second(QUERY_OUT, 0)
-    gather_z(KEY_VALUE, 2)
-    gather_second(UP, 3)
-    plane_z(UP, 1)
-    plane_z(DOWN, 2)
-    plane_z(UP, 2)
+    vector_z()
+    gather_second(KEY_VALUE, 2)
+    gather_third(UP_0, 1)
+    plane_z(DOWN_1, 3)
+    gather_third(DOWN_0, 0)
+    gather_third(KEY_VALUE, 3)
+    gather_third(DOWN_0, 3)
     gather_second(KEY_VALUE, 1)
-    plane_second(QUERY_OUT)
-    gather_second(UP, 2)
-    vector_add(1)
-    gather_second(QUERY_OUT, 2)
-    gather_z(KEY_VALUE, 3)
     gather_second(QUERY_OUT, 3)
-    vector_step(2, yn)
-    plane_out(QUERY_OUT)
+    gather_third(UP_1, 3)
+    gather_third(UP_0, 0)
+    gather_third(UP_1, 0)
+    gather_third(DOWN_1, 1)
+    gather_third(KEY_VALUE, 2)
+    gather_third(UP_1, 1)
+    plane_z(UP_1, 3)
+    gather_third(KEY_VALUE, 0)
+    gather_third(QUERY_OUT, 1)
+    gather_third(UP_0, 3)
+    gather_third(QUERY_OUT, 3)
     gather_third(KEY_VALUE, 1)
-    gather_second(DOWN, 1)
-    gather_second(KEY_VALUE, 2)
-    gather_second(DOWN, 3)
-    gather_third(DOWN, 0)
-    plane_z(UP, 3)
-    gather_third(UP, 3)
-    gather_second(QUERY_OUT, 1)
-    plane_z(QUERY_OUT, 1)
-    gather_third(UP, 2)
-    gather_second(DOWN, 2)
-    gather_second(UP, 1)
-    gather_second(KEY_VALUE, 0)
-    vector_add(2)
-    gather_third(DOWN, 1)
-    gather_third(KEY_VALUE, 2)
     gather_third(QUERY_OUT, 2)
-    gather_third(QUERY_OUT, 0)
-    gather_third(QUERY_OUT, 3)
-    plane_z(QUERY_OUT, 2)
-    vector_z()
-    gather_second(UP, 0)
-    gather_third(DOWN, 3)
-    gather_third(UP, 1)
-    gather_second(KEY_VALUE, 3)
-    gather_third(QUERY_OUT, 1)
-    gather_third(DOWN, 2)
-    plane_z(DOWN, 3)
-    gather_third(KEY_VALUE, 0)
-    input_grad_end()
-    gather_third(UP, 0)
-    gather_third(KEY_VALUE, 3)
     plane_z(QUERY_OUT, 3)
     vector_end()
     phase("gather_end")
@@ -1335,14 +1419,15 @@
     HW, T2, EIGHTH, FO = D // 2, 2 * T, D // 8, F // 8
     blocks = HW // LANES
     entries = clip_lengths.shape[1]
-    vmem, smem, hbm = (
-        pl.BlockSpec(memory_space=pltpu.VMEM),
-        pl.BlockSpec(memory_space=pltpu.SMEM),
-        pl.BlockSpec(memory_space=pl.ANY),
-    )
+    vmem, hbm = pl.BlockSpec(memory_space=pltpu.VMEM), pl.BlockSpec(memory_space=pl.ANY)
     dma, n = pltpu.SemaphoreType.DMA, len(PIECES)
     low, wide = (lambda *shape: pltpu.VMEM(shape, BF16)), (lambda *shape: pltpu.VMEM(shape, F32))
     scratch = dict(
+        frames_v=wide(T, D),
+        cotangent_v=wide(T, D),
+        lengths_v=pltpu.VMEM((1, entries), jnp.int32),
+        **{f"v{i}": wide(D) for i in range(8)},
+        up_v=wide(F),
         bias_rows=wide(8, D),
         up_rows=wide(4, 8, D),
         fall=low(S, D),
@@ -1375,18 +1460,18 @@
         doall=low(S, HW),
         dkv32=wide(T2, D),
         dall=low(T2, 3 * HW),
-        give_down=low(FO, D),
-        give_up=low(D, FO),
-        take_down=low(FO, D),
-        take_up=low(D, FO),
-        keep_down=wide(FO, D),
-        keep_up=wide(D, FO),
-        part_down=low(FO, D),
-        part_up=low(D, FO),
+        give_down=low(2, FO // 2, D),
+        give_up=low(2, D // 2, FO),
+        take_down=low(2, FO // 2, D),
+        take_up=low(2, D // 2, FO),
+        keep_down=wide(2, FO // 2, D),
+        keep_up=wide(2, D // 2, FO),
+        part_down=low(2, FO // 2, D),
+        part_up=low(2, D // 2, FO),
         part_qo=low(HW // 2, D),
         part_kv=low(HW // 2, D),
-        got_down=low(4, FO // 4, D),
-        got_up=low(4, D // 4, FO),
+        got_down=low(2, 4, FO // 8, D),
+        got_up=low(2, 4, D // 8, FO),
         got_qo=low(4, HW // 8, D),
         got_kv=low(4, HW // 8, D),
         gm=low(2, 2, 2, HW // 2, D),
@@ -1400,16 +1485,17 @@
         vrecv=wide(3, 16, D),
         vz=wide(4, 16, D),
         wsem=dma((6,)),
+        asem=dma((12,)),
         hes=dma((1,)),
         her=dma((blocks,)),
-        frs=dma((8,)),
+        frs=dma((CHUNKS, 8)),
         fss=dma((2,)),
-        msr=dma((19,)),
+        msr=dma((25,)),
         mss=dma((13,)),
         dor=dma((2, 4)),
         dos=dma((2,)),
-        zsr=dma((4, 4)),
-        zss=dma((4,)),
+        zsr=dma((6, 4)),
+        zss=dma((6,)),
         agr=dma((n, 19)),
         ags=dma((n,)),
         agdr=dma((n,)),
@@ -1426,7 +1512,7 @@
             pltpu.VMEM((D, F), BF16),
             pltpu.VMEM((4 * D, D), BF16),
         ),
-        in_specs=[vmem, vmem, smem] + [hbm] * 6 + [vmem] * 9,
+        in_specs=[hbm] * 18,
         out_specs=(vmem,) * 6,
         scratch_shapes=list(scratch.values()),
         compiler_params=pltpu.CompilerParams(

time: 147 us -> 146 us (level)
  Pallas kernels: 146 us -> 144 us
    pallas_call x1, Pallas kernels: 136 us -> 134 us  [fused_layer(): pl.pallas_call(partial(layer_kernel, T, D, S, entries), out_shape=(pltpu....]
where the time goes in v4:
time: 146 us; the launch traced here: 145 us
  Pallas kernels  144 us (99%)
    pallas_call x1, Pallas kernels, fused_layer(): pl.pallas_call(partial(layer_kernel, T, D, S, entries), out_shape=(pltpu....  134 us
    pallas_call x1, Pallas kernels, widen(): pl.pallas_call(partial(widen_kernel, steps - 1, T, D), grid=(steps,), out...  9.84 us

profile of v4, /device:TPU:0, one launch (start us, length us, event | category | flops | bytes accessed | tf_op | source)
XLA Modules:
  0.0 145.1 jit_solution(8315508514770215280)
XLA Ops:
  0.7 134.4 %layer.1 = (f32[128,768]{1,0:T(8,128)S(1)}, f32[128,768]{1,0:T(8,128)S(1)}, f32[16,768]{1,0:T(8,128)S(1)}, bf16[3072,768]{1,0:T(8,128)(2,1)S(1)}, bf16[768,3072]...) custom-call(f32[128,768]{1,0:T(8,128)} %bitcast.4, f32[128,768]{1,0:T(8,128)} %bitcast.5, s32[1,6]{1,0:T(1,128)} %lengths.1, ...), custom_call_target="tpu_custom_call" | custom-call | tf_op jit(solution)/shard_map/layer/pallas_call | solution.py:1505
  135.1 9.8 %widen.1 = (f32[128,768]{1,0:T(8,128)}, f32[128,768]{1,0:T(8,128)}, f32[768,768]{1,0:T(8,128)}, f32[768]{0:T(1024)}, f32[768,768]{1,0:T(8,128)}, /*index=5*/f32[...) custom-call(f32[128,768]{1,0:T(8,128)S(1)} %get-tuple-element.40.enc, ...), custom_call_target="tpu_custom_call" | custom-call | tf_op jit(solution)/shard_map/widen/pallas_call | solution.py:1649

commit v5 on v4

--- a/solution.py
+++ b/solution.py
@@ -382,16 +382,21 @@
 CHUNKS = 2
 
 PIECES = (
-    (DOWN_0, "zxy", 0, 3),
+    (DOWN_0, "zyx", 0, 1),
+    (DOWN_0, "zxy", 1, 2),
     (DOWN_1, "zyx", 0, 2),
     (DOWN_1, "xyz", 2, 1),
-    (UP_0, "zxy", 0, 3),
-    (UP_1, "zyx", 0, 2),
-    (UP_1, "xyz", 2, 1),
+    (UP_0, "zyx", 0, 3),
+    (UP_1, "zxy", 0, 3),
     (QUERY_OUT, "zxy", 0, 1),
     (QUERY_OUT, "yxz", 1, 2),
-    (KEY_VALUE, "zyx", 0, 3),
+    (KEY_VALUE, "zyx", 0, 1),
+    (KEY_VALUE, "zxy", 1, 2),
 )
+
+
+def gather_sems(piece):
+    return 12 + 1 + 1 if piece[1][2] == "z" else 3 + 4 + 4
 
 
 def dot(a, b):
@@ -614,7 +619,9 @@
     vectors_v = (v0, v1, v2, v3, v4, v5, v6, v7)
     arrays = (frames, cotangent, lengths, query_b, value_b, out_b, gain1, bias1, up_b, down_b, gain2, bias2)
     here_ = (frames_v, cotangent_v, lengths_v, *vectors_v[:5], up_v, *vectors_v[5:])
-    small = [pltpu.make_async_copy(array, ref, asem.at[i]) for i, (array, ref) in enumerate(zip(arrays, here_))]
+    small = [
+        pltpu.make_async_copy(array, ref, asem.at[min(i, 3)]) for i, (array, ref) in enumerate(zip(arrays, here_))
+    ]
     small[0].start()
     for load in loads[:3] + small[1:] + loads[3:]:
         load.start()
@@ -640,8 +647,10 @@
         pl.when(not_last)(lambda: push(z, h, 0))
         pl.when(not_first)(lambda: push(z, h, 1))
         push(z, h, 2)
-    for load in small[1:]:
+    for load in small[1:3]:
         load.wait()
+    nine = att32.at[pl.ds(0, (8 * D + wup.shape[1]) // HW), :]
+    pltpu.make_async_copy(nine, nine, asem.at[3]).wait()
     bias_rows[0:1, :] = query_b[...].reshape(1, D)
     bias_rows[1:2, :] = value_b[...].reshape(1, D)
     for quarter in range(4):
@@ -843,12 +852,31 @@
     share_y(fq, "ffn")
     vectors[9:10, :] = jnp.sum(fq[here, :].astype(F32), axis=0, keepdims=True)
     phase("ffn_back")
-    for x_, y_ in chips:
+
+    def ffn_back(order):
+        x_, y_ = chips[order]
         chip = 2 * y_ + x_
         low = grad_before(fq[here, :], chip, dgelu[chip])
         vectors[pl.ds(5 + chip, 1), :] = jnp.sum(low.astype(F32), axis=0, keepdims=True)
         gmid[...] += dot_nt(low, wup[:, at(D * chip, D)])
-    br[here, :] = low
+        if order == 3:
+            br[here, :] = low
+
+    def norm1_back():
+        grad_hidden = gmid[...]
+        unit = unit1[...]
+        grad_first = rows_norm_back(grad_hidden * gain1, unit, rstd1[:, 0:1])
+        vectors[3:4, :] = jnp.sum(grad_hidden * unit, axis=0, keepdims=True)
+        vectors[4:5, :] = jnp.sum(grad_hidden, axis=0, keepdims=True)
+        gfirst[...] = grad_first
+        low = grad_first.astype(BF16)
+        gbr[mine, :] = low
+        vectors[2:3, :] = jnp.sum(low.astype(F32), axis=0, keepdims=True)
+
+    def branch_send():
+        start(gbr.at[mine, :], gbr.at[mine, :], *one("gbr"), yn)
+
+    sent("gbr", gbr.at[mine, :], group("gbr"))
 
     def plane_active(x_, y_):
         rows = at(T * (2 * y_ + x_), T)
@@ -857,18 +885,6 @@
     def plane_back(x_, y_):
         rows = at(T * (2 * y_ + x_), T)
         br[rows, :] = grad_before(fq[rows, :], 2 * y + x, slopes[rows, :])
-
-    phase("norm1_back")
-    grad_hidden = gmid[...]
-    unit = unit1[...]
-    grad_first = rows_norm_back(grad_hidden * gain1, unit, rstd1[:, 0:1])
-    vectors[3:4, :] = jnp.sum(grad_hidden * unit, axis=0, keepdims=True)
-    vectors[4:5, :] = jnp.sum(grad_hidden, axis=0, keepdims=True)
-    gfirst[...] = grad_first
-    gbr[mine, :] = grad_first.astype(BF16)
-    start(gbr.at[mine, :], gbr.at[mine, :], *one("gbr"), yn)
-    sent("gbr", gbr.at[mine, :], group("gbr"))
-    vectors[2:3, :] = jnp.sum(gbr[mine, :].astype(F32), axis=0, keepdims=True)
 
     parts = (*(part_down.at[q] for q in range(2)), *(part_up.at[q] for q in range(2)), part_qo, part_kv)
     gots = (*(got_down.at[q] for q in range(2)), *(got_up.at[q] for q in range(2)), got_qo, got_kv)
@@ -955,19 +971,27 @@
     def z_last(u):
         return PIECES[u][1][2] == "z"
 
+    first_sem = [sum(gather_sems(piece) for piece in PIECES[:u]) for u in range(len(PIECES))]
+
+    def z_sem(u, p, z_, at_z):
+        return agr.at[first_sem[u] + 3 * p + lax.rem(z_ - at_z + 4, 4) - 1]
+
     def along_z(u, p, z_, direction):
         to = (zp, zm)[direction]
-        return gather_send(u, places[p], z_, ags.at[u], agr.at[u, 4 * p + z_], to)
+        return gather_send(u, places[p], z_, ags.at[u], z_sem(u, p, z_, (z + 1, z - 1)[direction]), to)
 
     def z_out(u, p):
         pl.when(not_last)(lambda: along_z(u, p, z, 0).start())
         pl.when(not_first)(lambda: along_z(u, p, z, 1).start())
 
+    def as_many(u, count):
+        return sum_down.at[pl.ds(0, unit * PIECES[u][3] * count), :]
+
     def second_sem(u, z_):
-        return agr.at[u, 16] if z_last(u) else agr.at[u, 4 + z_]
+        return agr.at[first_sem[u] + (12 if z_last(u) else 3 + z_)]
 
     def third_sem(u, slot):
-        return agr.at[u, (17 if z_last(u) else 8) + slot]
+        return agr.at[first_sem[u] + (13 if z_last(u) else 7 + lax.rem(slot, 4))]
 
     def to_second(u, place, z_):
         gather_send(u, place, z_, ags.at[u], second_sem(u, z_), order_of(u)[0][1]).start()
@@ -996,7 +1020,7 @@
         for u in pieces_of(t, False):
 
             def take(z_, more, direction):
-                arrived(tile(u, *places[0], z_), agr.at[u, z_])
+                arrived(tile(u, *places[0], z_), z_sem(u, 0, z_, z))
                 pl.when(more)(lambda: along_z(u, 0, z_, direction).start())
                 to_second(u, places[0], z_)
                 to_third(u, places[0], z_)
@@ -1019,8 +1043,8 @@
         for u in pieces_of(t, False):
 
             def take(z_, more, direction):
-                for offset, p in ((0, order_of(u)[1][0]), (4, 3)):
-                    arrived(tile(u, *places[p], z_), third_sem(u, offset + z_))
+                arrived(as_many(u, 2), third_sem(u, z_))
+                for p in (order_of(u)[1][0], 3):
                     to_sibling(u, places[p], z_)
 
             sides(k, take)
@@ -1034,8 +1058,8 @@
 
     def plane_second(t):
         for u in pieces_of(t, True):
-            for slot, p in ((0, order_of(u)[1][0]), (1, 3)):
-                arrived(tile(u, *places[p], z), third_sem(u, slot))
+            arrived(as_many(u, 2), third_sem(u, 0))
+            for p in (order_of(u)[1][0], 3):
                 to_sibling(u, places[p], z)
 
     def plane_out(t):
@@ -1048,23 +1072,19 @@
             for p in (0, order_of(u)[0][0], order_of(u)[1][0], 3):
 
                 def take(z_, more, direction):
-                    arrived(tile(u, *places[p], z_), agr.at[u, 4 * p + z_])
+                    arrived(tile(u, *places[p], z_), z_sem(u, p, z_, z))
                     pl.when(more)(lambda: along_z(u, p, z_, direction).start())
                     to_sibling(u, places[p], z_)
 
                 sides(k, take)
 
     def gather_end():
-        for u, (_, _, _, count) in enumerate(PIECES):
-
-            def as_many(blocks_sent):
-                return sum_down.at[pl.ds(0, unit * count * blocks_sent), :]
-
-            arrived(as_many(16), agdr.at[u])
+        for u in range(len(PIECES)):
+            arrived(as_many(u, 16), agdr.at[u])
             if z_last(u):
-                sent_along_z(("gather", u), as_many, ags.at[u], 19, 4)
+                sent_along_z(("gather", u), partial(as_many, u), ags.at[u], 19, 4)
             else:
-                sent_along_z(("gather", u), as_many, ags.at[u], 28)
+                sent_along_z(("gather", u), partial(as_many, u), ags.at[u], 28)
 
     def matrix_put(family, x_, value):
         for half_ in range(2):
@@ -1235,154 +1255,154 @@
     for i in range(3):
         sent(("v", i), vsend.at[i], group(("v", i)))
     sent("vz", vz.at[pl.ds(0, 3)], vzs.at[0])
+    ffn_back(0)
+    from_y(hq, "hid")
+    ffn_back(1)
+    ffn_back(2)
+    from_y(fq, "ffn")
+    ffn_back(3)
+    norm1_back()
+    branch_send()
     from_x(hq, "hid")
-    from_y(hq, "hid")
+    out_back()
+    rest_y(fq, "ffn")
+    rest_y(hq, "hid")
+    plane_active(x, 1 - y)
     rest_x(hq, "hid")
-    rest_y(hq, "hid")
-    from_y(fq, "ffn")
-    plane_active(x, 1 - y)
+    from_x(fq, "ffn")
+    queries_back()
     plane_active(1 - x, y)
-    out_back()
-    from_x(fq, "ffn")
-    rest_y(fq, "ffn")
-    queries_back()
-    rest_x(fq, "ffn")
     from_diagonal(hq, "hid")
+    query_weights()
     plane_active(1 - x, 1 - y)
     from_diagonal(fq, "ffn")
+    rest_x(fq, "ffn")
     pair_send(DOWN)
     grads_arrive(1)
+    attention_x(0)
+    pair_add(DOWN_1)
+    plane_back(1 - x, 1 - y)
+    keys_back_at(1)
     pair_add(DOWN_0)
-    plane_back(1 - x, 1 - y)
-    query_weights()
+    plane_back(1 - x, y)
+    sum_pass(DOWN_1)
+    grads_arrive(2)
     plane_back(x, 1 - y)
-    keys_back_at(1)
-    attention_x(0)
+    keys_back_at(2)
+    pair_send(UP)
     sum_pass(DOWN_0)
-    pair_add(DOWN_1)
-    plane_back(1 - x, y)
-    grads_arrive(2)
-    pair_send(UP)
-    sum_pass(DOWN_1)
-    keys_back_at(2)
+    sum_end(DOWN_1)
+    gather_own(DOWN_1)
+    keys_back_at(0)
+    pair_add(UP_0)
     sum_end(DOWN_0)
     gather_own(DOWN_0)
-    keys_back_at(0)
-    pair_add(UP_0)
-    sum_end(DOWN_1)
-    gather_own(DOWN_1)
+    gather_second(DOWN_1, 0)
+    plane_first(DOWN_1)
     grads_arrive(3)
     keys_back_at(3)
+    key_value_weights()
+    gather_z(DOWN_1, 1)
+    pair_add(UP_1)
+    gather_second(DOWN_0, 0)
+    sum_pass(UP_0)
+    attention_z(0)
     gather_z(DOWN_0, 1)
-    key_value_weights()
-    pair_add(UP_1)
-    sum_pass(UP_0)
     attention_x(1)
     input_grad()
-    gather_z(DOWN_0, 2)
-    attention_z(0)
+    vector_step(0, sib)
     sum_pass(UP_1)
-    gather_z(DOWN_1, 1)
-    vector_step(0, sib)
-    plane_first(DOWN_1)
-    gather_z(DOWN_0, 3)
-    gather_second(DOWN_0, 0)
+    gather_z(DOWN_1, 2)
+    sum_pass(QUERY_OUT)
     sum_end(UP_0)
     gather_own(UP_0)
+    gather_third(DOWN_1, 0)
     sum_end(UP_1)
     gather_own(UP_1)
-    attention_z(1)
-    gather_z(DOWN_1, 2)
-    sum_pass(QUERY_OUT)
+    gather_z(DOWN_0, 2)
+    sum_end(QUERY_OUT)
+    vector_add(0)
+    gather_z(DOWN_1, 3)
+    gather_own(QUERY_OUT)
     plane_second(DOWN_1)
     gather_z(UP_1, 1)
-    vector_add(0)
-    plane_out(DOWN_1)
-    gather_second(DOWN_1, 0)
+    vector_step(1, xn)
+    attention_z(1)
+    gather_z(QUERY_OUT, 1)
+    plane_first(QUERY_OUT)
+    input_grad_end()
+    gather_second(DOWN_0, 1)
+    gather_z(DOWN_0, 3)
+    gather_z(QUERY_OUT, 2)
+    gather_z(UP_0, 1)
     gather_z(UP_1, 2)
     sum_pass(KEY_VALUE)
-    sum_end(QUERY_OUT)
-    gather_z(UP_0, 1)
-    plane_first(UP_1)
-    plane_z(DOWN_1, 1)
-    gather_own(QUERY_OUT)
-    sum_end(KEY_VALUE)
-    gather_second(DOWN_0, 2)
-    gather_own(KEY_VALUE)
-    gather_second(DOWN_1, 2)
     gather_z(UP_1, 3)
     gather_z(UP_0, 2)
-    plane_second(UP_1)
-    gather_z(DOWN_1, 3)
-    plane_out(UP_1)
-    plane_first(QUERY_OUT)
-    input_grad_end()
-    gather_third(DOWN_0, 2)
+    sum_end(KEY_VALUE)
+    gather_own(KEY_VALUE)
+    plane_out(DOWN_1)
+    gather_second(UP_0, 1)
+    gather_second(QUERY_OUT, 1)
+    gather_second(DOWN_0, 3)
     gather_second(UP_1, 1)
-    gather_z(QUERY_OUT, 1)
+    gather_second(QUERY_OUT, 2)
+    gather_z(QUERY_OUT, 3)
+    plane_z(DOWN_1, 1)
+    gather_second(UP_1, 2)
+    gather_second(QUERY_OUT, 0)
+    gather_z(UP_0, 3)
+    plane_second(QUERY_OUT)
+    vector_add(1)
+    gather_second(DOWN_1, 3)
+    gather_second(UP_0, 0)
+    gather_second(QUERY_OUT, 3)
+    vector_step(2, yn)
     gather_z(KEY_VALUE, 1)
-    gather_second(UP_1, 2)
-    gather_second(DOWN_1, 3)
-    vector_step(1, xn)
-    gather_second(DOWN_0, 3)
-    plane_z(DOWN_1, 2)
-    gather_z(QUERY_OUT, 2)
-    plane_second(QUERY_OUT)
-    gather_z(UP_0, 3)
+    plane_out(QUERY_OUT)
     gather_second(UP_0, 2)
-    gather_second(DOWN_0, 1)
-    plane_z(UP_1, 1)
+    gather_second(UP_1, 3)
+    gather_third(DOWN_0, 3)
+    gather_third(QUERY_OUT, 2)
     gather_z(KEY_VALUE, 2)
-    plane_out(QUERY_OUT)
-    gather_third(DOWN_1, 0)
-    vector_add(1)
     gather_z(KEY_VALUE, 3)
     gather_second(DOWN_1, 1)
-    vector_step(2, yn)
-    gather_third(DOWN_1, 2)
+    gather_second(UP_1, 0)
+    plane_z(DOWN_1, 2)
+    gather_third(UP_0, 1)
     plane_z(QUERY_OUT, 1)
+    gather_third(UP_1, 1)
+    gather_third(DOWN_0, 0)
+    gather_third(DOWN_1, 3)
+    gather_second(DOWN_0, 2)
+    gather_second(UP_0, 3)
+    gather_third(UP_0, 2)
+    gather_third(UP_0, 0)
+    gather_second(KEY_VALUE, 1)
+    plane_z(DOWN_1, 3)
+    vector_add(2)
+    gather_third(QUERY_OUT, 1)
+    gather_third(QUERY_OUT, 3)
+    gather_third(UP_1, 3)
+    gather_third(UP_1, 2)
+    gather_third(QUERY_OUT, 0)
     gather_second(KEY_VALUE, 0)
-    gather_second(QUERY_OUT, 1)
-    gather_second(UP_1, 3)
-    gather_second(QUERY_OUT, 2)
-    gather_second(QUERY_OUT, 0)
-    gather_third(UP_0, 2)
-    gather_second(UP_1, 0)
-    gather_second(KEY_VALUE, 3)
-    gather_second(UP_0, 1)
-    gather_third(DOWN_1, 3)
-    gather_third(UP_1, 2)
-    vector_add(2)
-    gather_third(DOWN_0, 1)
-    plane_z(UP_1, 2)
-    gather_third(QUERY_OUT, 0)
-    gather_second(UP_0, 0)
     plane_z(QUERY_OUT, 2)
-    gather_second(UP_0, 3)
-    gather_z(QUERY_OUT, 3)
+    gather_second(DOWN_1, 2)
+    gather_third(DOWN_1, 1)
     vector_z()
     gather_second(KEY_VALUE, 2)
-    gather_third(UP_0, 1)
-    plane_z(DOWN_1, 3)
-    gather_third(DOWN_0, 0)
+    gather_third(UP_1, 0)
+    gather_third(UP_0, 3)
+    gather_third(DOWN_0, 2)
+    gather_second(KEY_VALUE, 3)
+    gather_third(DOWN_0, 1)
+    gather_third(KEY_VALUE, 1)
+    gather_third(KEY_VALUE, 0)
+    plane_z(QUERY_OUT, 3)
+    gather_third(DOWN_1, 2)
+    gather_third(KEY_VALUE, 2)
     gather_third(KEY_VALUE, 3)
-    gather_third(DOWN_0, 3)
-    gather_second(KEY_VALUE, 1)
-    gather_second(QUERY_OUT, 3)
-    gather_third(UP_1, 3)
-    gather_third(UP_0, 0)
-    gather_third(UP_1, 0)
-    gather_third(DOWN_1, 1)
-    gather_third(KEY_VALUE, 2)
-    gather_third(UP_1, 1)
-    plane_z(UP_1, 3)
-    gather_third(KEY_VALUE, 0)
-    gather_third(QUERY_OUT, 1)
-    gather_third(UP_0, 3)
-    gather_third(QUERY_OUT, 3)
-    gather_third(KEY_VALUE, 1)
-    gather_third(QUERY_OUT, 2)
-    plane_z(QUERY_OUT, 3)
     vector_end()
     phase("gather_end")
     gather_end()
@@ -1485,7 +1505,7 @@
         vrecv=wide(3, 16, D),
         vz=wide(4, 16, D),
         wsem=dma((6,)),
-        asem=dma((12,)),
+        asem=dma((4,)),
         hes=dma((1,)),
         her=dma((blocks,)),
         frs=dma((CHUNKS, 8)),
@@ -1496,7 +1516,7 @@
         dos=dma((2,)),
         zsr=dma((6, 4)),
         zss=dma((6,)),
-        agr=dma((n, 19)),
+        agr=dma((sum(map(gather_sems, PIECES)),)),
         ags=dma((n,)),
         agdr=dma((n,)),
         vzr=dma((4,)),

time: 146 us -> 143 us (0.979)
  Pallas kernels: 144 us -> 142 us
    pallas_call x1, Pallas kernels: 134 us -> 132 us  [fused_layer(): pl.pallas_call(partial(layer_kernel, T, D, S, entries), out_shape=(pltpu....]
where the time goes in v5:
time: 143 us; the launch traced here: 142 us
  Pallas kernels  142 us (99%)
    pallas_call x1, Pallas kernels, fused_layer(): pl.pallas_call(partial(layer_kernel, T, D, S, entries), out_shape=(pltpu....  132 us
    pallas_call x1, Pallas kernels, widen(): pl.pallas_call(partial(widen_kernel, steps - 1, T, D), grid=(steps,), out...  9.84 us

profile of v5, /device:TPU:0, one launch (start us, length us, event | category | flops | bytes accessed | tf_op | source)
XLA Modules:
  0.0 142.4 jit_solution(17434410360450937463)
XLA Ops:
  0.7 131.7 %layer.1 = (f32[128,768]{1,0:T(8,128)S(1)}, f32[128,768]{1,0:T(8,128)S(1)}, f32[16,768]{1,0:T(8,128)S(1)}, bf16[3072,768]{1,0:T(8,128)(2,1)S(1)}, bf16[768,3072]...) custom-call(f32[128,768]{1,0:T(8,128)} %bitcast.4, f32[128,768]{1,0:T(8,128)} %bitcast.5, s32[1,6]{1,0:T(1,128)} %lengths.1, ...), custom_call_target="tpu_custom_call" | custom-call | tf_op jit(solution)/shard_map/layer/pallas_call | solution.py:1525
  132.4 9.8 %widen.1 = (f32[128,768]{1,0:T(8,128)}, f32[128,768]{1,0:T(8,128)}, f32[768,768]{1,0:T(8,128)}, f32[768]{0:T(1024)}, f32[768,768]{1,0:T(8,128)}, /*index=5*/f32[...) custom-call(f32[128,768]{1,0:T(8,128)S(1)} %get-tuple-element.40.enc, ...), custom_call_target="tpu_custom_call" | custom-call | tf_op jit(solution)/shard_map/widen/pallas_call | solution.py:1669

commit v6 on v5

--- a/solution.py
+++ b/solution.py
@@ -379,7 +379,7 @@
 VMEM_GRANT = 49 << 20
 DOWN, UP = 0, 1
 DOWN_0, DOWN_1, UP_0, UP_1, QUERY_OUT, KEY_VALUE = range(6)
-CHUNKS = 2
+CHUNKS = 4
 
 PIECES = (
     (DOWN_0, "zyx", 0, 1),

time: 143 us -> 142 us (level)
  no operation moved by 1% of the time
where the time goes in v6:
time: 142 us; the launch traced here: 141 us
  Pallas kernels  141 us (99%)
    pallas_call x1, Pallas kernels, fused_layer(): pl.pallas_call(partial(layer_kernel, T, D, S, entries), out_shape=(pltpu....  131 us
    pallas_call x1, Pallas kernels, widen(): pl.pallas_call(partial(widen_kernel, steps - 1, T, D), grid=(steps,), out...  9.84 us

profile of v6, /device:TPU:0, one launch (start us, length us, event | category | flops | bytes accessed | tf_op | source)
XLA Modules:
  0.0 141.5 jit_solution(11261788424828009235)
XLA Ops:
  0.7 130.8 %layer.1 = (f32[128,768]{1,0:T(8,128)S(1)}, f32[128,768]{1,0:T(8,128)S(1)}, f32[16,768]{1,0:T(8,128)S(1)}, bf16[3072,768]{1,0:T(8,128)(2,1)S(1)}, bf16[768,3072]...) custom-call(f32[128,768]{1,0:T(8,128)} %bitcast.4, f32[128,768]{1,0:T(8,128)} %bitcast.5, s32[1,6]{1,0:T(1,128)} %lengths.1, ...), custom_call_target="tpu_custom_call" | custom-call | tf_op jit(solution)/shard_map/layer/pallas_call | solution.py:1525
  131.5 9.8 %widen.1 = (f32[128,768]{1,0:T(8,128)}, f32[128,768]{1,0:T(8,128)}, f32[768,768]{1,0:T(8,128)}, f32[768]{0:T(1024)}, f32[768,768]{1,0:T(8,128)}, /*index=5*/f32[...) custom-call(f32[128,768]{1,0:T(8,128)S(1)} %get-tuple-element.40.enc, ...), custom_call_target="tpu_custom_call" | custom-call | tf_op jit(solution)/shard_map/widen/pallas_call | solution.py:1669

commit v7 on v6

--- a/solution.py
+++ b/solution.py
@@ -526,6 +526,7 @@
     hes,
     her,
     frs,
+    fry,
     fss,
     msr,
     mss,
@@ -641,7 +642,8 @@
 
     def push(z_, h, direction):
         to = (zp, zm, yn)[direction]
-        start(chunk(z_, y, h), chunk(z_, y, h), fss.at[direction // 2], frs.at[h, 2 * z_ + y], to)
+        rsem = fry.at[z_] if direction == 2 else frs.at[h, z_]
+        start(chunk(z_, y, h), chunk(z_, y, h), fss.at[direction // 2], rsem, to)
 
     for h in range(CHUNKS):
         pl.when(not_last)(lambda: push(z, h, 0))
@@ -689,19 +691,18 @@
 
             @pl.when(left >= 0)
             def _():
-                arrived(chunk(left, y, h), frs.at[h, 2 * left + y])
+                arrived(chunk(left, y, h), frs.at[h, left])
                 pl.when(not_last)(lambda: push(left, h, 0))
                 push(left, h, 2)
 
             @pl.when(right <= 3)
             def _():
-                arrived(chunk(right, y, h), frs.at[h, 2 * right + y])
+                arrived(chunk(right, y, h), frs.at[h, right])
                 pl.when(not_first)(lambda: push(right, h, 1))
                 push(right, h, 2)
 
         def across_y(z_):
-            for h in range(CHUNKS):
-                arrived(chunk(z_, 1 - y, h), frs.at[h, 2 * z_ + 1 - y])
+            arrived(fall.at[at(T * (2 * z_ + 1 - y), T), :], fry.at[z_])
             project_slab(z_, 1 - y)
 
         pl.when(left >= 0)(lambda: project_slab(left, y))
@@ -1508,7 +1509,8 @@
         asem=dma((4,)),
         hes=dma((1,)),
         her=dma((blocks,)),
-        frs=dma((CHUNKS, 8)),
+        frs=dma((CHUNKS, 4)),
+        fry=dma((4,)),
         fss=dma((2,)),
         msr=dma((25,)),
         mss=dma((13,)),

time: 142 us -> 142 us (level)
  no operation moved by 1% of the time
where the time goes in v7:
time: 142 us; the launch traced here: 141 us
  Pallas kernels  141 us (99%)
    pallas_call x1, Pallas kernels, fused_layer(): pl.pallas_call(partial(layer_kernel, T, D, S, entries), out_shape=(pltpu....  131 us
    pallas_call x1, Pallas kernels, widen(): pl.pallas_call(partial(widen_kernel, steps - 1, T, D), grid=(steps,), out...  9.84 us

profile of v7, /device:TPU:0, one launch (start us, length us, event | category | flops | bytes accessed | tf_op | source)
XLA Modules:
  0.0 141.4 jit_solution(15497725938187235010)
XLA Ops:
  0.7 130.7 %layer.1 = (f32[128,768]{1,0:T(8,128)S(1)}, f32[128,768]{1,0:T(8,128)S(1)}, f32[16,768]{1,0:T(8,128)S(1)}, bf16[3072,768]{1,0:T(8,128)(2,1)S(1)}, bf16[768,3072]...) custom-call(f32[128,768]{1,0:T(8,128)} %bitcast.4, f32[128,768]{1,0:T(8,128)} %bitcast.5, s32[1,6]{1,0:T(1,128)} %lengths.1, ...), custom_call_target="tpu_custom_call" | custom-call | tf_op jit(solution)/shard_map/layer/pallas_call | solution.py:1527
  131.4 9.8 %widen.1 = (f32[128,768]{1,0:T(8,128)}, f32[128,768]{1,0:T(8,128)}, f32[768,768]{1,0:T(8,128)}, f32[768]{0:T(1024)}, f32[768,768]{1,0:T(8,128)}, /*index=5*/f32[...) custom-call(f32[128,768]{1,0:T(8,128)S(1)} %get-tuple-element.40.enc, ...), custom_call_target="tpu_custom_call" | custom-call | tf_op jit(solution)/shard_map/widen/pallas_call | solution.py:1671
